TPU v7x, 512 devices: a whole 4x8x8 slice. The times are simulated.
512 devices in a mesh: ctx: 16 (over y, x_hi), exp: 32 (over z, x_lo, core).
Axes of the slice: x: 4 (x_hi: 2, x_lo: 2; x = x_hi * 2 + x_lo), y: 8, z: 8, core: 2. Of those that a mesh axis runs over, the one named last changes fastest.
Arguments:
- queries: bfloat16 [1920, 64, 576], P('ctx', 'exp'), may hold values from -40 to 40
- latents: bfloat16 [1920, 576], P('ctx'), may hold values from -6 to 6
- block_mask: int32 [16, 16], replicated, may hold values from 0 to 1, as said below
- value_up: bfloat16 [64, 512, 128], P('exp'), may hold values from -0.25 to 0.25
- out_proj: bfloat16 [8192, 2560], P('exp'), may hold values from -0.125 to 0.125
- residual: bfloat16 [1920, 2560], P('ctx', 'exp'), may hold values from -9 to 9
- norm_gain: bfloat16 [2560], P('exp'), may hold values from 0.099609375 to 1.8984375
- group_ids: int32 [1920, 3], P('ctx'), may hold values from 0 to 15, all different within a row; in each aligned block of 120 rows (0 to 119, 120 to 239, ...) at most 30 rows name the same one
- expert_ids: int32 [1920, 3, 2], P('ctx'), may hold values from 0 to 5, all different within a row
- route_weights: bfloat16 [1920, 3, 2], P('ctx'), may hold values from 0.049804688 to 0.59765625
- w_gate: bfloat16 [96, 2560, 768], P('ctx', 'exp'), may hold values from -0.125 to 0.125
- w_up: bfloat16 [96, 2560, 768], P('ctx', 'exp'), may hold values from -0.125 to 0.125
- w_down: bfloat16 [96, 768, 2560], P('ctx', None, 'exp'), may hold values from -0.21875 to 0.21875
Outputs:
- layer_out: bfloat16 [1920, 2560], P('ctx', 'exp')
Inputs may be any that keep to these rules, and one draw needn't show every extreme that they name: block_mask[a, a] = 1, block_mask[a, b] = 0 for b > a, and block_mask[a, a - 8] = 1 for a >= 8. `group_ids`: the 3 groups of a token differ. Among the 120 tokens of one context block (aligned blocks of 120 rows) no group is named more than 30 times, a bound that some block reaches. `expert_ids`: the 2 experts of a token within one group differ.
All inputs are finite; a program needn't handle non-finite values.
Results may differ from a plain program's by a relative error of at most 0.024.
Values may be sent and summed in bfloat16 or wider, within the bound.
No kernel may reach another device: no remote copies, remote signals or barrier semaphores. Data moves between devices by JAX's collectives and lax.ppermute only.
A program may use at most 64 MiB of HBM per device.

v0:
```python
import jax
import jax.numpy as jnp
from jax import lax
from jax.sharding import PartitionSpec as P

D = 2560


MASKED_SCORE = -1e30
EPSILON = 1e-06


def lookup_flags(flags, wanted, ctx_count):
    table = jnp.arange(ctx_count)[None, :] == wanted[:, None]
    return jnp.sum(jnp.where(table, flags[None, :], 0), axis=1)


def on_device(
    queries,
    latents,
    block_mask,
    value_up,
    out_proj,
    residual,
    norm_gain,
    group_ids,
    expert_ids,
    route_weights,
    w_gate,
    w_up,
    w_down,
):
    ctx_count = lax.axis_size("ctx")
    my_block = lax.axis_index("ctx")
    block_rows = latents.shape[0]
    head_count = queries.shape[1]
    key_width = latents.shape[1]
    latent_width = value_up.shape[1]
    value_width = value_up.shape[2]
    inverse_root = key_width ** (-0.5)
    mask_row = lax.dynamic_index_in_dim(block_mask, my_block, 0, keepdims=False)
    query_pos = my_block * block_rows + jnp.arange(block_rows)
    initial = (
        jnp.zeros((block_rows, head_count, latent_width), jnp.float32),
        jnp.full((block_rows, head_count), MASKED_SCORE, jnp.float32),
        jnp.zeros((block_rows, head_count), jnp.float32),
    )
    part_rows = lax.all_gather(latents, "ctx", axis=0, tiled=True)
    row_count = part_rows.shape[0]
    key_pos = jnp.arange(row_count)
    key_block = key_pos // block_rows
    visible = lookup_flags(mask_row, key_block, ctx_count)
    allowed = (visible[None, :] == 1) & (
        (key_block[None, :] != my_block) | (key_pos[None, :] <= query_pos[:, None])
    )

    def compute(current):
        weighted, row_top, row_total = current
        scores = (
            jnp.einsum("rhq,tq->rht", queries, part_rows, preferred_element_type=jnp.float32)
            * inverse_root
        )
        masked = jnp.where(allowed[:, None, :], scores, MASKED_SCORE)
        new_top = jnp.maximum(row_top, jnp.max(masked, axis=2))
        exp_terms = jnp.where(allowed[:, None, :], jnp.exp(masked - new_top[:, :, None]), 0.0)
        added = jnp.einsum(
            "rht,tl->rhl",
            exp_terms.astype(jnp.bfloat16),
            part_rows[:, :latent_width],
            preferred_element_type=jnp.float32,
        )
        return (added, new_top, jnp.sum(exp_terms, axis=2))

    weighted, row_top, row_total = lax.cond(
        jnp.any(allowed), compute, lambda current: current, initial
    )
    attn_latent = weighted / row_total[..., None]
    attn_value = jnp.einsum(
        "rhl,hlv->rhv", attn_latent, value_up.astype(jnp.float32), precision=lax.Precision.HIGHEST
    )
    attn_value = attn_value.astype(jnp.bfloat16).reshape(block_rows, head_count * value_width)
    feature_run = residual.shape[1]
    mixed_rows = lax.psum_scatter(
        lax.dot_general(
            out_proj, attn_value, (((0,), (1,)), ((), ())), preferred_element_type=jnp.float32
        ).astype(jnp.bfloat16),
        "exp",
        scatter_dimension=0,
        tiled=True,
    ).astype(jnp.float32)
    hidden = (residual.astype(jnp.float32).T + mixed_rows).astype(jnp.bfloat16)
    hidden_wide = hidden.astype(jnp.float32)
    square_sum = lax.psum(jnp.sum(hidden_wide * hidden_wide, axis=0), "exp")
    row_scale = lax.rsqrt(square_sum / D + EPSILON)
    normed = (hidden_wide * row_scale[None, :] * norm_gain.astype(jnp.float32)[:, None]).astype(
        jnp.bfloat16
    )
    group_picks = group_ids.shape[1]
    expert_picks = expert_ids.shape[2]
    local_experts = w_gate.shape[0]
    hidden_units = w_gate.shape[2]
    capacity = min(block_rows, 4 * group_picks * block_rows // (3 * ctx_count))
    group_range = jnp.arange(ctx_count)
    expert_range = jnp.arange(local_experts)
    member = jnp.zeros((block_rows, ctx_count), jnp.int32)
    shares = jnp.zeros((block_rows, ctx_count, local_experts), jnp.float32)
    for group_slot in range(group_picks):
        group_hit = group_ids[:, group_slot, None] == group_range[None, :]
        member = member + group_hit.astype(jnp.int32)
        for expert_slot in range(expert_picks):
            expert_hit = (
                expert_ids[:, group_slot, expert_slot, None] == expert_range[None, :]
            ).astype(jnp.float32)
            shares = shares + group_hit.astype(jnp.float32)[:, :, None] * expert_hit[
                :, None, :
            ] * route_weights[:, group_slot, expert_slot, None, None].astype(jnp.float32)
    ranking = jnp.cumsum(member, axis=0) - 1
    placement = (
        (member[:, :, None] == 1) & (ranking[:, :, None] == jnp.arange(capacity)[None, None, :])
    ).astype(jnp.bfloat16)
    sent_rows = jnp.einsum(
        "dt,tgc->dgc", normed, placement, preferred_element_type=jnp.float32
    ).astype(jnp.bfloat16)
    sent_weights = jnp.einsum(
        "tge,tgc->egc", shares.astype(jnp.bfloat16), placement, preferred_element_type=jnp.float32
    ).astype(jnp.bfloat16)
    recv_rows, recv_weights = (
        lax.all_to_all(sent_rows, "ctx", split_axis=1, concat_axis=1, tiled=True),
        lax.all_to_all(sent_weights, "ctx", split_axis=1, concat_axis=1, tiled=True),
    )
    slots = ctx_count * capacity
    inputs = recv_rows.reshape(feature_run, slots)
    weights = recv_weights.reshape(local_experts, slots).astype(jnp.float32)
    chosen = (weights > 0.0).astype(jnp.int32)
    ordinal = jnp.cumsum(chosen, axis=0) - 1
    keep_masks = [
        [
            ((chosen[expert] == 1) & (ordinal[expert] == expert_slot)).astype(jnp.float32)
            for expert_slot in range(expert_picks)
        ]
        for expert in range(local_experts)
    ]
    gate_terms = [
        jnp.zeros((hidden_units, slots), jnp.float32) for expert_slot in range(expert_picks)
    ]
    up_terms = [
        jnp.zeros((hidden_units, slots), jnp.float32) for expert_slot in range(expert_picks)
    ]
    for expert in range(local_experts):
        gate_part = lax.dot_general(
            w_gate[expert], inputs, (((0,), (0,)), ((), ())), preferred_element_type=jnp.float32
        )
        up_part = lax.dot_general(
            w_up[expert], inputs, (((0,), (0,)), ((), ())), preferred_element_type=jnp.float32
        )
        for expert_slot in range(expert_picks):
            gate_terms[expert_slot] = (
                gate_terms[expert_slot] + keep_masks[expert][expert_slot][None, :] * gate_part
            )
            up_terms[expert_slot] = (
                up_terms[expert_slot] + keep_masks[expert][expert_slot][None, :] * up_part
            )
    gate_stack = jnp.stack(gate_terms, axis=0)
    up_stack = jnp.stack(up_terms, axis=0)
    gate_total, up_total = (
        lax.psum(gate_stack.astype(jnp.bfloat16), "exp").astype(jnp.float32),
        lax.psum(up_stack.astype(jnp.bfloat16), "exp").astype(jnp.float32),
    )
    activated = (jax.nn.silu(gate_total) * up_total).astype(jnp.bfloat16)
    outputs = jnp.zeros((feature_run, slots), jnp.float32)
    for expert in range(local_experts):
        picked = jnp.zeros((hidden_units, slots), jnp.bfloat16)
        for expert_slot in range(expert_picks):
            picked = jnp.where(
                keep_masks[expert][expert_slot][None, :] > 0.0, activated[expert_slot], picked
            )
        down_part = lax.dot_general(
            w_down[expert], picked, (((0,), (0,)), ((), ())), preferred_element_type=jnp.float32
        )
        outputs = outputs + weights[expert][None, :] * down_part
    returned = lax.all_to_all(
        outputs.astype(jnp.bfloat16).reshape(feature_run, ctx_count, capacity),
        "ctx",
        split_axis=1,
        concat_axis=1,
        tiled=True,
    )
    expert_sum = jnp.einsum("dgc,tgc->dt", returned, placement, preferred_element_type=jnp.float32)
    return (hidden_wide + expert_sum).astype(jnp.bfloat16).T


def solution(mesh):
    return jax.shard_map(
        on_device,
        mesh=mesh,
        in_specs=(
            P("ctx", "exp", None),
            P("ctx", None),
            P(),
            P("exp", None, None),
            P("exp", None),
            P("ctx", "exp"),
            P("exp"),
            P("ctx", None),
            P("ctx", None, None),
            P("ctx", None, None),
            P("ctx", "exp", None),
            P("ctx", "exp", None),
            P("ctx", None, "exp"),
        ),
        out_specs=P("ctx", "exp"),
        check_vma=False,
    )
```

profile of v0, /device:TPU:1, one launch (start us, length us, event | category | flops | bytes accessed | tf_op | source)
XLA Modules:
  0.0 593.0 jit_solution(10411176989885446846)
XLA Ops:
  10.3 1.6 fusion.29
  12.6 1.4 slice_bitcast_fusion.7
  15.2 90.3 %all-gather.3.cloned.1.call-done = bf16[16,120,576]{1,2,0:T(8,128)(2,1)} async-done(((bf16[1,120,576]{1,2,0:T(8,128)(2,1)}), bf16[16,120,576]{1,2,0:T(8,128)(2,1)}) %all-gather.3.cloned.1.call-update) | async-done | bytes 2211856 | tf_op jit(solution)/shard_map/all_gather | solution.py:48
  105.4 13.9 %conditional.1 = (f32[120,2,512]{2,0,1:T(8,128)}, f32[120,2]{0,1:T(2,128)}) conditional(s32[]{:T(128)} %convert_element_type.240, () %tuple.13, (pred[120,1920]{1,0:T(8,128)(4,1)}, bf16[120,2,576]{0,2,1:T(8,128)(2,1)}, bf16[16,120,576]{1,2,0:T(8,128)(2,1)}) %tuple.14), branch_computations={%region_2.3_spmd, %region_3.6_spmd} | conditional | flops 1006847744 | bytes 20941548 | solution.py:74
  105.4 4.6 copy.79
  110.0 4.4 reshape.523
  114.5 2.2 fusion.187
  116.7 1.6 fusion.2
  119.3 1.5 fusion.23
  121.3 1.1 copy.77
  123.3 4.7 all-to-all-start
  128.1 9.1 %all-to-all-done = bf16[6,16,30]{2,0,1:T(8,128)(2,1)S(1)} async-done(((bf16[6,16,30]{2,0,1:T(8,128)(2,1)}), bf16[6,16,30]{2,0,1:T(8,128)(2,1)S(1)}, u32[]{:S(2)}, u32[]{:S(2)}) %all-to-all-start) | async-done | bytes 5792 | tf_op jit(solution)/shard_map/all_to_all | solution.py:129
  138.1 100.9 %reduce-scatter.4.cloned.1.call-done = bf16[80,120]{1,0:T(8,128)(2,1)} async-done(((bf16[2560,120]{1,0:T(8,128)(2,1)}), bf16[80,120]{1,0:T(8,128)(2,1)}) %reduce-scatter.4.cloned.1.call-update) | async-done | bytes 19216 | tf_op jit(solution)/shard_map/reduce_scatter | solution.py:83
  239.8 56.5 %psum.21 = f32[120]{0:T(128)S(1)} all-reduce(f32[120]{0:T(128)S(1)} %fusion.147), channel_id=1, replica_groups=mesh['ctx'=16,'exp'=32] {'exp'}, use_global_device_ids=true, to_apply=%region_10.11 | all-reduce | flops 120 | bytes 960 | tf_op jit(solution)/shard_map/psum | solution.py:93
  296.3 1.6 convolution_convert_fusion.1
  298.0 8.7 %all-to-all-start.1 = ((bf16[80,16,30]{0,2,1:T(8,128)(2,1)}), bf16[80,16,30]{0,2,1:T(8,128)(2,1)S(1)}, u32[]{:S(2)}, u32[]{:S(2)}) async-start(bf16[80,16,30]{0,2,1:T(8,128)(2,1)} %convolution_convert_fusion.1), calls=%async_computation.1 | async-start | bytes 262144 | tf_op jit(solution)/shard_map/all_to_all | solution.py:128
  307.1 9.6 %all-to-all-done.1 = bf16[80,16,30]{0,2,1:T(8,128)(2,1)S(1)} async-done(((bf16[80,16,30]{0,2,1:T(8,128)(2,1)}), bf16[80,16,30]{0,2,1:T(8,128)(2,1)S(1)}, u32[]{:S(2)}, u32[]{:S(2)}) %all-to-all-start.1) | async-done | bytes 76832 | tf_op jit(solution)/shard_map/all_to_all | solution.py:128
  320.5 1.8 fusion.62
  322.3 1.3 pad_maximum_fusion.1
  323.6 1.7 fusion.60
  325.3 1.3 pad_maximum_fusion
  327.3 232.5 %all-reduce.3.cloned.1.call-done = (bf16[2,768,480]{1,2,0:T(8,128)(2,1)}, bf16[2,768,480]{1,2,0:T(8,128)(2,1)}) async-done(((bf16[2,768,480]{1,2,0:T(8,128)(2,1)}, bf16[2,768,480]{1,2,0:T(8,128)(2,1)}), (bf16[2,768,480]{1,2,0:T(8,128)(2,1)}, bf16[2,768,480]{1,2,0:T(8,128)(2,1)})) %all-reduce.3.cloned.1.call-update) | async-done | bytes 2949136 | tf_op jit(solution)/shard_map/psum | solution.py:167
  559.8 2.8 fusion.15
  565.8 19.8 %all_to_all.15 = bf16[80,16,30]{0,2,1:T(8,128)(2,1)S(1)} all-to-all(bf16[80,16,30]{0,2,1:T(8,128)(2,1)S(1)} %reshape.508), channel_id=1, replica_groups=mesh['ctx'=16,'exp'=32] {'ctx'}, dimensions={1} | all-to-all | bytes 153600 | tf_op jit(solution)/shard_map/all_to_all | solution.py:181
  (105 shorter events, 17.7 us)
Async XLA Ops:
  6.5 114.3 %copy-start = (bf16[256,2560]{1,0:T(8,128)(2,1)S(1)}, bf16[256,2560]{1,0:T(8,128)(2,1)}, u32[]{:S(2)}) copy-start(bf16[256,2560]{1,0:T(8,128)(2,1)} %param.19) | copy-start | bytes 3932164
  6.5 98.9 %all-gather.3.cloned.1.call-start = ((), (), s32[]{:S(2)}) async-start(), calls=%async_computation.4 | async-start | bytes 2506752 | tf_op jit(solution)/shard_map/all_gather | solution.py:48
  7.3 231.8 %reduce-scatter.4.cloned.1.call-start = ((), (), s32[]{:S(2)}) async-start(), calls=%async_computation.5 | async-start | bytes 675840 | tf_op jit(solution)/shard_map/reduce_scatter | solution.py:83
  114.4 2.2 copy-start.1
  120.9 1.6 copy-start.6
  120.9 1.6 copy-start.12
  120.9 1.6 copy-start.13
  121.2 1.2 copy-start.7
  121.2 1.2 copy-start.8
  121.3 1.2 copy-start.9
  121.3 1.2 copy-start.10
  121.3 1.2 copy-start.11
  121.3 6.8 %copy-start.15 = (bf16[80]{0:T(256)(128)(2,1)S(1)}, bf16[80]{0:T(256)(128)(2,1)}, u32[]{:S(2)}) copy-start(bf16[80]{0:T(256)(128)(2,1)} %param.21) | copy-start | bytes 484
  121.3 117.8 %copy-start.4 = (bf16[120,80]{0,1:T(8,128)(2,1)S(1)}, bf16[120,80]{0,1:T(8,128)(2,1)}, u32[]{:S(2)}) copy-start(bf16[120,80]{0,1:T(8,128)(2,1)} %param.20) | copy-start | bytes 57604
  122.4 194.3 %copy-start.2 = (bf16[6,80,768]{2,1,0:T(8,128)(2,1)S(1)}, bf16[6,80,768]{2,1,0:T(8,128)(2,1)}, u32[]{:S(2)}) copy-start(bf16[6,80,768]{2,1,0:T(8,128)(2,1)} %param.26) | copy-start | bytes 2211844
  123.3 13.8 %all-to-all-start = ((bf16[6,16,30]{2,0,1:T(8,128)(2,1)}), bf16[6,16,30]{2,0,1:T(8,128)(2,1)S(1)}, u32[]{:S(2)}, u32[]{:S(2)}) async-start(bf16[6,16,30]{2,0,1:T(8,128)(2,1)} %fusion.24), calls=%async_computation | async-start | bytes 65536 | tf_op jit(solution)/shard_map/all_to_all | solution.py:129
  298.0 18.7 %all-to-all-start.1 = ((bf16[80,16,30]{0,2,1:T(8,128)(2,1)}), bf16[80,16,30]{0,2,1:T(8,128)(2,1)S(1)}, u32[]{:S(2)}, u32[]{:S(2)}) async-start(bf16[80,16,30]{0,2,1:T(8,128)(2,1)} %convolution_convert_fusion.1), calls=%async_computation.1 | async-start | bytes 262144 | tf_op jit(solution)/shard_map/all_to_all | solution.py:128
  306.7 253.1 %all-reduce.3.cloned.1.call-start = ((), (), s32[]{:S(2)}) async-start(), calls=%async_computation.6 | async-start | bytes 5898240 | tf_op jit(solution)/shard_map/psum | solution.py:167
  317.7 1.1 copy-start.3
  559.8 2.8 copy-start.14
  565.1 20.5 %copy-start.5 = (bf16[80,120]{1,0:T(8,128)(2,1)S(1)}, bf16[80,120]{1,0:T(8,128)(2,1)}, u32[]{:S(2)}) copy-start(bf16[80,120]{1,0:T(8,128)(2,1)} %reduce-scatter.4.cloned.1.call-done) | copy-start | bytes 57604
Sparse Core Ops, SparseCore 0:
  10.5 94.8 all-gather.2
  122.5 116.4 reduce-scatter.3
  326.7 233.0 all-reduce.2
where the time goes:
time: 594 us; the launch traced here: 593 us
  waiting for transfers between devices  443 us (75%)
  blocking collectives  76.3 us (13%)
  matrix products  18.7 us (3%)
  local copies, waits for them, and re-layouts  16 us (3%)
  between operations  14.2 us (2%)
  starting transfers between devices  13.7 us (2%)
  other arithmetic  10.9 us (2%)
    psum x1, waiting for transfers between devices, on_device(): lax.psum(up_stack.astype(jnp.bfloat16), 'exp').astype(jnp.float32)  233 us
    reduce_scatter x1, waiting for transfers between devices, on_device(): lax.psum_scatter(lax.dot_general(out_proj, attn_value, (((0,), (1,)), (()...  101 us
    all_gather x1, waiting for transfers between devices, on_device(): part_rows = lax.all_gather(latents, 'ctx', axis=0, tiled=True)  90.3 us
    psum x1, blocking collectives, on_device(): square_sum = lax.psum(jnp.sum(hidden_wide * hidden_wide, axis=0), 'exp')  56.5 us
    all_to_all x1, blocking collectives, on_device(): lax.all_to_all(outputs.astype(jnp.bfloat16).reshape(feature_run, ctx_coun...  19.8 us
  transfers between devices with their start and end apart: 5, of which 5 were waited for; matrix products, arithmetic and copies ran while one was open for 2% of the time, Pallas kernels for 0%

commit v1 on v0

v1 whole, which is shorter than its diff:
```python
import functools

import jax
import jax.numpy as jnp
from jax import lax
from jax.experimental import pallas as pl
from jax.experimental.pallas import tpu as pltpu
from jax.sharding import Mesh
from jax.sharding import PartitionSpec as P

D = 2560
EPSILON = 1e-06
MASKED_SCORE = -1e30
CTX = ("y", "xh")
EXP = ("z", "xl", "core")
ZX = ("z", "xl")
XC = ("xl", "core")
TOK = 128
SLOT = 32
F32 = jnp.float32
BF16 = jnp.bfloat16
VMEM = pl.BlockSpec(memory_space=pltpu.VMEM)
SMEM = pl.BlockSpec(memory_space=pltpu.SMEM)


def call(body, out_shape, in_specs, scratch=(), flops=0, limit=40):
    many = isinstance(out_shape, (tuple, list))
    return pl.pallas_call(
        body,
        out_shape=out_shape,
        in_specs=in_specs,
        out_specs=[VMEM] * len(out_shape) if many else VMEM,
        scratch_shapes=scratch,
        compiler_params=pltpu.CompilerParams(vmem_limit_bytes=limit << 20),
    )


def shape(dims, dtype=BF16):
    return jax.ShapeDtypeStruct(dims, dtype)


def dot(a, b):
    return jnp.dot(a, b, preferred_element_type=F32)


def dot_nt(a, b):
    return lax.dot_general(a, b, (((1,), (1,)), ((), ())), preferred_element_type=F32)


def attend(
    rows, width, place, mask, qa, qb, ka, kb, va, vb, wo, mine, theirs, top, total, acc_a, acc_b
):
    block, core = place[0], place[1]
    inverse_root = width**-0.5
    q_a, q_b = qa[...], qb[...]
    query = lax.broadcasted_iota(jnp.int32, (2 * TOK, TOK), 0) % TOK
    key = lax.broadcasted_iota(jnp.int32, (2 * TOK, TOK), 1)

    def scores_of(b):
        return (dot(q_a, ka[b]) + dot(q_b, kb[b])) * inverse_root

    own = (key <= query) & (key < rows)
    masked = jnp.where(own, scores_of(block), MASKED_SCORE)
    best = jnp.max(masked, axis=1, keepdims=True)
    terms = jnp.where(own, jnp.exp(masked - best), 0.0)
    top[...] = best
    total[...] = jnp.sum(terms, axis=1, keepdims=True)
    acc_a[...] = dot_nt(terms.astype(BF16), ka[block])
    acc_b[...] = dot_nt(terms.astype(BF16), kb[block])

    def step(b, carry):
        @pl.when((mask[block, b] == 1) & (b != block))
        def _():
            inside = key < rows
            masked = jnp.where(inside, scores_of(b), MASKED_SCORE)
            old = top[...]
            best = jnp.maximum(old, jnp.max(masked, axis=1, keepdims=True))
            terms = jnp.where(inside, jnp.exp(masked - best), 0.0)
            shrink = jnp.exp(old - best)
            top[...] = best
            total[...] = total[...] * shrink + jnp.sum(terms, axis=1, keepdims=True)
            rounded = terms.astype(BF16)
            acc_a[...] = acc_a[...] * shrink + dot_nt(rounded, ka[b])
            acc_b[...] = acc_b[...] * shrink + dot_nt(rounded, kb[b])

        return carry

    lax.fori_loop(0, mask.shape[1], step, 0)
    inverse = 1.0 / total[...]
    values = []
    for head in range(2):
        span = slice(head * TOK, (head + 1) * TOK)
        value = jnp.zeros((TOK, TOK), F32)
        for acc, up in ((acc_a, va), (acc_b, vb)):
            latent = acc[span, :] * inverse[span, :]
            high = latent.astype(BF16)
            low = (latent - high.astype(F32)).astype(BF16)
            value = value + dot(high, up[head]) + dot(low, up[head])
        values.append(value.T.astype(BF16))
    stacked = jnp.concatenate(values, axis=0)
    runs, _, run, depth = wo.shape
    mine[...] = dot(wo[:, core].reshape(runs * run, depth), stacked).reshape(runs, run, TOK)
    theirs[...] = (
        dot(wo[:, 1 - core].reshape(runs * run, depth), stacked).reshape(runs, run, TOK).astype(BF16)
    )


def split_pair(value):
    high = value.astype(BF16).astype(F32)
    return high, (value - high).astype(BF16).astype(F32)


def tail_rows(value, count):
    high, low = split_pair(value)
    row = lax.broadcasted_iota(jnp.int32, (count, value.shape[1]), 0)
    return jnp.where(row == 0, high, jnp.where(row == 1, low, 0.0))


def make_rows(parts, residual, gain, places, hidden, sent):
    mixed = jnp.sum(parts[...].astype(F32), axis=0)
    held = (residual[...].astype(F32) + mixed).astype(BF16)
    hidden[...] = held
    wide = held.astype(F32)
    square = jnp.sum(wide * wide, axis=0, keepdims=True)
    run = wide.shape[0]
    rows = jnp.concatenate([wide * gain[...], tail_rows(square, TOK - run)], axis=0).astype(BF16)
    sent[...] = dot_nt(places[...], rows).astype(BF16)


def spread_rows(keep_rows, got, out):
    turned = got[...].T[:keep_rows]
    for i in range(out.shape[0]):
        out[i] = turned


def project_up(run, sub, inputs, weights, keep, out):
    count, _, slots = inputs.shape
    features = inputs[:, :run, :].reshape(count * run, slots)
    ends = inputs[:, run : run + 16, :].astype(F32)
    ends = jnp.sum(ends, axis=0)
    square = ends[0:1] + ends[1:2]
    unit = 2 * sub * out.shape[0]
    sums = [jnp.zeros((unit, slots), F32) for _ in range(2)]
    for expert in range(weights.shape[0] // unit):
        part = dot(weights[expert * unit : (expert + 1) * unit, :], features)
        for pick in range(2):
            sums[pick] = sums[pick] + keep[2 * expert + pick : 2 * expert + pick + 1, :] * part
    tail = tail_rows(square, 16)
    for dest in range(out.shape[0]):
        pieces = []
        for pick in range(2):
            for kind in range(2):
                start = kind * unit // 2 + dest * sub
                pieces.append(sums[pick][start : start + sub])
        out[dest] = jnp.concatenate(pieces + [tail], axis=0).astype(BF16)


def activate(sub, got, weight, out):
    total = jnp.sum(got[...].astype(F32), axis=0)
    square = total[4 * sub : 4 * sub + 1] + total[4 * sub + 1 : 4 * sub + 2]
    scale = lax.rsqrt(square / D + EPSILON)
    pieces = []
    for pick in range(2):
        gate = total[2 * pick * sub : (2 * pick + 1) * sub] * scale
        up = total[(2 * pick + 1) * sub : (2 * pick + 2) * sub] * scale
        act = gate / (1.0 + jnp.exp(-gate)) * up
        pieces.append(act * weight[pick : pick + 1, :])
    rounded = jnp.concatenate(pieces, axis=0).astype(BF16)
    for i in range(out.shape[0]):
        out[i] = rounded


def project_down(sub, acts, weights, keep, out):
    count, _, slots = acts.shape
    wide = acts[...].astype(F32)
    first = wide[:, :sub].reshape(count * sub, slots)
    second = wide[:, sub:].reshape(count * sub, slots)
    picked = []
    for expert in range(keep.shape[0] // 2):
        picked.append(
            (
                keep[2 * expert : 2 * expert + 1, :] * first
                + keep[2 * expert + 1 : 2 * expert + 2, :] * second
            ).astype(BF16)
        )
    stacked = jnp.concatenate(picked, axis=0)
    for dest in range(out.shape[0]):
        out[dest] = dot(weights[dest], stacked).astype(BF16)


def finish_rows(got, out):
    total = jnp.sum(got[...].astype(F32), axis=0).astype(BF16)
    run, slots = total.shape
    padded = jnp.concatenate([total, jnp.zeros((TOK - run, slots), BF16)], axis=0)
    out[...] = padded.T


def combine(got, places, hidden, out):
    run, rows = out.shape
    turned = got[...].T[:run]
    added = dot(turned, places[...])
    out[...] = (hidden[...].astype(F32) + added)[:, :rows].astype(BF16)


def exchange(x, axes):
    return lax.all_to_all(x, axes, split_axis=0, concat_axis=0, tiled=True)


def on_device(
    queries,
    latents,
    block_mask,
    value_up,
    out_proj,
    residual,
    norm_gain,
    group_ids,
    expert_ids,
    route_weights,
    w_gate,
    w_up,
    w_down,
):
    ctx_count = lax.axis_size(CTX)
    z_count = lax.axis_size("z")
    xc_count = lax.axis_size(XC)
    my_block = lax.axis_index(CTX)
    core = lax.axis_index("core")
    block_rows, key_width = latents.shape
    heads = queries.shape[1]
    latent_width, value_width = value_up.shape[1:]
    run = residual.shape[1]
    local_experts, _, hidden_units = w_gate.shape
    half = key_width // 2
    pad_rows = TOK - block_rows
    slots = ctx_count * SLOT
    part = hidden_units // z_count
    sub = part // xc_count

    keys = jnp.pad(latents.T, ((0, 0), (0, pad_rows)))
    own_half = lax.dynamic_slice_in_dim(keys, core * half, half, 0)
    keys_a = exchange(jnp.broadcast_to(own_half[None], (ctx_count, half, TOK)), CTX)
    keys_b = lax.ppermute(keys_a, "core", [(0, 1), (1, 0)])

    pairs = local_experts // 2
    both = jnp.stack([w_gate, w_up], axis=1).reshape(pairs, 2, 2, run, z_count, part)
    both = both.transpose(4, 0, 3, 1, 2, 5).reshape(z_count, pairs, run, 4 * part)
    both = exchange(both, "z")
    weights_in = both.transpose(1, 3, 0, 2).reshape(pairs * 4 * part, z_count * run)
    down = w_down.transpose(0, 2, 1).reshape(local_experts, run, z_count, xc_count, sub)
    down = down.transpose(3, 1, 0, 2, 4).reshape(xc_count, run, local_experts * z_count * sub)
    down = exchange(down, XC)

    group_range = jnp.arange(ctx_count)
    expert_range = jnp.arange(local_experts)
    member = jnp.zeros((block_rows, ctx_count), jnp.int32)
    shares = jnp.zeros((block_rows, ctx_count, local_experts), F32)
    for group_slot in range(group_ids.shape[1]):
        group_hit = group_ids[:, group_slot, None] == group_range[None, :]
        member = member + group_hit.astype(jnp.int32)
        for expert_slot in range(expert_ids.shape[2]):
            expert_hit = (
                expert_ids[:, group_slot, expert_slot, None] == expert_range[None, :]
            ).astype(F32)
            shares = shares + group_hit.astype(F32)[:, :, None] * expert_hit[
                :, None, :
            ] * route_weights[:, group_slot, expert_slot, None, None].astype(F32)
    ranking = jnp.cumsum(member, axis=0) - 1
    placement = (
        (member[:, :, None] == 1) & (ranking[:, :, None] == jnp.arange(SLOT)[None, None, :])
    ).astype(BF16)
    sent_weights = jnp.einsum(
        "tge,tgc->gec", shares.astype(BF16), placement, preferred_element_type=F32
    ).astype(BF16)
    got_weights = exchange(sent_weights, CTX)
    weights = got_weights.transpose(1, 0, 2).reshape(local_experts, slots).astype(F32)
    chosen = (weights > 0.0).astype(jnp.int32)
    ordinal = jnp.cumsum(chosen, axis=0) - 1
    keep = jnp.stack(
        [((chosen == 1) & (ordinal == pick)).astype(F32) for pick in range(2)], axis=1
    )
    pick_weight = jnp.sum(keep * weights[:, None, :], axis=0)
    keep = keep.reshape(2 * local_experts, slots)
    places = jnp.pad(placement.reshape(block_rows, slots).T, ((0, 0), (0, pad_rows)))

    wide_q = jnp.pad(queries.transpose(1, 0, 2), ((0, 0), (0, pad_rows), (0, 0)))
    wide_q = wide_q.reshape(heads * TOK, key_width)
    q_low, q_high = wide_q[:, :half], wide_q[:, half:]
    v_low = value_up[:, :half]
    v_high = jnp.pad(value_up[:, half:], ((0, 0), (0, key_width - latent_width), (0, 0)))
    flip = core == 1
    place = jnp.stack([my_block, core]).astype(jnp.int32)
    runs = D // run
    out_weights = out_proj.T.reshape(runs // 2, 2, run, heads * value_width)
    mine, theirs = call(
        functools.partial(attend, block_rows, key_width),
        [shape((runs // 2, run, TOK), F32), shape((runs // 2, run, TOK))],
        [SMEM, SMEM] + [VMEM] * 7,
        [
            pltpu.VMEM((2 * TOK, 1), F32),
            pltpu.VMEM((2 * TOK, 1), F32),
            pltpu.VMEM((2 * TOK, half), F32),
            pltpu.VMEM((2 * TOK, half), F32),
        ],
    )(
        place,
        block_mask,
        jnp.where(flip, q_high, q_low),
        jnp.where(flip, q_low, q_high),
        keys_a,
        keys_b,
        jnp.where(flip, v_high, v_low),
        jnp.where(flip, v_low, v_high),
        out_weights,
    )
    summed = (mine + lax.ppermute(theirs, "core", [(0, 1), (1, 0)]).astype(F32)).astype(BF16)
    parts = exchange(summed, ZX)

    hidden, sent = call(make_rows, [shape((run, TOK)), shape((slots, TOK))], [VMEM] * 4)(
        parts,
        jnp.pad(residual.T, ((0, 0), (0, pad_rows))),
        norm_gain.astype(F32)[:, None],
        places,
    )
    got = exchange(sent.reshape(ctx_count, SLOT, TOK), CTX).reshape(slots, TOK)
    spread = call(
        functools.partial(spread_rows, run + 16), shape((z_count, run + 16, slots)), [VMEM]
    )(got)
    inputs = exchange(spread, "z")
    partial_sums = call(
        functools.partial(project_up, run, sub),
        shape((xc_count, 4 * sub + 16, slots)),
        [VMEM] * 3,
    )(inputs, weights_in, keep)
    acts = call(functools.partial(activate, sub), shape((z_count, 2 * sub, slots)), [VMEM] * 2)(
        exchange(partial_sums, XC), pick_weight
    )
    outputs = call(
        functools.partial(project_down, sub), shape((xc_count, run, slots)), [VMEM] * 3
    )(exchange(acts, "z"), down, keep)
    returned = call(finish_rows, shape((slots, TOK)), [VMEM])(exchange(outputs, XC))
    returned = exchange(returned.reshape(ctx_count, SLOT, TOK), CTX).reshape(slots, TOK)
    out = call(combine, shape((run, block_rows)), [VMEM] * 3)(returned, places, hidden)
    return out.T


def solution(mesh):
    names = ("y", "xh", "z", "xl", "core")
    fine = Mesh(mesh.devices.reshape(8, 2, 8, 2, 2), names)
    return jax.shard_map(
        on_device,
        mesh=fine,
        in_specs=(
            P(CTX, EXP, None),
            P(CTX, None),
            P(),
            P(EXP, None, None),
            P(EXP, None),
            P(CTX, EXP),
            P(EXP),
            P(CTX, None),
            P(CTX, None, None),
            P(CTX, None, None),
            P(CTX, EXP, None),
            P(CTX, EXP, None),
            P(CTX, None, EXP),
        ),
        out_specs=P(CTX, EXP),
        check_vma=False,
    )
```

time: 594 us -> 267 us (0.45)
  waiting for transfers between devices: 443 us -> 98.1 us
  starting transfers between devices: 13.7 us -> 62.2 us
  blocking collectives: 76.3 us -> 47.6 us
  local copies, waits for them, and re-layouts: 16 us -> 34.8 us
  matrix products: 18.7 us -> 0.83 us
  between operations: 14.2 us -> 0.47 us
  Pallas kernels: 0 us -> 9.14 us
    psum x1 -> x0, waiting for transfers between devices: 233 us -> none  [on_device(): lax.psum(up_stack.astype(jnp.bfloat16), 'exp').astype(jnp.float32)]
    reduce_scatter x1 -> x0, waiting for transfers between devices: 101 us -> none  [on_device(): lax.psum_scatter(lax.dot_general(out_proj, attn_value, (((0,), (1,)), (()...]
    all_gather x1 -> x0, waiting for transfers between devices: 90.3 us -> none  [on_device(): part_rows = lax.all_gather(latents, 'ctx', axis=0, tiled=True)]
    all_to_all x2 -> x8, waiting for transfers between devices: 18.7 us -> 98.1 us  [exchange(): return lax.all_to_all(x, axes, split_axis=0, concat_axis=0, tiled=True)]
    psum x1 -> x0, blocking collectives: 56.5 us -> none  [on_device(): square_sum = lax.psum(jnp.sum(hidden_wide * hidden_wide, axis=0), 'exp')]
    all_to_all x2 -> x8, starting transfers between devices: 13.4 us -> 53.5 us  [exchange(): return lax.all_to_all(x, axes, split_axis=0, concat_axis=0, tiled=True)]
    all_to_all x1 -> x3, blocking collectives: 19.8 us -> 47.6 us  [exchange(): return lax.all_to_all(x, axes, split_axis=0, concat_axis=0, tiled=True)]
    dot_general x25 -> x1, matrix products: 18.7 us -> 0.83 us  [on_device(): jnp.einsum('tge,tgc->gec', shares.astype(BF16), placement, preferred_elem...]
  transfers between devices with their start and end apart: 5 -> 10, of which waited for: 5 -> 7; matrix products, arithmetic and copies ran while one was open for 2% -> 17% of each run, Pallas kernels for 0% -> 1%
where the time goes in v1:
time: 267 us; the launch traced here: 266 us
  waiting for transfers between devices  98.1 us (37%)
  starting transfers between devices  62.2 us (23%)
  blocking collectives  47.6 us (18%)
  local copies, waits for them, and re-layouts  34.8 us (13%)
  other arithmetic  12.4 us (5%)
  Pallas kernels  9.14 us (3%)
    all_to_all x8, waiting for transfers between devices, exchange(): return lax.all_to_all(x, axes, split_axis=0, concat_axis=0, tiled=True)  98.1 us
    all_to_all x8, starting transfers between devices, exchange(): return lax.all_to_all(x, axes, split_axis=0, concat_axis=0, tiled=True)  53.5 us
    all_to_all x3, blocking collectives, exchange(): return lax.all_to_all(x, axes, split_axis=0, concat_axis=0, tiled=True)  47.6 us
    another operation x4, local copies, waits for them, and re-layouts, on_device(): jnp.stack([w_gate, w_up], axis=1).reshape(pairs, 2, 2, run, z_count, part)  8.52 us
    reshape x2, local copies, waits for them, and re-layouts, on_device(): both.transpose(1, 3, 0, 2).reshape(pairs * 4 * part, z_count * run)  7.75 us
    transpose x1, other arithmetic, on_device(): both.transpose(4, 0, 3, 1, 2, 5).reshape(z_count, pairs, run, 4 * part)  7.28 us
    ppermute x1, starting transfers between devices, on_device(): keys_b = lax.ppermute(keys_a, 'core', [(0, 1), (1, 0)])  6.67 us
  transfers between devices with their start and end apart: 10, of which 7 were waited for; matrix products, arithmetic and copies ran while one was open for 17% of the time, Pallas kernels for 1%

profile of v1, /device:TPU:1, one launch (start us, length us, event | category | flops | bytes accessed | tf_op | source)
XLA Modules:
  0.0 265.7 jit_solution(12481622798618938267)
XLA Ops:
  2.2 10.2 %all-to-all-start = ((bf16[16,288,128]{2,1,0:T(8,128)(2,1)}), bf16[16,288,128]{2,1,0:T(8,128)(2,1)S(1)}, u32[]{:S(2)}, u32[]{:S(2)}) async-start(bf16[16,288,128]{2,1,0:T(8,128)(2,1)} %broadcast_in_dim.6), calls=%async_computation | async-start | bytes 2359296 | tf_op jit(solution)/shard_map/all_to_all | solution.py:206
  13.1 28.4 %all-to-all-done.ka = bf16[16,288,128]{2,1,0:T(8,128)(2,1)S(1)} async-done(((bf16[16,288,128]{2,1,0:T(8,128)(2,1)}), bf16[16,288,128]{2,1,0:T(8,128)(2,1)S(1)}, u32[]{:S(2)}, u32[]{:S(2)}) %all-to-all-start) | async-done | bytes 1179680 | tf_op jit(solution)/shard_map/all_to_all | solution.py:206
  41.5 6.7 %collective-permute-start = (bf16[16,288,128]{2,1,0:T(8,128)(2,1)S(1)}, bf16[16,288,128]{2,1,0:T(8,128)(2,1)}, u32[]{:S(2)}, u32[]{:S(2)}) collective-permute-start(bf16[16,288,128]{2,1,0:T(8,128)(2,1)S(1)} %all-to-all-done.ka), channel_id=1, source_target_pairs={{0,1},{1,0},{2,3},{3,2},{4,5},{5,4},{6,7},{7,6},{8,9},{9,8},{10,11... | collective-permute-start | bytes 3538952 | tf_op jit(solution)/shard_map/ppermute | solution.py:243
  53.4 3.1 %shard_map.127 = (f32[16,80,128]{2,1,0:T(8,128)S(1)}, bf16[16,80,128]{2,1,0:T(8,128)(2,1)S(1)}) custom-call(s32[2]{0:T(128)S(1)} %pad_add_fusion.1.place, s32[16,16]{1,0:T(8,128)S(1)} %copy-done, bf16[256,288]{1,0:T(8,128)(2,1)S(1)} %get-tuple-element.16.qa, bf16[256,288]{1,0:T(8,128)(2,1)S(1)} %get-tuple-element.15.qb, ...), custom_call_target="tpu_custom_call" | custom-call | tf_op jit(solution)/shard_map/pallas_call | solution.py:295
  63.9 10.2 %all-to-all-start.1 = ((bf16[16,80,128]{2,1,0:T(8,128)(2,1)}), bf16[16,80,128]{2,1,0:T(8,128)(2,1)S(1)}, u32[]{:S(2)}, u32[]{:S(2)}) async-start(bf16[16,80,128]{2,1,0:T(8,128)(2,1)} %add_convert_fusion), calls=%async_computation.1 | async-start | bytes 655360 | tf_op jit(solution)/shard_map/all_to_all | solution.py:206
  75.0 11.2 %all-to-all-done.1.parts = bf16[16,80,128]{2,1,0:T(8,128)(2,1)S(1)} async-done(((bf16[16,80,128]{2,1,0:T(8,128)(2,1)}), bf16[16,80,128]{2,1,0:T(8,128)(2,1)S(1)}, u32[]{:S(2)}, u32[]{:S(2)}) %all-to-all-start.1) | async-done | bytes 327712 | tf_op jit(solution)/shard_map/all_to_all | solution.py:206
  86.2 5.4 %all-to-all-start.5 = ((bf16[16,6,32]{2,1,0:T(8,128)(2,1)}), bf16[16,6,32]{2,1,0:T(8,128)(2,1)S(1)}, u32[]{:S(2)}, u32[]{:S(2)}) async-start(bf16[16,6,32]{2,1,0:T(8,128)(2,1)} %convolution_convert_fusion), calls=%async_computation.5 | async-start | bytes 65536 | tf_op jit(solution)/shard_map/all_to_all | solution.py:206
  92.9 3.2 %copy.47 = bf16[3,2,1,80,8,96]{5,2,1,3,0,4:T(2,128)(2,1)} copy(bf16[3,2,1,80,8,96]{5,4,3,1,0,2:T(8,128)(2,1)S(1)} %stack.27) | data formatting | bytes 1474560 | tf_op jit(solution)/shard_map/stack | solution.py:246
  97.1 3.3 %copy.48 = bf16[3,2,1,80,8,96]{5,2,1,3,0,4:T(2,128)(2,1)} copy(bf16[3,2,1,80,8,96]{5,4,3,1,0,2:T(8,128)(2,1)S(1)} %stack.28) | data formatting | bytes 1474560 | tf_op jit(solution)/shard_map/stack | solution.py:246
  101.3 9.1 %all-to-all-start.2 = ((bf16[16,32,128]{2,1,0:T(8,128)(2,1)}), bf16[16,32,128]{2,1,0:T(8,128)(2,1)S(1)}, u32[]{:S(2)}, u32[]{:S(2)}) async-start(bf16[16,32,128]{2,1,0:T(8,128)(2,1)} %bitcast.15), calls=%async_computation.2 | async-start | bytes 262144 | tf_op jit(solution)/shard_map/all_to_all | solution.py:206
  110.4 7.3 %maximum_bitcast_fusion = bf16[8,3,80,2,2,96]{5,4,3,2,1,0:T(2,128)(2,1)S(1)} fusion(bf16[3,2,1,80,8,96]{5,2,1,3,0,4:T(2,128)(2,1)} %copy.48, bf16[3,2,1,80,8,96]{5,2,1,3,0,4:T(2,128)(2,1)} %copy.47), kind=kLoop, calls=%fused_computation | loop fusion | flops 2949120 | bytes 2949120 | tf_op jit(solution)/shard_map/transpose | solution.py:247
  120.4 3.8 %all-to-all-start.4 = ((bf16[8,3,80,384]{3,2,1,0:T(8,128)(2,1)}), bf16[8,3,80,384]{3,2,1,0:T(8,128)(2,1)S(1)}, u32[]{:S(2)}, u32[]{:S(2)}) async-start(bf16[8,3,80,384]{3,2,1,0:T(8,128)(2,1)} %reshape.448), calls=%async_computation.4 | async-start | bytes 2949120 | tf_op jit(solution)/shard_map/all_to_all | solution.py:206
  125.3 34.7 %all-to-all-done.4 = bf16[8,3,80,384]{3,2,1,0:T(8,128)(2,1)S(1)} async-done(((bf16[8,3,80,384]{3,2,1,0:T(8,128)(2,1)}), bf16[8,3,80,384]{3,2,1,0:T(8,128)(2,1)S(1)}, u32[]{:S(2)}, u32[]{:S(2)}) %all-to-all-start.4) | async-done | bytes 1474592 | tf_op jit(solution)/shard_map/all_to_all | solution.py:206
  161.1 3.5 %all-to-all-start.3 = ((bf16[8,96,512]{2,1,0:T(8,128)(2,1)}), bf16[8,96,512]{2,1,0:T(8,128)(2,1)S(1)}, u32[]{:S(2)}, u32[]{:S(2)}) async-start(bf16[8,96,512]{2,1,0:T(8,128)(2,1)} %shard_map.129), calls=%async_computation.3 | async-start | bytes 1572864 | tf_op jit(solution)/shard_map/all_to_all | solution.py:206
  165.1 4.1 %copy.60 = bf16[3,384,8,80]{3,2,1,0:T(8,128)(2,1)} copy(bf16[3,384,8,80]{1,3,0,2:T(8,128)(2,1)} %bitcast.82) | data formatting | bytes 2949120 | tf_op jit(solution)/shard_map/reshape | solution.py:249
  169.2 3.6 %reshape.466.weights = bf16[1152,640]{1,0:T(8,128)(2,1)S(1)} reshape(bf16[3,384,8,80]{3,2,1,0:T(8,128)(2,1)} %copy.60) | data formatting | bytes 2949120 | tf_op jit(solution)/shard_map/reshape | solution.py:249
  172.8 12.4 %all-to-all-done.3.inputs = bf16[8,96,512]{2,1,0:T(8,128)(2,1)S(1)} async-done(((bf16[8,96,512]{2,1,0:T(8,128)(2,1)}), bf16[8,96,512]{2,1,0:T(8,128)(2,1)S(1)}, u32[]{:S(2)}, u32[]{:S(2)}) %all-to-all-start.3) | async-done | bytes 786464 | tf_op jit(solution)/shard_map/all_to_all | solution.py:206
  187.2 6.9 %all-to-all-start.6 = ((bf16[4,112,512]{2,1,0:T(8,128)(2,1)}), bf16[4,112,512]{2,1,0:T(8,128)(2,1)S(1)}, u32[]{:S(2)}, u32[]{:S(2)}) async-start(bf16[4,112,512]{2,1,0:T(8,128)(2,1)} %shard_map.130), calls=%async_computation.6 | async-start | bytes 917504 | tf_op jit(solution)/shard_map/all_to_all | solution.py:206
  195.5 2.6 copy.58
  201.4 4.3 %all-to-all-start.8 = ((bf16[4,80,1152]{2,1,0:T(8,128)(2,1)}), bf16[4,80,1152]{2,1,0:T(8,128)(2,1)S(1)}, u32[]{:S(2)}, u32[]{:S(2)}) async-start(bf16[4,80,1152]{2,1,0:T(8,128)(2,1)} %copy.59), calls=%async_computation.8 | async-start | bytes 1474560 | tf_op jit(solution)/shard_map/all_to_all | solution.py:206
  205.8 10.1 %all-to-all-done.8.weights = bf16[4,80,1152]{2,1,0:T(8,128)(2,1)S(1)} async-done(((bf16[4,80,1152]{2,1,0:T(8,128)(2,1)}), bf16[4,80,1152]{2,1,0:T(8,128)(2,1)S(1)}, u32[]{:S(2)}, u32[]{:S(2)}) %all-to-all-start.8) | async-done | bytes 737312 | tf_op jit(solution)/shard_map/all_to_all | solution.py:206
  216.0 15.9 %all_to_all.55.acts = bf16[8,48,512]{2,1,0:T(8,128)(2,1)S(1)} all-to-all(bf16[8,48,512]{2,1,0:T(8,128)(2,1)S(1)} %shard_map.131), channel_id=1, replica_groups=mesh['y'=8,'xh'=2,'z'=8,'xl'=2,'core'=2] {'z'}, dimensions={0} | all-to-all | bytes 786432 | tf_op jit(solution)/shard_map/all_to_all | solution.py:206
  233.0 10.4 %all_to_all.56.got = bf16[4,80,512]{2,1,0:T(8,128)(2,1)S(1)} all-to-all(bf16[4,80,512]{2,1,0:T(8,128)(2,1)S(1)} %shard_map.132), channel_id=1, replica_groups=mesh['y'=8,'xh'=2,'z'=8,'xl'=2,'core'=2] {'xl','core'}, dimensions={0} | all-to-all | bytes 655360 | tf_op jit(solution)/shard_map/all_to_all | solution.py:206
  243.6 21.3 %all_to_all.57 = bf16[16,32,128]{2,1,0:T(8,128)(2,1)S(1)} all-to-all(bf16[16,32,128]{2,1,0:T(8,128)(2,1)S(1)} %bitcast.80), channel_id=1, replica_groups=mesh['y'=8,'xh'=2,'z'=8,'xl'=2,'core'=2] {'y','xh'}, dimensions={0} | all-to-all | bytes 262144 | tf_op jit(solution)/shard_map/all_to_all | solution.py:206
  (95 shorter events, 33.3 us)
Async XLA Ops:
  0.0 12.4 %copy-start.13 = (s32[120,3]{0,1:T(4,128)S(1)}, s32[120,3]{0,1:T(4,128)}, u32[]{:S(2)}) copy-start(s32[120,3]{0,1:T(4,128)} %param.20) | copy-start | bytes 4324
  0.0 12.4 %copy-start.10 = (s32[120,3,2]{0,2,1:T(2,128)S(1)}, s32[120,3,2]{0,2,1:T(2,128)}, u32[]{:S(2)}) copy-start(s32[120,3,2]{0,2,1:T(2,128)} %param.21) | copy-start | bytes 8644
  0.9 48.1 %copy-start.6 = (bf16[120,2,576]{0,2,1:T(8,128)(2,1)S(1)}, bf16[120,2,576]{0,2,1:T(8,128)(2,1)}, u32[]{:S(2)}) copy-start(bf16[120,2,576]{0,2,1:T(8,128)(2,1)} %param.13) | copy-start | bytes 829444
  2.2 39.3 %all-to-all-start = ((bf16[16,288,128]{2,1,0:T(8,128)(2,1)}), bf16[16,288,128]{2,1,0:T(8,128)(2,1)S(1)}, u32[]{:S(2)}, u32[]{:S(2)}) async-start(bf16[16,288,128]{2,1,0:T(8,128)(2,1)} %broadcast_in_dim.6), calls=%async_computation | async-start | bytes 2359296 | tf_op jit(solution)/shard_map/all_to_all | solution.py:206
  41.5 11.9 %collective-permute-start = (bf16[16,288,128]{2,1,0:T(8,128)(2,1)S(1)}, bf16[16,288,128]{2,1,0:T(8,128)(2,1)}, u32[]{:S(2)}, u32[]{:S(2)}) collective-permute-start(bf16[16,288,128]{2,1,0:T(8,128)(2,1)S(1)} %all-to-all-done.ka), channel_id=1, source_target_pairs={{0,1},{1,0},{2,3},{3,2},{4,5},{5,4},{6,7},{7,6},{8,9},{9,8},{10,11... | collective-permute-start | bytes 3538952 | tf_op jit(solution)/shard_map/ppermute | solution.py:243
  49.2 4.0 %copy-start.5 = (bf16[2,512,128]{2,1,0:T(8,128)(2,1)S(1)}, bf16[2,512,128]{2,1,0:T(8,128)(2,1)}, u32[]{:S(2)}) copy-start(bf16[2,512,128]{2,1,0:T(8,128)(2,1)} %param.16) | copy-start | bytes 786436
  49.2 4.2 %copy-start = (s32[16,16]{1,0:T(8,128)S(1)}, s32[16,16]{1,0:T(8,128)}, u32[]{:S(2)}) copy-start(s32[16,16]{1,0:T(8,128)} %mask.1) | copy-start | bytes 3076
  53.4 5.3 %copy-start.9 = (bf16[120,3,2]{0,2,1:T(2,128)(2,1)S(1)}, bf16[120,3,2]{0,2,1:T(2,128)(2,1)}, u32[]{:S(2)}) copy-start(bf16[120,3,2]{0,2,1:T(2,128)(2,1)} %param.22) | copy-start | bytes 4324
  53.4 8.8 %copy-start.7 = (s32[120,16]{1,0:T(8,128)S(1)}, s32[120,16]{1,0:T(8,128)}, u32[]{:S(2)}) copy-start(s32[120,16]{1,0:T(8,128)} %broadcast_add_fusion) | copy-start | bytes 23044
  56.5 17.6 %copy-start.14 = (bf16[80]{0:T(256)(128)(2,1)S(1)}, bf16[80]{0:T(256)(128)(2,1)}, u32[]{:S(2)}) copy-start(bf16[80]{0:T(256)(128)(2,1)} %param.19) | copy-start | bytes 484
  56.6 17.6 %copy-start.11 = (s32[120]{0:T(128)S(1)}, s32[120]{0:T(128)}, u32[]{:S(2)}) copy-start(s32[120]{0:T(128)} %get-tuple-element.23) | copy-start | bytes 1444
  56.6 17.6 %copy-start.12 = (s32[120]{0:T(128)S(1)}, s32[120]{0:T(128)}, u32[]{:S(2)}) copy-start(s32[120]{0:T(128)} %get-tuple-element.24) | copy-start | bytes 1444
  56.6 35.2 %copy-start.8 = (bf16[120,80]{0,1:T(8,128)(2,1)S(1)}, bf16[120,80]{0,1:T(8,128)(2,1)}, u32[]{:S(2)}) copy-start(bf16[120,80]{0,1:T(8,128)(2,1)} %param.18) | copy-start | bytes 57604
  56.6 35.2 %copy-start.2 = (bf16[6,80,768]{2,1,0:T(8,128)(2,1)S(1)}, bf16[6,80,768]{2,1,0:T(8,128)(2,1)}, u32[]{:S(2)}) copy-start(bf16[6,80,768]{2,1,0:T(8,128)(2,1)} %param.23) | copy-start | bytes 2211844
  56.6 6.5 %collective-permute-start.1 = (bf16[16,80,128]{2,1,0:T(8,128)(2,1)S(1)}, bf16[16,80,128]{2,1,0:T(8,128)(2,1)S(1)}, u32[]{:S(2)}, u32[]{:S(2)}) collective-permute-start(bf16[16,80,128]{2,1,0:T(8,128)(2,1)S(1)} %get-tuple-element.10), channel_id=1, source_target_pairs={{0,1},{1,0},{2,3},{3,2},{4,5},{5,4},{6,7},{7,6},{8,9},{9,8},{10,11... | collective-permute-start | bytes 983048 | tf_op jit(solution)/shard_map/ppermute | solution.py:316
  63.9 22.3 %all-to-all-start.1 = ((bf16[16,80,128]{2,1,0:T(8,128)(2,1)}), bf16[16,80,128]{2,1,0:T(8,128)(2,1)S(1)}, u32[]{:S(2)}, u32[]{:S(2)}) async-start(bf16[16,80,128]{2,1,0:T(8,128)(2,1)} %add_convert_fusion), calls=%async_computation.1 | async-start | bytes 655360 | tf_op jit(solution)/shard_map/all_to_all | solution.py:206
  86.2 15.1 %all-to-all-start.5 = ((bf16[16,6,32]{2,1,0:T(8,128)(2,1)}), bf16[16,6,32]{2,1,0:T(8,128)(2,1)S(1)}, u32[]{:S(2)}, u32[]{:S(2)}) async-start(bf16[16,6,32]{2,1,0:T(8,128)(2,1)} %convolution_convert_fusion), calls=%async_computation.5 | async-start | bytes 65536 | tf_op jit(solution)/shard_map/all_to_all | solution.py:206
  91.8 4.3 %copy-start.3 = (bf16[6,80,768]{2,1,0:T(8,128)(2,1)S(1)}, bf16[6,80,768]{2,1,0:T(8,128)(2,1)}, u32[]{:S(2)}) copy-start(bf16[6,80,768]{2,1,0:T(8,128)(2,1)} %param.24) | copy-start | bytes 2211844
  101.3 19.1 %all-to-all-start.2 = ((bf16[16,32,128]{2,1,0:T(8,128)(2,1)}), bf16[16,32,128]{2,1,0:T(8,128)(2,1)S(1)}, u32[]{:S(2)}, u32[]{:S(2)}) async-start(bf16[16,32,128]{2,1,0:T(8,128)(2,1)} %bitcast.15), calls=%async_computation.2 | async-start | bytes 262144 | tf_op jit(solution)/shard_map/all_to_all | solution.py:206
  120.4 39.5 %all-to-all-start.4 = ((bf16[8,3,80,384]{3,2,1,0:T(8,128)(2,1)}), bf16[8,3,80,384]{3,2,1,0:T(8,128)(2,1)S(1)}, u32[]{:S(2)}, u32[]{:S(2)}) async-start(bf16[8,3,80,384]{3,2,1,0:T(8,128)(2,1)} %reshape.448), calls=%async_computation.4 | async-start | bytes 2949120 | tf_op jit(solution)/shard_map/all_to_all | solution.py:206
  161.1 24.1 %all-to-all-start.3 = ((bf16[8,96,512]{2,1,0:T(8,128)(2,1)}), bf16[8,96,512]{2,1,0:T(8,128)(2,1)S(1)}, u32[]{:S(2)}, u32[]{:S(2)}) async-start(bf16[8,96,512]{2,1,0:T(8,128)(2,1)} %shard_map.129), calls=%async_computation.3 | async-start | bytes 1572864 | tf_op jit(solution)/shard_map/all_to_all | solution.py:206
  172.8 21.3 %copy-start.4 = (bf16[6,768,80]{1,2,0:T(8,128)(2,1)S(1)}, bf16[6,768,80]{1,2,0:T(8,128)(2,1)}, u32[]{:S(2)}) copy-start(bf16[6,768,80]{1,2,0:T(8,128)(2,1)} %param.25) | copy-start | bytes 2211844
  187.2 14.2 %all-to-all-start.6 = ((bf16[4,112,512]{2,1,0:T(8,128)(2,1)}), bf16[4,112,512]{2,1,0:T(8,128)(2,1)S(1)}, u32[]{:S(2)}, u32[]{:S(2)}) async-start(bf16[4,112,512]{2,1,0:T(8,128)(2,1)} %shard_map.130), calls=%async_computation.6 | async-start | bytes 917504 | tf_op jit(solution)/shard_map/all_to_all | solution.py:206
  201.4 14.6 %all-to-all-start.8 = ((bf16[4,80,1152]{2,1,0:T(8,128)(2,1)}), bf16[4,80,1152]{2,1,0:T(8,128)(2,1)S(1)}, u32[]{:S(2)}, u32[]{:S(2)}) async-start(bf16[4,80,1152]{2,1,0:T(8,128)(2,1)} %copy.59), calls=%async_computation.8 | async-start | bytes 1474560 | tf_op jit(solution)/shard_map/all_to_all | solution.py:206
  (2 other events, 5.1 us)

commit v2 on v1

--- a/solution.py
+++ b/solution.py
@@ -116,7 +116,7 @@
     return jnp.where(row == 0, high, jnp.where(row == 1, low, 0.0))
 
 
-def make_rows(parts, residual, gain, places, hidden, sent):
+def make_rows(parts, residual, gain, places, shares, hidden, sent):
     mixed = jnp.sum(parts[...].astype(F32), axis=0)
     held = (residual[...].astype(F32) + mixed).astype(BF16)
     hidden[...] = held
@@ -124,18 +124,84 @@
     square = jnp.sum(wide * wide, axis=0, keepdims=True)
     run = wide.shape[0]
     rows = jnp.concatenate([wide * gain[...], tail_rows(square, TOK - run)], axis=0).astype(BF16)
-    sent[...] = dot_nt(places[...], rows).astype(BF16)
-
-
-def spread_rows(keep_rows, got, out):
-    turned = got[...].T[:keep_rows]
+    sent[...] = (dot_nt(places[...], rows) + shares[...].astype(F32)).astype(BF16)
+
+
+def spread_rows(keep_rows, first, got, out, keep, weight):
+    turned = got[...].T
+    kept = turned[:keep_rows]
     for i in range(out.shape[0]):
-        out[i] = turned
-
-
-def project_up(run, sub, inputs, weights, keep, out):
+        out[i] = kept
+    count = keep.shape[0] // 2
+    weights = turned[first : first + 16].astype(F32)
+    seen = jnp.zeros((1, weights.shape[1]), F32)
+    picked = [jnp.zeros((1, weights.shape[1]), F32) for _ in range(2)]
+    for expert in range(count):
+        row = weights[expert : expert + 1]
+        chosen = jnp.where(row > 0.0, 1.0, 0.0)
+        for pick in range(2):
+            flag = jnp.where(seen == pick, chosen, 0.0)
+            keep[2 * expert + pick : 2 * expert + pick + 1, :] = flag
+            picked[pick] = picked[pick] + flag * row
+        seen = seen + chosen
+    weight[...] = jnp.concatenate(picked, axis=0)
+
+
+def pack_in(place, gate, up, *refs):
+    outs, held = refs[:-1], refs[-1]
+    count = held.shape[0]
+    part = gate.shape[2] // count
+    for pair in range(held.shape[1]):
+        for z in range(count):
+            span = slice(z * part, (z + 1) * part)
+            pieces = []
+            for expert in (2 * pair, 2 * pair + 1):
+                pieces += [gate[expert, :, span], up[expert, :, span]]
+            held[z, pair] = jnp.concatenate(pieces, axis=1)
+    for shift in range(count):
+        outs[shift][...] = held[lax.rem(place[2] + shift, count)]
+
+
+def turn_in(*refs):
+    got, out = refs[:-1], refs[-1]
+    for pair in range(got[0].shape[0]):
+        wide = jnp.concatenate([g[pair] for g in got], axis=0)
+        out[pair * wide.shape[1] : (pair + 1) * wide.shape[1], :] = wide.T
+
+
+def pack_down(sub, place, weights, *refs):
+    outs, held = refs[:-1], refs[-1]
+    experts, run, hidden = weights.shape
+    count = held.shape[0]
+    per = hidden // count
+    source = lax.broadcasted_iota(jnp.int32, (hidden, 1), 0)
+    dest = (source % (count * sub)) // sub
+    spot = (source // (count * sub)) * sub + source % sub
+    column = lax.broadcasted_iota(jnp.int32, (hidden, count * 2 * TOK), 1)
+    for odd in range(2):
+        goal = dest * 2 * TOK + spot + jnp.where(spot >= TOK, odd * (2 * TOK - per), 0)
+        order = jnp.where(column == goal, 1.0, 0.0).astype(BF16)
+        stacked = jnp.concatenate([weights[i] for i in range(odd, experts, 2)], axis=0)
+        moved = dot(stacked, order).astype(BF16).reshape(experts // 2, run, count * 2 * TOK)
+        for pair in range(experts // 2):
+            for i in range(count):
+                a = moved[pair, :, i * 2 * TOK : i * 2 * TOK + TOK]
+                b = moved[pair, :, i * 2 * TOK + TOK : (i + 1) * 2 * TOK]
+                first, last = (2 * pair + odd) * TOK, (experts + pair) * TOK
+                held[i, :, first : first + TOK] = a
+                if odd == 0:
+                    held[i, :, last : last + TOK] = b
+                else:
+                    held[i, :, last : last + TOK] += b
+    for flip in range(count):
+        outs[flip][...] = held[place[3] ^ flip]
+
+
+def project_up(run, sub, place, inputs, weights, keep, out):
     count, _, slots = inputs.shape
-    features = inputs[:, :run, :].reshape(count * run, slots)
+    features = jnp.concatenate(
+        [inputs[lax.rem(place[2] + count - i, count), :run, :] for i in range(count)], axis=0
+    )
     ends = inputs[:, run : run + 16, :].astype(F32)
     ends = jnp.sum(ends, axis=0)
     square = ends[0:1] + ends[1:2]
@@ -170,22 +236,23 @@
         out[i] = rounded
 
 
-def project_down(sub, acts, weights, keep, out):
+def project_down(sub, place, acts, keep, *refs):
+    weights, out = refs[:-1], refs[-1]
     count, _, slots = acts.shape
     wide = acts[...].astype(F32)
     first = wide[:, :sub].reshape(count * sub, slots)
     second = wide[:, sub:].reshape(count * sub, slots)
-    picked = []
+    heads, tails = [], []
     for expert in range(keep.shape[0] // 2):
-        picked.append(
-            (
-                keep[2 * expert : 2 * expert + 1, :] * first
-                + keep[2 * expert + 1 : 2 * expert + 2, :] * second
-            ).astype(BF16)
-        )
-    stacked = jnp.concatenate(picked, axis=0)
-    for dest in range(out.shape[0]):
-        out[dest] = dot(weights[dest], stacked).astype(BF16)
+        picked = (
+            keep[2 * expert : 2 * expert + 1, :] * first
+            + keep[2 * expert + 1 : 2 * expert + 2, :] * second
+        ).astype(BF16)
+        heads.append(picked[:TOK])
+        tails.append(picked[TOK:])
+    stacked = jnp.concatenate(heads + tails, axis=0)
+    for flip in range(len(weights)):
+        out[place[3] ^ flip] = dot(weights[flip][...], stacked).astype(BF16)
 
 
 def finish_rows(got, out):
@@ -242,14 +309,30 @@
     keys_a = exchange(jnp.broadcast_to(own_half[None], (ctx_count, half, TOK)), CTX)
     keys_b = lax.ppermute(keys_a, "core", [(0, 1), (1, 0)])
 
+    place = jnp.stack([my_block, core, lax.axis_index("z"), lax.axis_index(XC)]).astype(jnp.int32)
     pairs = local_experts // 2
-    both = jnp.stack([w_gate, w_up], axis=1).reshape(pairs, 2, 2, run, z_count, part)
-    both = both.transpose(4, 0, 3, 1, 2, 5).reshape(z_count, pairs, run, 4 * part)
-    both = exchange(both, "z")
-    weights_in = both.transpose(1, 3, 0, 2).reshape(pairs * 4 * part, z_count * run)
-    down = w_down.transpose(0, 2, 1).reshape(local_experts, run, z_count, xc_count, sub)
-    down = down.transpose(3, 1, 0, 2, 4).reshape(xc_count, run, local_experts * z_count * sub)
-    down = exchange(down, XC)
+    block = (pairs, run, 4 * part)
+    packed = call(
+        pack_in,
+        [shape(block)] * z_count,
+        [SMEM] + [VMEM] * 2,
+        [pltpu.VMEM((z_count,) + block, BF16)],
+    )(place, w_gate, w_up)
+    moved_in = [packed[0]] + [
+        lax.ppermute(packed[i], "z", [(a, (a + i) % z_count) for a in range(z_count)])
+        for i in range(1, z_count)
+    ]
+    block = (run, local_experts * z_count * sub)
+    packed = call(
+        functools.partial(pack_down, sub),
+        [shape(block)] * xc_count,
+        [SMEM, VMEM],
+        [pltpu.VMEM((xc_count,) + block, BF16)],
+    )(place, w_down.transpose(0, 2, 1))
+    moved_down = [packed[0]] + [
+        lax.ppermute(packed[i], XC, [(a, a ^ i) for a in range(xc_count)])
+        for i in range(1, xc_count)
+    ]
 
     group_range = jnp.arange(ctx_count)
     expert_range = jnp.arange(local_experts)
@@ -269,18 +352,14 @@
     placement = (
         (member[:, :, None] == 1) & (ranking[:, :, None] == jnp.arange(SLOT)[None, None, :])
     ).astype(BF16)
-    sent_weights = jnp.einsum(
-        "tge,tgc->gec", shares.astype(BF16), placement, preferred_element_type=F32
+    first_share = run + 16
+    slot_shares = jnp.einsum(
+        "tge,tgc->gce", shares.astype(BF16), placement, preferred_element_type=F32
     ).astype(BF16)
-    got_weights = exchange(sent_weights, CTX)
-    weights = got_weights.transpose(1, 0, 2).reshape(local_experts, slots).astype(F32)
-    chosen = (weights > 0.0).astype(jnp.int32)
-    ordinal = jnp.cumsum(chosen, axis=0) - 1
-    keep = jnp.stack(
-        [((chosen == 1) & (ordinal == pick)).astype(F32) for pick in range(2)], axis=1
-    )
-    pick_weight = jnp.sum(keep * weights[:, None, :], axis=0)
-    keep = keep.reshape(2 * local_experts, slots)
+    slot_shares = jnp.pad(
+        slot_shares.reshape(slots, local_experts),
+        ((0, 0), (first_share, TOK - first_share - local_experts)),
+    )
     places = jnp.pad(placement.reshape(block_rows, slots).T, ((0, 0), (0, pad_rows)))
 
     wide_q = jnp.pad(queries.transpose(1, 0, 2), ((0, 0), (0, pad_rows), (0, 0)))
@@ -289,7 +368,6 @@
     v_low = value_up[:, :half]
     v_high = jnp.pad(value_up[:, half:], ((0, 0), (0, key_width - latent_width), (0, 0)))
     flip = core == 1
-    place = jnp.stack([my_block, core]).astype(jnp.int32)
     runs = D // run
     out_weights = out_proj.T.reshape(runs // 2, 2, run, heads * value_width)
     mine, theirs = call(
@@ -315,29 +393,42 @@
     )
     summed = (mine + lax.ppermute(theirs, "core", [(0, 1), (1, 0)]).astype(F32)).astype(BF16)
     parts = exchange(summed, ZX)
-
-    hidden, sent = call(make_rows, [shape((run, TOK)), shape((slots, TOK))], [VMEM] * 4)(
+    hidden, sent = call(make_rows, [shape((run, TOK)), shape((slots, TOK))], [VMEM] * 5)(
         parts,
         jnp.pad(residual.T, ((0, 0), (0, pad_rows))),
         norm_gain.astype(F32)[:, None],
         places,
-    )
+        slot_shares,
+    )
+    sent, *moved_in = lax.optimization_barrier((sent, *moved_in))
+    weights_in = call(
+        turn_in, shape((pairs * 4 * part, z_count * run)), [VMEM] * z_count
+    )(*moved_in)
     got = exchange(sent.reshape(ctx_count, SLOT, TOK), CTX).reshape(slots, TOK)
-    spread = call(
-        functools.partial(spread_rows, run + 16), shape((z_count, run + 16, slots)), [VMEM]
+    spread, keep, pick_weight = call(
+        functools.partial(spread_rows, run + 16, first_share),
+        [
+            shape((z_count, run + 16, slots)),
+            shape((2 * local_experts, slots), F32),
+            shape((2, slots), F32),
+        ],
+        [VMEM],
     )(got)
+    spread, *moved_down = lax.optimization_barrier((spread, *moved_down))
     inputs = exchange(spread, "z")
     partial_sums = call(
         functools.partial(project_up, run, sub),
         shape((xc_count, 4 * sub + 16, slots)),
-        [VMEM] * 3,
-    )(inputs, weights_in, keep)
+        [SMEM] + [VMEM] * 3,
+    )(place, inputs, weights_in, keep)
     acts = call(functools.partial(activate, sub), shape((z_count, 2 * sub, slots)), [VMEM] * 2)(
         exchange(partial_sums, XC), pick_weight
     )
     outputs = call(
-        functools.partial(project_down, sub), shape((xc_count, run, slots)), [VMEM] * 3
-    )(exchange(acts, "z"), down, keep)
+        functools.partial(project_down, sub),
+        shape((xc_count, run, slots)),
+        [SMEM] + [VMEM] * (2 + xc_count),
+    )(place, exchange(acts, "z"), keep, *moved_down)
     returned = call(finish_rows, shape((slots, TOK)), [VMEM])(exchange(outputs, XC))
     returned = exchange(returned.reshape(ctx_count, SLOT, TOK), CTX).reshape(slots, TOK)
     out = call(combine, shape((run, block_rows)), [VMEM] * 3)(returned, places, hidden)

time: 267 us -> 219 us (0.82)
  waiting for transfers between devices: 98.1 us -> 46.1 us
  local copies, waits for them, and re-layouts: 34.8 us -> 13 us
  starting transfers between devices: 62.2 us -> 78.8 us
  blocking collectives: 47.6 us -> 55.2 us
  Pallas kernels: 9.14 us -> 15 us
  other arithmetic: 12.4 us -> 8.56 us
    all_to_all x8 -> x4, waiting for transfers between devices: 98.1 us -> 33.7 us  [exchange(): return lax.all_to_all(x, axes, split_axis=0, concat_axis=0, tiled=True)]
    ppermute x0 -> x10, starting transfers between devices: none -> 47.3 us  [the longest x7 38.7 us: on_device(): lax.ppermute(packed[i], 'z', [(a, (a + i) % z_count) for a in range(z_cou...]
    all_to_all x8 -> x4, starting transfers between devices: 53.5 us -> 22.8 us  [exchange(): return lax.all_to_all(x, axes, split_axis=0, concat_axis=0, tiled=True)]
    reshape x6 -> x0, local copies, waits for them, and re-layouts: 12.6 us -> none  [the longest x2 7.75 us: on_device(): both.transpose(1, 3, 0, 2).reshape(pairs * 4 * part, z_count * run)]
    ppermute x0 -> x10, waiting for transfers between devices: none -> 11 us  [the longest x7 8.64 us: on_device(): lax.ppermute(packed[i], 'z', [(a, (a + i) % z_count) for a in range(z_cou...]
    another operation x4 -> x0, local copies, waits for them, and re-layouts: 8.52 us -> none  [on_device(): jnp.stack([w_gate, w_up], axis=1).reshape(pairs, 2, 2, run, z_count, part)]
    all_to_all x3 -> x4, blocking collectives: 47.6 us -> 55.2 us  [exchange(): return lax.all_to_all(x, axes, split_axis=0, concat_axis=0, tiled=True)]
    transpose x1 -> x0, other arithmetic: 7.28 us -> none  [on_device(): both.transpose(4, 0, 3, 1, 2, 5).reshape(z_count, pairs, run, 4 * part)]
  transfers between devices with their start and end apart: 10 -> 16, of which waited for: 7 -> 7; matrix products, arithmetic and copies ran while one was open for 17% -> 7% of each run, Pallas kernels for 1% -> 5%
where the time goes in v2:
time: 219 us; the launch traced here: 218 us
  starting transfers between devices  78.8 us (36%)
  blocking collectives  55.2 us (25%)
  waiting for transfers between devices  46.1 us (21%)
  Pallas kernels  15 us (7%)
  local copies, waits for them, and re-layouts  13 us (6%)
  other arithmetic  8.56 us (4%)
    all_to_all x4, blocking collectives, exchange(): return lax.all_to_all(x, axes, split_axis=0, concat_axis=0, tiled=True)  55.2 us
    ppermute x7, starting transfers between devices, on_device(): lax.ppermute(packed[i], 'z', [(a, (a + i) % z_count) for a in range(z_cou...  38.7 us
    all_to_all x4, waiting for transfers between devices, exchange(): return lax.all_to_all(x, axes, split_axis=0, concat_axis=0, tiled=True)  33.7 us
    all_to_all x4, starting transfers between devices, exchange(): return lax.all_to_all(x, axes, split_axis=0, concat_axis=0, tiled=True)  22.8 us
    ppermute x7, waiting for transfers between devices, on_device(): lax.ppermute(packed[i], 'z', [(a, (a + i) % z_count) for a in range(z_cou...  8.64 us
    ppermute x3, starting transfers between devices, on_device(): lax.ppermute(packed[i], XC, [(a, a ^ i) for a in range(xc_count)])  8.59 us
    unnamed x67, local copies, waits for them, and re-layouts  6.76 us
    ppermute x1, starting transfers between devices, on_device(): keys_b = lax.ppermute(keys_a, 'core', [(0, 1), (1, 0)])  6.67 us
  transfers between devices with their start and end apart: 16, of which 7 were waited for; matrix products, arithmetic and copies ran while one was open for 7% of the time, Pallas kernels for 5%

profile of v2, /device:TPU:1, one launch (start us, length us, event | category | flops | bytes accessed | tf_op | source)
XLA Modules:
  0.0 217.5 jit_solution(1184874020149166560)
XLA Ops:
  2.1 10.3 %all-to-all-start = ((bf16[16,288,128]{2,1,0:T(8,128)(2,1)}), bf16[16,288,128]{2,1,0:T(8,128)(2,1)S(1)}, u32[]{:S(2)}, u32[]{:S(2)}) async-start(bf16[16,288,128]{2,1,0:T(8,128)(2,1)} %broadcast_in_dim.6), calls=%async_computation | async-start | bytes 2359296 | tf_op jit(solution)/shard_map/all_to_all | solution.py:273
  14.7 4.0 %collective-permute-start.2 = (bf16[3,80,384]{2,1,0:T(8,128)(2,1)}, bf16[3,80,384]{2,1,0:T(8,128)(2,1)S(1)}, u32[]{:S(2)}, u32[]{:S(2)}) collective-permute-start(bf16[3,80,384]{2,1,0:T(8,128)(2,1)} %get-tuple-element.42), channel_id=1, source_target_pairs={{0,4},{4,8},{8,12},{12,16},{16,20},{20,24},{24,28},{28,0},{1,5},{5... | collective-permute-start | bytes 552968 | tf_op jit(solution)/shard_map/ppermute | solution.py:322
  18.7 5.8 %collective-permute-start.3 = (bf16[3,80,384]{2,1,0:T(8,128)(2,1)}, bf16[3,80,384]{2,1,0:T(8,128)(2,1)S(1)}, u32[]{:S(2)}, u32[]{:S(2)}) collective-permute-start(bf16[3,80,384]{2,1,0:T(8,128)(2,1)} %get-tuple-element.43), channel_id=1, source_target_pairs={{0,8},{4,12},{8,16},{12,20},{16,24},{20,28},{24,0},{28,4},{1,9},{5... | collective-permute-start | bytes 552968 | tf_op jit(solution)/shard_map/ppermute | solution.py:322
  24.5 7.0 %collective-permute-start.4 = (bf16[3,80,384]{2,1,0:T(8,128)(2,1)}, bf16[3,80,384]{2,1,0:T(8,128)(2,1)S(1)}, u32[]{:S(2)}, u32[]{:S(2)}) collective-permute-start(bf16[3,80,384]{2,1,0:T(8,128)(2,1)} %get-tuple-element.44), channel_id=1, source_target_pairs={{0,12},{4,16},{8,20},{12,24},{16,28},{20,0},{24,4},{28,8},{1,13},{... | collective-permute-start | bytes 552968 | tf_op jit(solution)/shard_map/ppermute | solution.py:322
  31.6 2.8 %collective-permute-start.5 = (bf16[3,80,384]{2,1,0:T(8,128)(2,1)}, bf16[3,80,384]{2,1,0:T(8,128)(2,1)S(1)}, u32[]{:S(2)}, u32[]{:S(2)}) collective-permute-start(bf16[3,80,384]{2,1,0:T(8,128)(2,1)} %get-tuple-element.45), channel_id=1, source_target_pairs={{0,16},{4,20},{8,24},{12,28},{16,0},{20,4},{24,8},{28,12},{1,17},{... | collective-permute-start | bytes 552968 | tf_op jit(solution)/shard_map/ppermute | solution.py:322
  35.2 6.4 %all-to-all-done.ka = bf16[16,288,128]{2,1,0:T(8,128)(2,1)S(1)} async-done(((bf16[16,288,128]{2,1,0:T(8,128)(2,1)}), bf16[16,288,128]{2,1,0:T(8,128)(2,1)S(1)}, u32[]{:S(2)}, u32[]{:S(2)}) %all-to-all-start) | async-done | bytes 1179680 | tf_op jit(solution)/shard_map/all_to_all | solution.py:273
  41.6 6.7 %collective-permute-start = (bf16[16,288,128]{2,1,0:T(8,128)(2,1)S(1)}, bf16[16,288,128]{2,1,0:T(8,128)(2,1)}, u32[]{:S(2)}, u32[]{:S(2)}) collective-permute-start(bf16[16,288,128]{2,1,0:T(8,128)(2,1)S(1)} %all-to-all-done.ka), channel_id=1, source_target_pairs={{0,1},{1,0},{2,3},{3,2},{4,5},{5,4},{6,7},{7,6},{8,9},{9,8},{10,11... | collective-permute-start | bytes 3538952 | tf_op jit(solution)/shard_map/ppermute | solution.py:310
  60.0 3.1 %shard_map.127 = (f32[16,80,128]{2,1,0:T(8,128)S(1)}, bf16[16,80,128]{2,1,0:T(8,128)(2,1)S(1)}) custom-call(s32[4]{0:T(128)S(1)} %pad_add_fusion.place, s32[16,16]{1,0:T(8,128)S(1)} %copy-done.17, bf16[256,288]{1,0:T(8,128)(2,1)S(1)} %get-tuple-element.74.qa, bf16[256,288]{1,0:T(8,128)(2,1)S(1)} %get-tuple-element.73.qb, ...), custom_call_target="tpu_custom_call" | custom-call | tf_op jit(solution)/shard_map/pallas_call | solution.py:373
  66.9 10.6 %collective-permute-start.6 = (bf16[3,80,384]{2,1,0:T(8,128)(2,1)}, bf16[3,80,384]{2,1,0:T(8,128)(2,1)S(1)}, u32[]{:S(2)}, u32[]{:S(2)}) collective-permute-start(bf16[3,80,384]{2,1,0:T(8,128)(2,1)} %get-tuple-element.46), channel_id=1, source_target_pairs={{0,20},{4,24},{8,28},{12,0},{16,4},{20,8},{24,12},{28,16},{1,21},{... | collective-permute-start | bytes 552968 | tf_op jit(solution)/shard_map/ppermute | solution.py:322
  78.3 3.7 %all-to-all-start.1 = ((bf16[16,80,128]{2,1,0:T(8,128)(2,1)}), bf16[16,80,128]{2,1,0:T(8,128)(2,1)S(1)}, u32[]{:S(2)}, u32[]{:S(2)}) async-start(bf16[16,80,128]{2,1,0:T(8,128)(2,1)} %add_convert_fusion), calls=%async_computation.1 | async-start | bytes 655360 | tf_op jit(solution)/shard_map/all_to_all | solution.py:273
  82.7 5.3 %collective-permute-start.7 = (bf16[3,80,384]{2,1,0:T(8,128)(2,1)S(1)}, bf16[3,80,384]{2,1,0:T(8,128)(2,1)S(1)}, u32[]{:S(2)}, u32[]{:S(2)}) collective-permute-start(bf16[3,80,384]{2,1,0:T(8,128)(2,1)S(1)} %copy-done.21), channel_id=1, source_target_pairs={{0,24},{4,28},{8,0},{12,4},{16,8},{20,12},{24,16},{28,20},{1,25},{... | collective-permute-start | bytes 552968 | tf_op jit(solution)/shard_map/ppermute | solution.py:322
  88.1 3.1 %collective-permute-start.8 = (bf16[3,80,384]{2,1,0:T(8,128)(2,1)S(1)}, bf16[3,80,384]{2,1,0:T(8,128)(2,1)S(1)}, u32[]{:S(2)}, u32[]{:S(2)}) collective-permute-start(bf16[3,80,384]{2,1,0:T(8,128)(2,1)S(1)} %copy-done.19), channel_id=1, source_target_pairs={{0,28},{4,0},{8,4},{12,8},{16,12},{20,16},{24,20},{28,24},{1,29},{... | collective-permute-start | bytes 552968 | tf_op jit(solution)/shard_map/ppermute | solution.py:322
  91.9 6.9 %all-to-all-done.1.parts = bf16[16,80,128]{2,1,0:T(8,128)(2,1)S(1)} async-done(((bf16[16,80,128]{2,1,0:T(8,128)(2,1)}), bf16[16,80,128]{2,1,0:T(8,128)(2,1)S(1)}, u32[]{:S(2)}, u32[]{:S(2)}) %all-to-all-start.1) | async-done | bytes 327712 | tf_op jit(solution)/shard_map/all_to_all | solution.py:273
  99.7 4.5 %collective-permute-done.7.refs_6_ = bf16[3,80,384]{2,1,0:T(8,128)(2,1)S(1)} collective-permute-done((bf16[3,80,384]{2,1,0:T(8,128)(2,1)S(1)}, bf16[3,80,384]{2,1,0:T(8,128)(2,1)S(1)}, u32[]{:S(2)}, u32[]{:S(2)}) %collective-permute-start.7) | collective-permute-done | bytes 184352 | tf_op jit(solution)/shard_map/ppermute | solution.py:322
  104.3 4.1 %collective-permute-done.8.refs_7_ = bf16[3,80,384]{2,1,0:T(8,128)(2,1)S(1)} collective-permute-done((bf16[3,80,384]{2,1,0:T(8,128)(2,1)S(1)}, bf16[3,80,384]{2,1,0:T(8,128)(2,1)S(1)}, u32[]{:S(2)}, u32[]{:S(2)}) %collective-permute-start.8) | collective-permute-done | bytes 184352 | tf_op jit(solution)/shard_map/ppermute | solution.py:322
  108.4 4.1 %all-to-all-start.2 = ((bf16[16,32,128]{2,1,0:T(8,128)(2,1)}), bf16[16,32,128]{2,1,0:T(8,128)(2,1)S(1)}, u32[]{:S(2)}, u32[]{:S(2)}) async-start(bf16[16,32,128]{2,1,0:T(8,128)(2,1)} %bitcast.30), calls=%async_computation.2 | async-start | bytes 262144 | tf_op jit(solution)/shard_map/all_to_all | solution.py:273
  112.5 3.0 %shard_map.131 = (bf16[80,1152]{1,0:T(8,128)(2,1)S(1)}, bf16[80,1152]{1,0:T(8,128)(2,1)}, bf16[80,1152]{1,0:T(8,128)(2,1)}, bf16[80,1152]{1,0:T(8,128)(2,1)}) custom-call(s32[4]{0:T(128)S(1)} %pad_add_fusion.place, bf16[6,80,768]{2,1,0:T(8,128)(2,1)S(1)} %bitcast.64), custom_call_target="tpu_custom_call" | custom-call | tf_op jit(solution)/shard_map/pallas_call | solution.py:326
  117.7 4.5 %collective-permute-start.11 = (bf16[80,1152]{1,0:T(8,128)(2,1)}, bf16[80,1152]{1,0:T(8,128)(2,1)S(1)}, u32[]{:S(2)}, u32[]{:S(2)}) collective-permute-start(bf16[80,1152]{1,0:T(8,128)(2,1)} %get-tuple-element.54), channel_id=1, source_target_pairs={{0,3},{1,2},{2,1},{3,0},{4,7},{5,6},{6,5},{7,4},{8,11},{9,10},{10,... | collective-permute-start | bytes 552968 | tf_op jit(solution)/shard_map/ppermute | solution.py:333
  129.5 4.7 %all-to-all-start.3 = ((bf16[8,96,512]{2,1,0:T(8,128)(2,1)}), bf16[8,96,512]{2,1,0:T(8,128)(2,1)S(1)}, u32[]{:S(2)}, u32[]{:S(2)}) async-start(bf16[8,96,512]{2,1,0:T(8,128)(2,1)} %get-tuple-element.55), calls=%async_computation.3 | async-start | bytes 1572864 | tf_op jit(solution)/shard_map/all_to_all | solution.py:273
  137.4 20.4 %all-to-all-done.3.inputs = bf16[8,96,512]{2,1,0:T(8,128)(2,1)S(1)} async-done(((bf16[8,96,512]{2,1,0:T(8,128)(2,1)}), bf16[8,96,512]{2,1,0:T(8,128)(2,1)S(1)}, u32[]{:S(2)}, u32[]{:S(2)}) %all-to-all-start.3) | async-done | bytes 786464 | tf_op jit(solution)/shard_map/all_to_all | solution.py:273
  159.6 10.4 %all_to_all.40.got = bf16[4,112,512]{2,1,0:T(8,128)(2,1)S(1)} all-to-all(bf16[4,112,512]{2,1,0:T(8,128)(2,1)S(1)} %shard_map.133), channel_id=1, replica_groups=mesh['y'=8,'xh'=2,'z'=8,'xl'=2,'core'=2] {'xl','core'}, dimensions={0} | all-to-all | bytes 917504 | tf_op jit(solution)/shard_map/all_to_all | solution.py:273
  170.0 15.9 %all_to_all.41.acts = bf16[8,48,512]{2,1,0:T(8,128)(2,1)S(1)} all-to-all(bf16[8,48,512]{2,1,0:T(8,128)(2,1)S(1)} %shard_map.134), channel_id=1, replica_groups=mesh['y'=8,'xh'=2,'z'=8,'xl'=2,'core'=2] {'z'}, dimensions={0} | all-to-all | bytes 786432 | tf_op jit(solution)/shard_map/all_to_all | solution.py:273
  187.7 10.4 %all_to_all.42.got = bf16[4,80,512]{2,1,0:T(8,128)(2,1)S(1)} all-to-all(bf16[4,80,512]{2,1,0:T(8,128)(2,1)S(1)} %shard_map.135), channel_id=1, replica_groups=mesh['y'=8,'xh'=2,'z'=8,'xl'=2,'core'=2] {'xl','core'}, dimensions={0} | all-to-all | bytes 655360 | tf_op jit(solution)/shard_map/all_to_all | solution.py:273
  198.2 18.4 %all_to_all.43 = bf16[16,32,128]{2,1,0:T(8,128)(2,1)S(1)} all-to-all(bf16[16,32,128]{2,1,0:T(8,128)(2,1)S(1)} %bitcast.65), channel_id=1, replica_groups=mesh['y'=8,'xh'=2,'z'=8,'xl'=2,'core'=2] {'y','xh'}, dimensions={0} | all-to-all | bytes 262144 | tf_op jit(solution)/shard_map/all_to_all | solution.py:273
  (125 shorter events, 40.6 us)
Async XLA Ops:
  2.1 39.4 %all-to-all-start = ((bf16[16,288,128]{2,1,0:T(8,128)(2,1)}), bf16[16,288,128]{2,1,0:T(8,128)(2,1)S(1)}, u32[]{:S(2)}, u32[]{:S(2)}) async-start(bf16[16,288,128]{2,1,0:T(8,128)(2,1)} %broadcast_in_dim.6), calls=%async_computation | async-start | bytes 2359296 | tf_op jit(solution)/shard_map/all_to_all | solution.py:273
  12.5 35.8 %copy-start.28 = (s32[120,3,2]{0,2,1:T(2,128)S(1)}, s32[120,3,2]{0,2,1:T(2,128)}, u32[]{:S(2)}) copy-start(s32[120,3,2]{0,2,1:T(2,128)} %param.21) | copy-start | bytes 8644
  14.7 36.0 %copy-start.18 = (bf16[3,80,384]{2,1,0:T(8,128)(2,1)}, bf16[3,80,384]{2,1,0:T(8,128)(2,1)S(1)}, u32[]{:S(2)}) copy-start(bf16[3,80,384]{2,1,0:T(8,128)(2,1)S(1)} %get-tuple-element.48) | copy-start | bytes 552964
  14.7 36.0 %copy-start.20 = (bf16[3,80,384]{2,1,0:T(8,128)(2,1)}, bf16[3,80,384]{2,1,0:T(8,128)(2,1)S(1)}, u32[]{:S(2)}) copy-start(bf16[3,80,384]{2,1,0:T(8,128)(2,1)S(1)} %get-tuple-element.47) | copy-start | bytes 552964
  14.7 67.9 %collective-permute-start.2 = (bf16[3,80,384]{2,1,0:T(8,128)(2,1)}, bf16[3,80,384]{2,1,0:T(8,128)(2,1)S(1)}, u32[]{:S(2)}, u32[]{:S(2)}) collective-permute-start(bf16[3,80,384]{2,1,0:T(8,128)(2,1)} %get-tuple-element.42), channel_id=1, source_target_pairs={{0,4},{4,8},{8,12},{12,16},{16,20},{20,24},{24,28},{28,0},{1,5},{5... | collective-permute-start | bytes 552968 | tf_op jit(solution)/shard_map/ppermute | solution.py:322
  18.7 69.3 %collective-permute-start.3 = (bf16[3,80,384]{2,1,0:T(8,128)(2,1)}, bf16[3,80,384]{2,1,0:T(8,128)(2,1)S(1)}, u32[]{:S(2)}, u32[]{:S(2)}) collective-permute-start(bf16[3,80,384]{2,1,0:T(8,128)(2,1)} %get-tuple-element.43), channel_id=1, source_target_pairs={{0,8},{4,12},{8,16},{12,20},{16,24},{20,28},{24,0},{28,4},{1,9},{5... | collective-permute-start | bytes 552968 | tf_op jit(solution)/shard_map/ppermute | solution.py:322
  24.5 75.2 %collective-permute-start.4 = (bf16[3,80,384]{2,1,0:T(8,128)(2,1)}, bf16[3,80,384]{2,1,0:T(8,128)(2,1)S(1)}, u32[]{:S(2)}, u32[]{:S(2)}) collective-permute-start(bf16[3,80,384]{2,1,0:T(8,128)(2,1)} %get-tuple-element.44), channel_id=1, source_target_pairs={{0,12},{4,16},{8,20},{12,24},{16,28},{20,0},{24,4},{28,8},{1,13},{... | collective-permute-start | bytes 552968 | tf_op jit(solution)/shard_map/ppermute | solution.py:322
  31.6 68.1 %collective-permute-start.5 = (bf16[3,80,384]{2,1,0:T(8,128)(2,1)}, bf16[3,80,384]{2,1,0:T(8,128)(2,1)S(1)}, u32[]{:S(2)}, u32[]{:S(2)}) collective-permute-start(bf16[3,80,384]{2,1,0:T(8,128)(2,1)} %get-tuple-element.45), channel_id=1, source_target_pairs={{0,16},{4,20},{8,24},{12,28},{16,0},{20,4},{24,8},{28,12},{1,17},{... | collective-permute-start | bytes 552968 | tf_op jit(solution)/shard_map/ppermute | solution.py:322
  41.6 18.4 %collective-permute-start = (bf16[16,288,128]{2,1,0:T(8,128)(2,1)S(1)}, bf16[16,288,128]{2,1,0:T(8,128)(2,1)}, u32[]{:S(2)}, u32[]{:S(2)}) collective-permute-start(bf16[16,288,128]{2,1,0:T(8,128)(2,1)S(1)} %all-to-all-done.ka), channel_id=1, source_target_pairs={{0,1},{1,0},{2,3},{3,2},{4,5},{5,4},{6,7},{7,6},{8,9},{9,8},{10,11... | collective-permute-start | bytes 3538952 | tf_op jit(solution)/shard_map/ppermute | solution.py:310
  63.2 3.7 %collective-permute-start.1 = (bf16[16,80,128]{2,1,0:T(8,128)(2,1)S(1)}, bf16[16,80,128]{2,1,0:T(8,128)(2,1)S(1)}, u32[]{:S(2)}, u32[]{:S(2)}) collective-permute-start(bf16[16,80,128]{2,1,0:T(8,128)(2,1)S(1)} %get-tuple-element.39), channel_id=1, source_target_pairs={{0,1},{1,0},{2,3},{3,2},{4,5},{5,4},{6,7},{7,6},{8,9},{9,8},{10,11... | collective-permute-start | bytes 983048 | tf_op jit(solution)/shard_map/ppermute | solution.py:394
  66.9 32.9 %collective-permute-start.6 = (bf16[3,80,384]{2,1,0:T(8,128)(2,1)}, bf16[3,80,384]{2,1,0:T(8,128)(2,1)S(1)}, u32[]{:S(2)}, u32[]{:S(2)}) collective-permute-start(bf16[3,80,384]{2,1,0:T(8,128)(2,1)} %get-tuple-element.46), channel_id=1, source_target_pairs={{0,20},{4,24},{8,28},{12,0},{16,4},{20,8},{24,12},{28,16},{1,21},{... | collective-permute-start | bytes 552968 | tf_op jit(solution)/shard_map/ppermute | solution.py:322
  78.3 20.5 %all-to-all-start.1 = ((bf16[16,80,128]{2,1,0:T(8,128)(2,1)}), bf16[16,80,128]{2,1,0:T(8,128)(2,1)S(1)}, u32[]{:S(2)}, u32[]{:S(2)}) async-start(bf16[16,80,128]{2,1,0:T(8,128)(2,1)} %add_convert_fusion), calls=%async_computation.1 | async-start | bytes 655360 | tf_op jit(solution)/shard_map/all_to_all | solution.py:273
  82.0 30.4 %copy-start = (bf16[6,768,80]{1,2,0:T(8,128)(2,1)S(1)}, bf16[6,768,80]{1,2,0:T(8,128)(2,1)}, u32[]{:S(2)}) copy-start(bf16[6,768,80]{1,2,0:T(8,128)(2,1)} %param.25) | copy-start | bytes 2211844
  82.7 21.6 %collective-permute-start.7 = (bf16[3,80,384]{2,1,0:T(8,128)(2,1)S(1)}, bf16[3,80,384]{2,1,0:T(8,128)(2,1)S(1)}, u32[]{:S(2)}, u32[]{:S(2)}) collective-permute-start(bf16[3,80,384]{2,1,0:T(8,128)(2,1)S(1)} %copy-done.21), channel_id=1, source_target_pairs={{0,24},{4,28},{8,0},{12,4},{16,8},{20,12},{24,16},{28,20},{1,25},{... | collective-permute-start | bytes 552968 | tf_op jit(solution)/shard_map/ppermute | solution.py:322
  88.1 20.3 %collective-permute-start.8 = (bf16[3,80,384]{2,1,0:T(8,128)(2,1)S(1)}, bf16[3,80,384]{2,1,0:T(8,128)(2,1)S(1)}, u32[]{:S(2)}, u32[]{:S(2)}) collective-permute-start(bf16[3,80,384]{2,1,0:T(8,128)(2,1)S(1)} %copy-done.19), channel_id=1, source_target_pairs={{0,28},{4,0},{8,4},{12,8},{16,12},{20,16},{24,20},{28,24},{1,29},{... | collective-permute-start | bytes 552968 | tf_op jit(solution)/shard_map/ppermute | solution.py:322
  99.7 29.1 %copy-start.3 = (bf16[3,80,384]{2,1,0:T(8,128)(2,1)}, bf16[3,80,384]{2,1,0:T(8,128)(2,1)S(1)}, u32[]{:S(2)}) copy-start(bf16[3,80,384]{2,1,0:T(8,128)(2,1)S(1)} %collective-permute-done.6.refs_5_) | copy-start | bytes 552964
  108.4 15.7 %all-to-all-start.2 = ((bf16[16,32,128]{2,1,0:T(8,128)(2,1)}), bf16[16,32,128]{2,1,0:T(8,128)(2,1)S(1)}, u32[]{:S(2)}, u32[]{:S(2)}) async-start(bf16[16,32,128]{2,1,0:T(8,128)(2,1)} %bitcast.30), calls=%async_computation.2 | async-start | bytes 262144 | tf_op jit(solution)/shard_map/all_to_all | solution.py:273
  115.4 9.6 %collective-permute-start.10 = (bf16[80,1152]{1,0:T(8,128)(2,1)}, bf16[80,1152]{1,0:T(8,128)(2,1)S(1)}, u32[]{:S(2)}, u32[]{:S(2)}) collective-permute-start(bf16[80,1152]{1,0:T(8,128)(2,1)} %get-tuple-element.53), channel_id=1, source_target_pairs={{0,2},{1,3},{2,0},{3,1},{4,6},{5,7},{6,4},{7,5},{8,10},{9,11},{10,... | collective-permute-start | bytes 552968 | tf_op jit(solution)/shard_map/ppermute | solution.py:333
  117.7 10.5 %collective-permute-start.11 = (bf16[80,1152]{1,0:T(8,128)(2,1)}, bf16[80,1152]{1,0:T(8,128)(2,1)S(1)}, u32[]{:S(2)}, u32[]{:S(2)}) collective-permute-start(bf16[80,1152]{1,0:T(8,128)(2,1)} %get-tuple-element.54), channel_id=1, source_target_pairs={{0,3},{1,2},{2,1},{3,0},{4,7},{5,6},{6,5},{7,4},{8,11},{9,10},{10,... | collective-permute-start | bytes 552968 | tf_op jit(solution)/shard_map/ppermute | solution.py:333
  122.1 6.7 %collective-permute-start.9 = (bf16[80,1152]{1,0:T(8,128)(2,1)}, bf16[80,1152]{1,0:T(8,128)(2,1)S(1)}, u32[]{:S(2)}, u32[]{:S(2)}) collective-permute-start(bf16[80,1152]{1,0:T(8,128)(2,1)} %get-tuple-element.52), channel_id=1, source_target_pairs={{0,1},{1,0},{2,3},{3,2},{4,5},{5,4},{6,7},{7,6},{8,9},{9,8},{10,11... | collective-permute-start | bytes 552968 | tf_op jit(solution)/shard_map/ppermute | solution.py:333
  129.5 28.3 %all-to-all-start.3 = ((bf16[8,96,512]{2,1,0:T(8,128)(2,1)}), bf16[8,96,512]{2,1,0:T(8,128)(2,1)S(1)}, u32[]{:S(2)}, u32[]{:S(2)}) async-start(bf16[8,96,512]{2,1,0:T(8,128)(2,1)} %get-tuple-element.55), calls=%async_computation.3 | async-start | bytes 1572864 | tf_op jit(solution)/shard_map/all_to_all | solution.py:273
  159.5 26.5 %copy-start.10 = (bf16[80,1152]{1,0:T(8,128)(2,1)S(1)}, bf16[80,1152]{1,0:T(8,128)(2,1)}, u32[]{:S(2)}) copy-start(bf16[80,1152]{1,0:T(8,128)(2,1)} %copy-done.9) | copy-start | bytes 552964
  159.5 26.5 %copy-start.12 = (bf16[80,1152]{1,0:T(8,128)(2,1)S(1)}, bf16[80,1152]{1,0:T(8,128)(2,1)}, u32[]{:S(2)}) copy-start(bf16[80,1152]{1,0:T(8,128)(2,1)} %copy-done.11) | copy-start | bytes 552964
  159.5 26.5 %copy-start.14 = (bf16[80,1152]{1,0:T(8,128)(2,1)S(1)}, bf16[80,1152]{1,0:T(8,128)(2,1)}, u32[]{:S(2)}) copy-start(bf16[80,1152]{1,0:T(8,128)(2,1)} %copy-done.13) | copy-start | bytes 552964
  (26 other events, 297.5 us)

commit v3 on v1

--- a/solution.py
+++ b/solution.py
@@ -12,9 +12,10 @@
 EPSILON = 1e-06
 MASKED_SCORE = -1e30
 CTX = ("y", "xh")
-EXP = ("z", "xl", "core")
-ZX = ("z", "xl")
-XC = ("xl", "core")
+EXP = ("za", "zb", "xl", "core")
+ZX = ("za", "zb", "xl")
+NEAR = ("zb", "xl", "core")
+FAR = "za"
 TOK = 128
 SLOT = 32
 F32 = jnp.float32
@@ -116,7 +117,7 @@
     return jnp.where(row == 0, high, jnp.where(row == 1, low, 0.0))
 
 
-def make_rows(parts, residual, gain, places, hidden, sent):
+def make_rows(parts, residual, gain, places, shares, hidden, sent):
     mixed = jnp.sum(parts[...].astype(F32), axis=0)
     held = (residual[...].astype(F32) + mixed).astype(BF16)
     hidden[...] = held
@@ -124,18 +125,60 @@
     square = jnp.sum(wide * wide, axis=0, keepdims=True)
     run = wide.shape[0]
     rows = jnp.concatenate([wide * gain[...], tail_rows(square, TOK - run)], axis=0).astype(BF16)
-    sent[...] = dot_nt(places[...], rows).astype(BF16)
-
-
-def spread_rows(keep_rows, got, out):
-    turned = got[...].T[:keep_rows]
+    sent[...] = (dot_nt(places[...], rows) + shares[...].astype(F32)).astype(BF16)
+
+
+def spread_rows(keep_rows, first, got, out, keep, weight):
+    turned = got[...].T
+    kept = turned[:keep_rows]
     for i in range(out.shape[0]):
-        out[i] = turned
-
-
-def project_up(run, sub, inputs, weights, keep, out):
+        out[i] = kept
+    count = keep.shape[0] // 2
+    weights = turned[first : first + 16].astype(F32)
+    seen = jnp.zeros((1, weights.shape[1]), F32)
+    picked = [jnp.zeros((1, weights.shape[1]), F32) for _ in range(2)]
+    for expert in range(count):
+        row = weights[expert : expert + 1]
+        chosen = jnp.where(row > 0.0, 1.0, 0.0)
+        for pick in range(2):
+            flag = jnp.where(seen == pick, chosen, 0.0)
+            keep[2 * expert + pick : 2 * expert + pick + 1, :] = flag
+            picked[pick] = picked[pick] + flag * row
+        seen = seen + chosen
+    weight[...] = jnp.concatenate(picked, axis=0)
+
+
+def pack(place, gate, up, down, *refs):
+    outs, held = refs[:-1], refs[-1]
+    count = held.shape[0]
+    part = gate.shape[2] // count
+    for pair in range(held.shape[1]):
+        for near in range(count):
+            span = slice(near * part, (near + 1) * part)
+            pieces = []
+            for expert in (2 * pair, 2 * pair + 1):
+                pieces += [gate[expert, :, span], up[expert, :, span]]
+            pieces += [down[2 * pair, :, span], down[2 * pair + 1, :, span]]
+            held[near, pair] = jnp.concatenate(pieces, axis=1)
+    for flip in range(count):
+        outs[flip][...] = held[place[2] ^ flip]
+
+
+def unpack(part, *refs):
+    got, into, back = refs[:-2], refs[-2], refs[-1]
+    pairs = got[0].shape[0]
+    for pair in range(pairs):
+        wide = jnp.concatenate([g[pair, :, : 4 * part] for g in got], axis=0)
+        into[pair * 4 * part : (pair + 1) * 4 * part, :] = wide.T
+    for flip, g in enumerate(got):
+        back[flip] = jnp.concatenate([g[pair, :, 4 * part :] for pair in range(pairs)], axis=1)
+
+
+def project_up(run, sub, place, inputs, weights, keep, out):
     count, _, slots = inputs.shape
-    features = inputs[:, :run, :].reshape(count * run, slots)
+    features = jnp.concatenate(
+        [inputs[place[2] ^ flip, :run, :] for flip in range(count)], axis=0
+    )
     ends = inputs[:, run : run + 16, :].astype(F32)
     ends = jnp.sum(ends, axis=0)
     square = ends[0:1] + ends[1:2]
@@ -170,7 +213,7 @@
         out[i] = rounded
 
 
-def project_down(sub, acts, weights, keep, out):
+def project_down(sub, place, acts, keep, weights, out):
     count, _, slots = acts.shape
     wide = acts[...].astype(F32)
     first = wide[:, :sub].reshape(count * sub, slots)
@@ -184,8 +227,8 @@
             ).astype(BF16)
         )
     stacked = jnp.concatenate(picked, axis=0)
-    for dest in range(out.shape[0]):
-        out[dest] = dot(weights[dest], stacked).astype(BF16)
+    for flip in range(weights.shape[0]):
+        out[place[2] ^ flip] = dot(weights[flip], stacked).astype(BF16)
 
 
 def finish_rows(got, out):
@@ -222,8 +265,8 @@
     w_down,
 ):
     ctx_count = lax.axis_size(CTX)
-    z_count = lax.axis_size("z")
-    xc_count = lax.axis_size(XC)
+    near_count = lax.axis_size(NEAR)
+    far_count = lax.axis_size(FAR)
     my_block = lax.axis_index(CTX)
     core = lax.axis_index("core")
     block_rows, key_width = latents.shape
@@ -234,22 +277,27 @@
     half = key_width // 2
     pad_rows = TOK - block_rows
     slots = ctx_count * SLOT
-    part = hidden_units // z_count
-    sub = part // xc_count
+    part = hidden_units // near_count
+    sub = part // far_count
 
     keys = jnp.pad(latents.T, ((0, 0), (0, pad_rows)))
     own_half = lax.dynamic_slice_in_dim(keys, core * half, half, 0)
     keys_a = exchange(jnp.broadcast_to(own_half[None], (ctx_count, half, TOK)), CTX)
-    keys_b = lax.ppermute(keys_a, "core", [(0, 1), (1, 0)])
-
+
+    place = jnp.stack([my_block, core, lax.axis_index(NEAR)]).astype(jnp.int32)
     pairs = local_experts // 2
-    both = jnp.stack([w_gate, w_up], axis=1).reshape(pairs, 2, 2, run, z_count, part)
-    both = both.transpose(4, 0, 3, 1, 2, 5).reshape(z_count, pairs, run, 4 * part)
-    both = exchange(both, "z")
-    weights_in = both.transpose(1, 3, 0, 2).reshape(pairs * 4 * part, z_count * run)
-    down = w_down.transpose(0, 2, 1).reshape(local_experts, run, z_count, xc_count, sub)
-    down = down.transpose(3, 1, 0, 2, 4).reshape(xc_count, run, local_experts * z_count * sub)
-    down = exchange(down, XC)
+    block = (pairs, run, 6 * part)
+    packed = call(
+        pack,
+        [shape(block)] * near_count,
+        [SMEM] + [VMEM] * 3,
+        [pltpu.VMEM((near_count,) + block, BF16)],
+    )(place, w_gate, w_up, w_down.transpose(0, 2, 1))
+
+    def flipped(x, flip):
+        return lax.ppermute(x, NEAR, [(a, a ^ flip) for a in range(near_count)])
+
+    moved = [packed[0]] + [flipped(packed[i], i) for i in range(1, near_count)]
 
     group_range = jnp.arange(ctx_count)
     expert_range = jnp.arange(local_experts)
@@ -269,18 +317,14 @@
     placement = (
         (member[:, :, None] == 1) & (ranking[:, :, None] == jnp.arange(SLOT)[None, None, :])
     ).astype(BF16)
-    sent_weights = jnp.einsum(
-        "tge,tgc->gec", shares.astype(BF16), placement, preferred_element_type=F32
+    first_share = run + 16
+    slot_shares = jnp.einsum(
+        "tge,tgc->gce", shares.astype(BF16), placement, preferred_element_type=F32
     ).astype(BF16)
-    got_weights = exchange(sent_weights, CTX)
-    weights = got_weights.transpose(1, 0, 2).reshape(local_experts, slots).astype(F32)
-    chosen = (weights > 0.0).astype(jnp.int32)
-    ordinal = jnp.cumsum(chosen, axis=0) - 1
-    keep = jnp.stack(
-        [((chosen == 1) & (ordinal == pick)).astype(F32) for pick in range(2)], axis=1
-    )
-    pick_weight = jnp.sum(keep * weights[:, None, :], axis=0)
-    keep = keep.reshape(2 * local_experts, slots)
+    slot_shares = jnp.pad(
+        slot_shares.reshape(slots, local_experts),
+        ((0, 0), (first_share, TOK - first_share - local_experts)),
+    )
     places = jnp.pad(placement.reshape(block_rows, slots).T, ((0, 0), (0, pad_rows)))
 
     wide_q = jnp.pad(queries.transpose(1, 0, 2), ((0, 0), (0, pad_rows), (0, 0)))
@@ -289,9 +333,22 @@
     v_low = value_up[:, :half]
     v_high = jnp.pad(value_up[:, half:], ((0, 0), (0, key_width - latent_width), (0, 0)))
     flip = core == 1
-    place = jnp.stack([my_block, core]).astype(jnp.int32)
     runs = D // run
     out_weights = out_proj.T.reshape(runs // 2, 2, run, heads * value_width)
+    operands = (
+        jnp.where(flip, q_high, q_low),
+        jnp.where(flip, q_low, q_high),
+        jnp.where(flip, v_high, v_low),
+        jnp.where(flip, v_low, v_high),
+        out_weights,
+    )
+    resid = jnp.pad(residual.T, ((0, 0), (0, pad_rows)))
+    gain = norm_gain.astype(F32)[:, None]
+    keys_a, operands, moved, places, slot_shares, resid, gain = lax.optimization_barrier(
+        (keys_a, operands, moved, places, slot_shares, resid, gain)
+    )
+    keys_b = lax.ppermute(keys_a, "core", [(0, 1), (1, 0)])
+    q_a, q_b, v_a, v_b, out_weights = operands
     mine, theirs = call(
         functools.partial(attend, block_rows, key_width),
         [shape((runs // 2, run, TOK), F32), shape((runs // 2, run, TOK))],
@@ -302,51 +359,58 @@
             pltpu.VMEM((2 * TOK, half), F32),
             pltpu.VMEM((2 * TOK, half), F32),
         ],
-    )(
-        place,
-        block_mask,
-        jnp.where(flip, q_high, q_low),
-        jnp.where(flip, q_low, q_high),
-        keys_a,
-        keys_b,
-        jnp.where(flip, v_high, v_low),
-        jnp.where(flip, v_low, v_high),
-        out_weights,
-    )
+    )(place, block_mask, q_a, q_b, keys_a, keys_b, v_a, v_b, out_weights)
     summed = (mine + lax.ppermute(theirs, "core", [(0, 1), (1, 0)]).astype(F32)).astype(BF16)
     parts = exchange(summed, ZX)
 
-    hidden, sent = call(make_rows, [shape((run, TOK)), shape((slots, TOK))], [VMEM] * 4)(
+    hidden, sent = call(make_rows, [shape((run, TOK)), shape((slots, TOK))], [VMEM] * 5)(
         parts,
-        jnp.pad(residual.T, ((0, 0), (0, pad_rows))),
-        norm_gain.astype(F32)[:, None],
+        resid,
+        gain,
         places,
-    )
+        slot_shares,
+    )
+    weights_in, weights_back = call(
+        functools.partial(unpack, part),
+        [
+            shape((pairs * 4 * part, near_count * run)),
+            shape((near_count, run, local_experts * part)),
+        ],
+        [VMEM] * near_count,
+    )(*moved)
     got = exchange(sent.reshape(ctx_count, SLOT, TOK), CTX).reshape(slots, TOK)
-    spread = call(
-        functools.partial(spread_rows, run + 16), shape((z_count, run + 16, slots)), [VMEM]
+    spread, keep, pick_weight = call(
+        functools.partial(spread_rows, run + 16, first_share),
+        [
+            shape((near_count, run + 16, slots)),
+            shape((2 * local_experts, slots), F32),
+            shape((2, slots), F32),
+        ],
+        [VMEM],
     )(got)
-    inputs = exchange(spread, "z")
+    inputs = exchange(spread, NEAR)
     partial_sums = call(
         functools.partial(project_up, run, sub),
-        shape((xc_count, 4 * sub + 16, slots)),
-        [VMEM] * 3,
-    )(inputs, weights_in, keep)
-    acts = call(functools.partial(activate, sub), shape((z_count, 2 * sub, slots)), [VMEM] * 2)(
-        exchange(partial_sums, XC), pick_weight
+        shape((far_count, 4 * sub + 16, slots)),
+        [SMEM] + [VMEM] * 3,
+    )(place, inputs, weights_in, keep)
+    acts = call(functools.partial(activate, sub), shape((far_count, 2 * sub, slots)), [VMEM] * 2)(
+        exchange(partial_sums, FAR), pick_weight
     )
     outputs = call(
-        functools.partial(project_down, sub), shape((xc_count, run, slots)), [VMEM] * 3
-    )(exchange(acts, "z"), down, keep)
-    returned = call(finish_rows, shape((slots, TOK)), [VMEM])(exchange(outputs, XC))
+        functools.partial(project_down, sub),
+        shape((near_count, run, slots)),
+        [SMEM] + [VMEM] * 3,
+    )(place, exchange(acts, FAR), keep, weights_back)
+    returned = call(finish_rows, shape((slots, TOK)), [VMEM])(exchange(outputs, NEAR))
     returned = exchange(returned.reshape(ctx_count, SLOT, TOK), CTX).reshape(slots, TOK)
     out = call(combine, shape((run, block_rows)), [VMEM] * 3)(returned, places, hidden)
     return out.T
 
 
 def solution(mesh):
-    names = ("y", "xh", "z", "xl", "core")
-    fine = Mesh(mesh.devices.reshape(8, 2, 8, 2, 2), names)
+    names = ("y", "xh", "za", "zb", "xl", "core")
+    fine = Mesh(mesh.devices.reshape(8, 2, 4, 2, 2, 2), names)
     return jax.shard_map(
         on_device,
         mesh=fine,

time: 267 us -> 197 us (0.74)
  waiting for transfers between devices: 98.1 us -> 37.4 us
  blocking collectives: 47.6 us -> 77.2 us
  local copies, waits for them, and re-layouts: 34.8 us -> 11.1 us
  other arithmetic: 12.4 us -> 1.67 us
  starting transfers between devices: 62.2 us -> 54.7 us
  Pallas kernels: 9.14 us -> 12.9 us
    all_to_all x8 -> x3, waiting for transfers between devices: 98.1 us -> 18.3 us  [exchange(): return lax.all_to_all(x, axes, split_axis=0, concat_axis=0, tiled=True)]
    all_to_all x3 -> x5, blocking collectives: 47.6 us -> 77.2 us  [exchange(): return lax.all_to_all(x, axes, split_axis=0, concat_axis=0, tiled=True)]
    all_to_all x8 -> x3, starting transfers between devices: 53.5 us -> 27.3 us  [exchange(): return lax.all_to_all(x, axes, split_axis=0, concat_axis=0, tiled=True)]
    ppermute x0 -> x7, starting transfers between devices: none -> 22.9 us  [flipped(): return lax.ppermute(x, NEAR, [(a, a ^ flip) for a in range(near_count)])]
    ppermute x0 -> x7, waiting for transfers between devices: none -> 15.4 us  [flipped(): return lax.ppermute(x, NEAR, [(a, a ^ flip) for a in range(near_count)])]
    reshape x6 -> x0, local copies, waits for them, and re-layouts: 12.6 us -> none  [the longest x2 7.75 us: on_device(): both.transpose(1, 3, 0, 2).reshape(pairs * 4 * part, z_count * run)]
    another operation x4 -> x0, local copies, waits for them, and re-layouts: 8.52 us -> none  [on_device(): jnp.stack([w_gate, w_up], axis=1).reshape(pairs, 2, 2, run, z_count, part)]
    transpose x1 -> x0, other arithmetic: 7.28 us -> none  [on_device(): both.transpose(4, 0, 3, 1, 2, 5).reshape(z_count, pairs, run, 4 * part)]
  transfers between devices with their start and end apart: 10 -> 12, of which waited for: 7 -> 5; matrix products, arithmetic and copies ran while one was open for 17% -> 3% of each run, Pallas kernels for 1% -> 2%
where the time goes in v3:
time: 197 us; the launch traced here: 196 us
  blocking collectives  77.2 us (39%)
  starting transfers between devices  54.7 us (28%)
  waiting for transfers between devices  37.4 us (19%)
  Pallas kernels  12.9 us (7%)
  local copies, waits for them, and re-layouts  11.1 us (6%)
    all_to_all x5, blocking collectives, exchange(): return lax.all_to_all(x, axes, split_axis=0, concat_axis=0, tiled=True)  77.2 us
    all_to_all x3, starting transfers between devices, exchange(): return lax.all_to_all(x, axes, split_axis=0, concat_axis=0, tiled=True)  27.3 us
    ppermute x7, starting transfers between devices, flipped(): return lax.ppermute(x, NEAR, [(a, a ^ flip) for a in range(near_count)])  22.9 us
    all_to_all x3, waiting for transfers between devices, exchange(): return lax.all_to_all(x, axes, split_axis=0, concat_axis=0, tiled=True)  18.3 us
    ppermute x7, waiting for transfers between devices, flipped(): return lax.ppermute(x, NEAR, [(a, a ^ flip) for a in range(near_count)])  15.4 us
    unnamed x35, local copies, waits for them, and re-layouts  5.01 us
  transfers between devices with their start and end apart: 12, of which 5 were waited for; matrix products, arithmetic and copies ran while one was open for 3% of the time, Pallas kernels for 2%

profile of v3, /device:TPU:1, one launch (start us, length us, event | category | flops | bytes accessed | tf_op | source)
XLA Modules:
  0.0 195.8 jit_solution(12105316813364097471)
XLA Ops:
  2.1 10.3 %all-to-all-start = ((bf16[16,288,128]{2,1,0:T(8,128)(2,1)}), bf16[16,288,128]{2,1,0:T(8,128)(2,1)S(1)}, u32[]{:S(2)}, u32[]{:S(2)}) async-start(bf16[16,288,128]{2,1,0:T(8,128)(2,1)} %broadcast_in_dim.7), calls=%async_computation | async-start | bytes 2359296 | tf_op jit(solution)/shard_map/all_to_all | solution.py:249
  13.7 2.9 %shard_map.127 = (bf16[3,80,576]{2,1,0:T(8,128)(2,1)S(1)}, bf16[3,80,576]{2,1,0:T(8,128)(2,1)}, bf16[3,80,576]{2,1,0:T(8,128)(2,1)}, bf16[3,80,576]{2,1,0:T(8,12...) custom-call(s32[3]{0:T(128)S(1)} %pad_add_fusion.place, ...), custom_call_target="tpu_custom_call" | custom-call | tf_op jit(solution)/shard_map/pallas_call | solution.py:290
  16.6 3.0 %collective-permute-start = (bf16[3,80,576]{2,1,0:T(8,128)(2,1)}, bf16[3,80,576]{2,1,0:T(8,128)(2,1)S(1)}, u32[]{:S(2)}, u32[]{:S(2)}) collective-permute-start(bf16[3,80,576]{2,1,0:T(8,128)(2,1)} %get-tuple-element.41), channel_id=1, source_target_pairs={{0,1},{1,0},{2,3},{3,2},{4,5},{5,4},{6,7},{7,6},{8,9},{9,8},{10,11... | collective-permute-start | bytes 829448 | tf_op jit(solution)/shard_map/ppermute | solution.py:298
  19.6 2.2 %collective-permute-start.1 = (bf16[3,80,576]{2,1,0:T(8,128)(2,1)}, bf16[3,80,576]{2,1,0:T(8,128)(2,1)S(1)}, u32[]{:S(2)}, u32[]{:S(2)}) collective-permute-start(bf16[3,80,576]{2,1,0:T(8,128)(2,1)} %get-tuple-element.42), channel_id=1, source_target_pairs={{0,2},{1,3},{2,0},{3,1},{4,6},{5,7},{6,4},{7,5},{8,10},{9,11},{10,... | collective-permute-start | bytes 829448 | tf_op jit(solution)/shard_map/ppermute | solution.py:298
  21.8 3.2 %collective-permute-start.2 = (bf16[3,80,576]{2,1,0:T(8,128)(2,1)}, bf16[3,80,576]{2,1,0:T(8,128)(2,1)}, u32[]{:S(2)}, u32[]{:S(2)}) collective-permute-start(bf16[3,80,576]{2,1,0:T(8,128)(2,1)} %get-tuple-element.43), channel_id=1, source_target_pairs={{0,3},{1,2},{2,1},{3,0},{4,7},{5,6},{6,5},{7,4},{8,11},{9,10},{10,... | collective-permute-start | bytes 829448 | tf_op jit(solution)/shard_map/ppermute | solution.py:298
  25.1 4.0 %collective-permute-start.3 = (bf16[3,80,576]{2,1,0:T(8,128)(2,1)}, bf16[3,80,576]{2,1,0:T(8,128)(2,1)}, u32[]{:S(2)}, u32[]{:S(2)}) collective-permute-start(bf16[3,80,576]{2,1,0:T(8,128)(2,1)} %get-tuple-element.44), channel_id=1, source_target_pairs={{0,4},{1,5},{2,6},{3,7},{4,0},{5,1},{6,2},{7,3},{8,12},{9,13},{10,... | collective-permute-start | bytes 829448 | tf_op jit(solution)/shard_map/ppermute | solution.py:298
  29.1 2.0 %collective-permute-start.4 = (bf16[3,80,576]{2,1,0:T(8,128)(2,1)}, bf16[3,80,576]{2,1,0:T(8,128)(2,1)}, u32[]{:S(2)}, u32[]{:S(2)}) collective-permute-start(bf16[3,80,576]{2,1,0:T(8,128)(2,1)} %get-tuple-element.45), channel_id=1, source_target_pairs={{0,5},{1,4},{2,7},{3,6},{4,1},{5,0},{6,3},{7,2},{8,13},{9,12},{10,... | collective-permute-start | bytes 829448 | tf_op jit(solution)/shard_map/ppermute | solution.py:298
  33.3 3.7 %collective-permute-start.5 = (bf16[3,80,576]{2,1,0:T(8,128)(2,1)}, bf16[3,80,576]{2,1,0:T(8,128)(2,1)}, u32[]{:S(2)}, u32[]{:S(2)}) collective-permute-start(bf16[3,80,576]{2,1,0:T(8,128)(2,1)} %get-tuple-element.46), channel_id=1, source_target_pairs={{0,6},{1,7},{2,4},{3,5},{4,2},{5,3},{6,0},{7,1},{8,14},{9,15},{10,... | collective-permute-start | bytes 829448 | tf_op jit(solution)/shard_map/ppermute | solution.py:298
  37.0 4.7 %collective-permute-start.6 = (bf16[3,80,576]{2,1,0:T(8,128)(2,1)}, bf16[3,80,576]{2,1,0:T(8,128)(2,1)}, u32[]{:S(2)}, u32[]{:S(2)}) collective-permute-start(bf16[3,80,576]{2,1,0:T(8,128)(2,1)} %get-tuple-element.47), channel_id=1, source_target_pairs={{0,7},{1,6},{2,5},{3,4},{4,3},{5,2},{6,1},{7,0},{8,15},{9,14},{10,... | collective-permute-start | bytes 829448 | tf_op jit(solution)/shard_map/ppermute | solution.py:298
  45.7 15.4 %collective-permute-done.2.refs_3_ = bf16[3,80,576]{2,1,0:T(8,128)(2,1)} collective-permute-done((bf16[3,80,576]{2,1,0:T(8,128)(2,1)}, bf16[3,80,576]{2,1,0:T(8,128)(2,1)}, u32[]{:S(2)}, u32[]{:S(2)}) %collective-permute-start.2) | collective-permute-done | bytes 276512 | tf_op jit(solution)/shard_map/ppermute | solution.py:298
  61.1 2.3 %collective-permute-start.7 = (bf16[16,288,128]{2,1,0:T(8,128)(2,1)S(1)}, bf16[16,288,128]{2,1,0:T(8,128)(2,1)S(1)}, u32[]{:S(2)}, u32[]{:S(2)}) collective-permute-start(bf16[16,288,128]{2,1,0:T(8,128)(2,1)S(1)} %all-to-all-done.ka), channel_id=1, source_target_pairs={{0,1},{1,0},{2,3},{3,2},{4,5},{5,4},{6,7},{7,6},{8,9},{9,8},{10,11... | collective-permute-start | bytes 3538952 | tf_op jit(solution)/shard_map/ppermute | solution.py:350
  63.4 2.5 %collective-permute-done.7.kb = bf16[16,288,128]{2,1,0:T(8,128)(2,1)S(1)} collective-permute-done((bf16[16,288,128]{2,1,0:T(8,128)(2,1)S(1)}, bf16[16,288,128]{2,1,0:T(8,128)(2,1)S(1)}, u32[]{:S(2)}, u32[]{:S(2)}) %collective-permute-start.7) | collective-permute-done | bytes 1179680 | tf_op jit(solution)/shard_map/ppermute | solution.py:350
  65.8 2.5 %shard_map.128 = (f32[16,80,128]{2,1,0:T(8,128)S(1)}, bf16[16,80,128]{2,1,0:T(8,128)(2,1)S(1)}) custom-call(s32[3]{0:T(128)S(1)} %pad_add_fusion.place, s32[16,16]{1,0:T(8,128)S(1)} %copy-done.9, bf16[256,288]{1,0:T(8,128)(2,1)S(1)} %get-tuple-element.48.qa, bf16[256,288]{1,0:T(8,128)(2,1)S(1)} %get-tuple-element.49.qb, ...), custom_call_target="tpu_custom_call" | custom-call | tf_op jit(solution)/shard_map/pallas_call | solution.py:352
  68.3 2.3 %collective-permute-start.8 = (bf16[16,80,128]{2,1,0:T(8,128)(2,1)S(1)}, bf16[16,80,128]{2,1,0:T(8,128)(2,1)S(1)}, u32[]{:S(2)}, u32[]{:S(2)}) collective-permute-start(bf16[16,80,128]{2,1,0:T(8,128)(2,1)S(1)} %get-tuple-element.55), channel_id=1, source_target_pairs={{0,1},{1,0},{2,3},{3,2},{4,5},{5,4},{6,7},{7,6},{8,9},{9,8},{10,11... | collective-permute-start | bytes 983048 | tf_op jit(solution)/shard_map/ppermute | solution.py:363
  72.7 10.3 %all-to-all-start.1 = ((bf16[16,80,128]{2,1,0:T(8,128)(2,1)}), bf16[16,80,128]{2,1,0:T(8,128)(2,1)S(1)}, u32[]{:S(2)}, u32[]{:S(2)}) async-start(bf16[16,80,128]{2,1,0:T(8,128)(2,1)} %add_convert_fusion), calls=%async_computation.1 | async-start | bytes 655360 | tf_op jit(solution)/shard_map/all_to_all | solution.py:249
  83.0 12.3 %all-to-all-done.1.parts = bf16[16,80,128]{2,1,0:T(8,128)(2,1)S(1)} async-done(((bf16[16,80,128]{2,1,0:T(8,128)(2,1)}), bf16[16,80,128]{2,1,0:T(8,128)(2,1)S(1)}, u32[]{:S(2)}, u32[]{:S(2)}) %all-to-all-start.1) | async-done | bytes 327712 | tf_op jit(solution)/shard_map/all_to_all | solution.py:249
  95.6 21.2 %all_to_all.40 = bf16[16,32,128]{2,1,0:T(8,128)(2,1)S(1)} all-to-all(bf16[16,32,128]{2,1,0:T(8,128)(2,1)S(1)} %bitcast.67), channel_id=1, replica_groups=mesh['y'=8,'xh'=2,'za'=4,'zb'=2,'xl'=2,'core'=2] {'y','xh'}, dimensions={0} | all-to-all | bytes 262144 | tf_op jit(solution)/shard_map/all_to_all | solution.py:249
  117.8 6.7 %all-to-all-start.3 = ((bf16[8,96,512]{2,1,0:T(8,128)(2,1)}), bf16[8,96,512]{2,1,0:T(8,128)(2,1)S(1)}, u32[]{:S(2)}, u32[]{:S(2)}) async-start(bf16[8,96,512]{2,1,0:T(8,128)(2,1)} %get-tuple-element.61), calls=%async_computation.3 | async-start | bytes 1572864 | tf_op jit(solution)/shard_map/all_to_all | solution.py:249
  127.3 1.9 shard_map.131
  129.2 6.0 %all-to-all-done.3.inputs = bf16[8,96,512]{2,1,0:T(8,128)(2,1)S(1)} async-done(((bf16[8,96,512]{2,1,0:T(8,128)(2,1)}), bf16[8,96,512]{2,1,0:T(8,128)(2,1)S(1)}, u32[]{:S(2)}, u32[]{:S(2)}) %all-to-all-start.3) | async-done | bytes 786464 | tf_op jit(solution)/shard_map/all_to_all | solution.py:249
  137.0 16.1 %all_to_all.41.got = bf16[4,112,512]{2,1,0:T(8,128)(2,1)S(1)} all-to-all(bf16[4,112,512]{2,1,0:T(8,128)(2,1)S(1)} %shard_map.132), channel_id=1, replica_groups=mesh['y'=8,'xh'=2,'za'=4,'zb'=2,'xl'=2,'core'=2] {'za'}, dimensions={0} | all-to-all | bytes 917504 | tf_op jit(solution)/shard_map/all_to_all | solution.py:249
  153.2 11.8 %all_to_all.42.acts = bf16[4,48,512]{2,1,0:T(8,128)(2,1)S(1)} all-to-all(bf16[4,48,512]{2,1,0:T(8,128)(2,1)S(1)} %shard_map.133), channel_id=1, replica_groups=mesh['y'=8,'xh'=2,'za'=4,'zb'=2,'xl'=2,'core'=2] {'za'}, dimensions={0} | all-to-all | bytes 393216 | tf_op jit(solution)/shard_map/all_to_all | solution.py:249
  166.7 15.4 %all_to_all.43.got = bf16[8,80,512]{2,1,0:T(8,128)(2,1)S(1)} all-to-all(bf16[8,80,512]{2,1,0:T(8,128)(2,1)S(1)} %shard_map.134), channel_id=1, replica_groups=mesh['y'=8,'xh'=2,'za'=4,'zb'=2,'xl'=2,'core'=2] {'zb','xl','core'}, dimensions={0} | all-to-all | bytes 1310720 | tf_op jit(solution)/shard_map/all_to_all | solution.py:249
  182.3 12.6 %all_to_all.44 = bf16[16,32,128]{2,1,0:T(8,128)(2,1)S(1)} all-to-all(bf16[16,32,128]{2,1,0:T(8,128)(2,1)S(1)} %bitcast.66), channel_id=1, replica_groups=mesh['y'=8,'xh'=2,'za'=4,'zb'=2,'xl'=2,'core'=2] {'y','xh'}, dimensions={0} | all-to-all | bytes 262144 | tf_op jit(solution)/shard_map/all_to_all | solution.py:249
  (85 shorter events, 20.0 us)
Async XLA Ops:
  2.1 10.5 %copy-start = (bf16[6,80,768]{2,1,0:T(8,128)(2,1)S(1)}, bf16[6,80,768]{2,1,0:T(8,128)(2,1)}, u32[]{:S(2)}) copy-start(bf16[6,80,768]{2,1,0:T(8,128)(2,1)} %gate.1) | copy-start | bytes 2211844
  2.1 10.5 %copy-start.1 = (bf16[6,80,768]{2,1,0:T(8,128)(2,1)S(1)}, bf16[6,80,768]{2,1,0:T(8,128)(2,1)}, u32[]{:S(2)}) copy-start(bf16[6,80,768]{2,1,0:T(8,128)(2,1)} %up.1) | copy-start | bytes 2211844
  2.1 59.0 %all-to-all-start = ((bf16[16,288,128]{2,1,0:T(8,128)(2,1)}), bf16[16,288,128]{2,1,0:T(8,128)(2,1)S(1)}, u32[]{:S(2)}, u32[]{:S(2)}) async-start(bf16[16,288,128]{2,1,0:T(8,128)(2,1)} %broadcast_in_dim.7), calls=%async_computation | async-start | bytes 2359296 | tf_op jit(solution)/shard_map/all_to_all | solution.py:249
  12.5 18.6 %copy-start.15 = (s32[120,3]{0,1:T(4,128)S(1)}, s32[120,3]{0,1:T(4,128)}, u32[]{:S(2)}) copy-start(s32[120,3]{0,1:T(4,128)} %param.20) | copy-start | bytes 4324
  13.7 18.2 %copy-start.13 = (bf16[120,3,2]{0,2,1:T(2,128)(2,1)S(1)}, bf16[120,3,2]{0,2,1:T(2,128)(2,1)}, u32[]{:S(2)}) copy-start(bf16[120,3,2]{0,2,1:T(2,128)(2,1)} %param.22) | copy-start | bytes 4324
  13.7 18.2 %copy-start.14 = (s32[120,3,2]{0,2,1:T(2,128)S(1)}, s32[120,3,2]{0,2,1:T(2,128)}, u32[]{:S(2)}) copy-start(s32[120,3,2]{0,2,1:T(2,128)} %param.21) | copy-start | bytes 8644
  13.7 18.5 %copy-start.16 = (bf16[80]{0:T(256)(128)(2,1)S(1)}, bf16[80]{0:T(256)(128)(2,1)}, u32[]{:S(2)}) copy-start(bf16[80]{0:T(256)(128)(2,1)} %param.19) | copy-start | bytes 484
  16.6 25.4 %copy-start.3 = (bf16[3,80,576]{2,1,0:T(8,128)(2,1)}, bf16[3,80,576]{2,1,0:T(8,128)(2,1)S(1)}, u32[]{:S(2)}) copy-start(bf16[3,80,576]{2,1,0:T(8,128)(2,1)S(1)} %get-tuple-element.62.refs_0_) | copy-start | bytes 829444
  16.6 15.9 %copy-start.10 = (bf16[2,512,128]{2,1,0:T(8,128)(2,1)S(1)}, bf16[2,512,128]{2,1,0:T(8,128)(2,1)}, u32[]{:S(2)}) copy-start(bf16[2,512,128]{2,1,0:T(8,128)(2,1)} %param.16) | copy-start | bytes 786436
  16.6 15.9 %slice-start = ((bf16[2,512,128]{2,1,0:T(8,128)(2,1)}), bf16[2,224,128]{2,1,0:T(8,128)(2,1)S(1)}, s32[]{:S(2)}) async-start(bf16[2,512,128]{2,1,0:T(8,128)(2,1)} %param.16), calls=%async_computation.8 | async-start | bytes 229376 | tf_op jit(solution)/shard_map/slice | solution.py:334
  16.6 25.2 %copy-start.11 = (bf16[120,2,576]{0,2,1:T(8,128)(2,1)S(1)}, bf16[120,2,576]{0,2,1:T(8,128)(2,1)}, u32[]{:S(2)}) copy-start(bf16[120,2,576]{0,2,1:T(8,128)(2,1)} %param.13) | copy-start | bytes 829444
  16.6 16.0 %collective-permute-start = (bf16[3,80,576]{2,1,0:T(8,128)(2,1)}, bf16[3,80,576]{2,1,0:T(8,128)(2,1)S(1)}, u32[]{:S(2)}, u32[]{:S(2)}) collective-permute-start(bf16[3,80,576]{2,1,0:T(8,128)(2,1)} %get-tuple-element.41), channel_id=1, source_target_pairs={{0,1},{1,0},{2,3},{3,2},{4,5},{5,4},{6,7},{7,6},{8,9},{9,8},{10,11... | collective-permute-start | bytes 829448 | tf_op jit(solution)/shard_map/ppermute | solution.py:298
  19.6 17.4 %collective-permute-start.1 = (bf16[3,80,576]{2,1,0:T(8,128)(2,1)}, bf16[3,80,576]{2,1,0:T(8,128)(2,1)S(1)}, u32[]{:S(2)}, u32[]{:S(2)}) collective-permute-start(bf16[3,80,576]{2,1,0:T(8,128)(2,1)} %get-tuple-element.42), channel_id=1, source_target_pairs={{0,2},{1,3},{2,0},{3,1},{4,6},{5,7},{6,4},{7,5},{8,10},{9,11},{10,... | collective-permute-start | bytes 829448 | tf_op jit(solution)/shard_map/ppermute | solution.py:298
  21.8 39.3 %collective-permute-start.2 = (bf16[3,80,576]{2,1,0:T(8,128)(2,1)}, bf16[3,80,576]{2,1,0:T(8,128)(2,1)}, u32[]{:S(2)}, u32[]{:S(2)}) collective-permute-start(bf16[3,80,576]{2,1,0:T(8,128)(2,1)} %get-tuple-element.43), channel_id=1, source_target_pairs={{0,3},{1,2},{2,1},{3,0},{4,7},{5,6},{6,5},{7,4},{8,11},{9,10},{10,... | collective-permute-start | bytes 829448 | tf_op jit(solution)/shard_map/ppermute | solution.py:298
  25.1 36.0 %collective-permute-start.3 = (bf16[3,80,576]{2,1,0:T(8,128)(2,1)}, bf16[3,80,576]{2,1,0:T(8,128)(2,1)}, u32[]{:S(2)}, u32[]{:S(2)}) collective-permute-start(bf16[3,80,576]{2,1,0:T(8,128)(2,1)} %get-tuple-element.44), channel_id=1, source_target_pairs={{0,4},{1,5},{2,6},{3,7},{4,0},{5,1},{6,2},{7,3},{8,12},{9,13},{10,... | collective-permute-start | bytes 829448 | tf_op jit(solution)/shard_map/ppermute | solution.py:298
  29.1 32.0 %collective-permute-start.4 = (bf16[3,80,576]{2,1,0:T(8,128)(2,1)}, bf16[3,80,576]{2,1,0:T(8,128)(2,1)}, u32[]{:S(2)}, u32[]{:S(2)}) collective-permute-start(bf16[3,80,576]{2,1,0:T(8,128)(2,1)} %get-tuple-element.45), channel_id=1, source_target_pairs={{0,5},{1,4},{2,7},{3,6},{4,1},{5,0},{6,3},{7,2},{8,13},{9,12},{10,... | collective-permute-start | bytes 829448 | tf_op jit(solution)/shard_map/ppermute | solution.py:298
  33.3 27.8 %collective-permute-start.5 = (bf16[3,80,576]{2,1,0:T(8,128)(2,1)}, bf16[3,80,576]{2,1,0:T(8,128)(2,1)}, u32[]{:S(2)}, u32[]{:S(2)}) collective-permute-start(bf16[3,80,576]{2,1,0:T(8,128)(2,1)} %get-tuple-element.46), channel_id=1, source_target_pairs={{0,6},{1,7},{2,4},{3,5},{4,2},{5,3},{6,0},{7,1},{8,14},{9,15},{10,... | collective-permute-start | bytes 829448 | tf_op jit(solution)/shard_map/ppermute | solution.py:298
  37.0 5.0 %copy-start.7 = (bf16[3,80,576]{2,1,0:T(8,128)(2,1)}, bf16[3,80,576]{2,1,0:T(8,128)(2,1)S(1)}, u32[]{:S(2)}) copy-start(bf16[3,80,576]{2,1,0:T(8,128)(2,1)S(1)} %collective-permute-done.1.refs_2_) | copy-start | bytes 829444
  37.0 24.1 %collective-permute-start.6 = (bf16[3,80,576]{2,1,0:T(8,128)(2,1)}, bf16[3,80,576]{2,1,0:T(8,128)(2,1)}, u32[]{:S(2)}, u32[]{:S(2)}) collective-permute-start(bf16[3,80,576]{2,1,0:T(8,128)(2,1)} %get-tuple-element.47), channel_id=1, source_target_pairs={{0,7},{1,6},{2,5},{3,4},{4,3},{5,2},{6,1},{7,0},{8,15},{9,14},{10,... | collective-permute-start | bytes 829448 | tf_op jit(solution)/shard_map/ppermute | solution.py:298
  43.6 22.2 %copy-start.9 = (s32[16,16]{1,0:T(8,128)S(1)}, s32[16,16]{1,0:T(8,128)}, u32[]{:S(2)}) copy-start(s32[16,16]{1,0:T(8,128)} %mask.1) | copy-start | bytes 3076
  61.1 4.7 %collective-permute-start.7 = (bf16[16,288,128]{2,1,0:T(8,128)(2,1)S(1)}, bf16[16,288,128]{2,1,0:T(8,128)(2,1)S(1)}, u32[]{:S(2)}, u32[]{:S(2)}) collective-permute-start(bf16[16,288,128]{2,1,0:T(8,128)(2,1)S(1)} %all-to-all-done.ka), channel_id=1, source_target_pairs={{0,1},{1,0},{2,3},{3,2},{4,5},{5,4},{6,7},{7,6},{8,9},{9,8},{10,11... | collective-permute-start | bytes 3538952 | tf_op jit(solution)/shard_map/ppermute | solution.py:350
  68.3 3.5 %collective-permute-start.8 = (bf16[16,80,128]{2,1,0:T(8,128)(2,1)S(1)}, bf16[16,80,128]{2,1,0:T(8,128)(2,1)S(1)}, u32[]{:S(2)}, u32[]{:S(2)}) collective-permute-start(bf16[16,80,128]{2,1,0:T(8,128)(2,1)S(1)} %get-tuple-element.55), channel_id=1, source_target_pairs={{0,1},{1,0},{2,3},{3,2},{4,5},{5,4},{6,7},{7,6},{8,9},{9,8},{10,11... | collective-permute-start | bytes 983048 | tf_op jit(solution)/shard_map/ppermute | solution.py:363
  72.7 22.7 %all-to-all-start.1 = ((bf16[16,80,128]{2,1,0:T(8,128)(2,1)}), bf16[16,80,128]{2,1,0:T(8,128)(2,1)S(1)}, u32[]{:S(2)}, u32[]{:S(2)}) async-start(bf16[16,80,128]{2,1,0:T(8,128)(2,1)} %add_convert_fusion), calls=%async_computation.1 | async-start | bytes 655360 | tf_op jit(solution)/shard_map/all_to_all | solution.py:249
  117.8 17.5 %all-to-all-start.3 = ((bf16[8,96,512]{2,1,0:T(8,128)(2,1)}), bf16[8,96,512]{2,1,0:T(8,128)(2,1)S(1)}, u32[]{:S(2)}, u32[]{:S(2)}) async-start(bf16[8,96,512]{2,1,0:T(8,128)(2,1)} %get-tuple-element.61), calls=%async_computation.3 | async-start | bytes 1572864 | tf_op jit(solution)/shard_map/all_to_all | solution.py:249
  (6 other events, 8.3 us)

commit v4 on v3

--- a/solution.py
+++ b/solution.py
@@ -284,21 +284,6 @@
     own_half = lax.dynamic_slice_in_dim(keys, core * half, half, 0)
     keys_a = exchange(jnp.broadcast_to(own_half[None], (ctx_count, half, TOK)), CTX)
 
-    place = jnp.stack([my_block, core, lax.axis_index(NEAR)]).astype(jnp.int32)
-    pairs = local_experts // 2
-    block = (pairs, run, 6 * part)
-    packed = call(
-        pack,
-        [shape(block)] * near_count,
-        [SMEM] + [VMEM] * 3,
-        [pltpu.VMEM((near_count,) + block, BF16)],
-    )(place, w_gate, w_up, w_down.transpose(0, 2, 1))
-
-    def flipped(x, flip):
-        return lax.ppermute(x, NEAR, [(a, a ^ flip) for a in range(near_count)])
-
-    moved = [packed[0]] + [flipped(packed[i], i) for i in range(1, near_count)]
-
     group_range = jnp.arange(ctx_count)
     expert_range = jnp.arange(local_experts)
     member = jnp.zeros((block_rows, ctx_count), jnp.int32)
@@ -327,6 +312,22 @@
     )
     places = jnp.pad(placement.reshape(block_rows, slots).T, ((0, 0), (0, pad_rows)))
 
+    place = jnp.stack([my_block, core, lax.axis_index(NEAR)]).astype(jnp.int32)
+    pairs = local_experts // 2
+    block = (pairs, run, 6 * part)
+    w_gate, places, slot_shares = lax.optimization_barrier((w_gate, places, slot_shares))
+    packed = call(
+        pack,
+        [shape(block)] * near_count,
+        [SMEM] + [VMEM] * 3,
+        [pltpu.VMEM((near_count,) + block, BF16)],
+    )(place, w_gate, w_up, w_down.transpose(0, 2, 1))
+
+    def flipped(x, flip):
+        return lax.ppermute(x, NEAR, [(a, a ^ flip) for a in range(near_count)])
+
+    moved = [packed[0]] + [flipped(packed[i], i) for i in range(1, 6)]
+
     wide_q = jnp.pad(queries.transpose(1, 0, 2), ((0, 0), (0, pad_rows), (0, 0)))
     wide_q = wide_q.reshape(heads * TOK, key_width)
     q_low, q_high = wide_q[:, :half], wide_q[:, half:]
@@ -361,7 +362,9 @@
         ],
     )(place, block_mask, q_a, q_b, keys_a, keys_b, v_a, v_b, out_weights)
     summed = (mine + lax.ppermute(theirs, "core", [(0, 1), (1, 0)]).astype(F32)).astype(BF16)
+    summed, late = lax.optimization_barrier((summed, packed[6:]))
     parts = exchange(summed, ZX)
+    moved += [flipped(x, i + 6) for i, x in enumerate(late)]
 
     hidden, sent = call(make_rows, [shape((run, TOK)), shape((slots, TOK))], [VMEM] * 5)(
         parts,
@@ -370,14 +373,6 @@
         places,
         slot_shares,
     )
-    weights_in, weights_back = call(
-        functools.partial(unpack, part),
-        [
-            shape((pairs * 4 * part, near_count * run)),
-            shape((near_count, run, local_experts * part)),
-        ],
-        [VMEM] * near_count,
-    )(*moved)
     got = exchange(sent.reshape(ctx_count, SLOT, TOK), CTX).reshape(slots, TOK)
     spread, keep, pick_weight = call(
         functools.partial(spread_rows, run + 16, first_share),
@@ -388,7 +383,16 @@
         ],
         [VMEM],
     )(got)
+    spread, moved = lax.optimization_barrier((spread, moved))
     inputs = exchange(spread, NEAR)
+    weights_in, weights_back = call(
+        functools.partial(unpack, part),
+        [
+            shape((pairs * 4 * part, near_count * run)),
+            shape((near_count, run, local_experts * part)),
+        ],
+        [VMEM] * near_count,
+    )(*moved)
     partial_sums = call(
         functools.partial(project_up, run, sub),
         shape((far_count, 4 * sub + 16, slots)),

time: 197 us -> 187 us (0.949)
  waiting for transfers between devices: 37.4 us -> 26.2 us
    all_to_all x3, waiting for transfers between devices: 18.3 us -> 11.8 us  [exchange(): return lax.all_to_all(x, axes, split_axis=0, concat_axis=0, tiled=True)]
    ppermute x7, waiting for transfers between devices: 15.4 us -> 10.7 us  [flipped(): return lax.ppermute(x, NEAR, [(a, a ^ flip) for a in range(near_count)])]
    unnamed x35 -> x39, local copies, waits for them, and re-layouts: 5.01 us -> 7.46 us
  transfers between devices with their start and end apart: 12 -> 12, of which waited for: 5 -> 6; matrix products, arithmetic and copies ran while one was open for 3% -> 4% of each run, Pallas kernels for 2% -> 3%
where the time goes in v4:
time: 187 us; the launch traced here: 186 us
  blocking collectives  76.4 us (41%)
  starting transfers between devices  53.9 us (29%)
  waiting for transfers between devices  26.2 us (14%)
  local copies, waits for them, and re-layouts  12.8 us (7%)
  Pallas kernels  12.7 us (7%)
  other arithmetic  3.62 us (2%)
    all_to_all x5, blocking collectives, exchange(): return lax.all_to_all(x, axes, split_axis=0, concat_axis=0, tiled=True)  76.4 us
    all_to_all x3, starting transfers between devices, exchange(): return lax.all_to_all(x, axes, split_axis=0, concat_axis=0, tiled=True)  28 us
    ppermute x7, starting transfers between devices, flipped(): return lax.ppermute(x, NEAR, [(a, a ^ flip) for a in range(near_count)])  21.3 us
    all_to_all x3, waiting for transfers between devices, exchange(): return lax.all_to_all(x, axes, split_axis=0, concat_axis=0, tiled=True)  11.8 us
    ppermute x7, waiting for transfers between devices, flipped(): return lax.ppermute(x, NEAR, [(a, a ^ flip) for a in range(near_count)])  10.7 us
    unnamed x39, local copies, waits for them, and re-layouts  7.46 us
  transfers between devices with their start and end apart: 12, of which 6 were waited for; matrix products, arithmetic and copies ran while one was open for 4% of the time, Pallas kernels for 3%

profile of v4, /device:TPU:1, one launch (start us, length us, event | category | flops | bytes accessed | tf_op | source)
XLA Modules:
  0.0 186.3 jit_solution(14157842286506563483)
XLA Ops:
  2.1 10.3 %all-to-all-start = ((bf16[16,288,128]{2,1,0:T(8,128)(2,1)}), bf16[16,288,128]{2,1,0:T(8,128)(2,1)S(1)}, u32[]{:S(2)}, u32[]{:S(2)}) async-start(bf16[16,288,128]{2,1,0:T(8,128)(2,1)} %broadcast_in_dim.7), calls=%async_computation | async-start | bytes 2359296 | tf_op jit(solution)/shard_map/all_to_all | solution.py:249
  15.4 2.6 %shard_map.127 = (bf16[3,80,576]{2,1,0:T(8,128)(2,1)S(1)}, bf16[3,80,576]{2,1,0:T(8,128)(2,1)}, bf16[3,80,576]{2,1,0:T(8,128)(2,1)}, bf16[3,80,576]{2,1,0:T(8,12...) custom-call(s32[3]{0:T(128)S(1)} %pad_add_fusion.place, ...), custom_call_target="tpu_custom_call" | custom-call | tf_op jit(solution)/shard_map/pallas_call | solution.py:319
  19.5 2.9 %collective-permute-start = (bf16[3,80,576]{2,1,0:T(8,128)(2,1)}, bf16[3,80,576]{2,1,0:T(8,128)(2,1)}, u32[]{:S(2)}, u32[]{:S(2)}) collective-permute-start(bf16[3,80,576]{2,1,0:T(8,128)(2,1)} %get-tuple-element.55), channel_id=1, source_target_pairs={{0,1},{1,0},{2,3},{3,2},{4,5},{5,4},{6,7},{7,6},{8,9},{9,8},{10,11... | collective-permute-start | bytes 829448 | tf_op jit(solution)/shard_map/ppermute | solution.py:327
  22.3 2.2 %collective-permute-start.1 = (bf16[3,80,576]{2,1,0:T(8,128)(2,1)}, bf16[3,80,576]{2,1,0:T(8,128)(2,1)}, u32[]{:S(2)}, u32[]{:S(2)}) collective-permute-start(bf16[3,80,576]{2,1,0:T(8,128)(2,1)} %get-tuple-element.56), channel_id=1, source_target_pairs={{0,2},{1,3},{2,0},{3,1},{4,6},{5,7},{6,4},{7,5},{8,10},{9,11},{10,... | collective-permute-start | bytes 829448 | tf_op jit(solution)/shard_map/ppermute | solution.py:327
  24.6 3.2 %collective-permute-start.2 = (bf16[3,80,576]{2,1,0:T(8,128)(2,1)}, bf16[3,80,576]{2,1,0:T(8,128)(2,1)}, u32[]{:S(2)}, u32[]{:S(2)}) collective-permute-start(bf16[3,80,576]{2,1,0:T(8,128)(2,1)} %get-tuple-element.57), channel_id=1, source_target_pairs={{0,3},{1,2},{2,1},{3,0},{4,7},{5,6},{6,5},{7,4},{8,11},{9,10},{10,... | collective-permute-start | bytes 829448 | tf_op jit(solution)/shard_map/ppermute | solution.py:327
  27.8 4.0 %collective-permute-start.3 = (bf16[3,80,576]{2,1,0:T(8,128)(2,1)}, bf16[3,80,576]{2,1,0:T(8,128)(2,1)}, u32[]{:S(2)}, u32[]{:S(2)}) collective-permute-start(bf16[3,80,576]{2,1,0:T(8,128)(2,1)} %get-tuple-element.58), channel_id=1, source_target_pairs={{0,4},{1,5},{2,6},{3,7},{4,0},{5,1},{6,2},{7,3},{8,12},{9,13},{10,... | collective-permute-start | bytes 829448 | tf_op jit(solution)/shard_map/ppermute | solution.py:327
  31.8 2.0 %collective-permute-start.4 = (bf16[3,80,576]{2,1,0:T(8,128)(2,1)}, bf16[3,80,576]{2,1,0:T(8,128)(2,1)}, u32[]{:S(2)}, u32[]{:S(2)}) collective-permute-start(bf16[3,80,576]{2,1,0:T(8,128)(2,1)} %get-tuple-element.59), channel_id=1, source_target_pairs={{0,5},{1,4},{2,7},{3,6},{4,1},{5,0},{6,3},{7,2},{8,13},{9,12},{10,... | collective-permute-start | bytes 829448 | tf_op jit(solution)/shard_map/ppermute | solution.py:327
  39.6 4.0 %collective-permute-done.1.refs_2_ = bf16[3,80,576]{2,1,0:T(8,128)(2,1)} collective-permute-done((bf16[3,80,576]{2,1,0:T(8,128)(2,1)}, bf16[3,80,576]{2,1,0:T(8,128)(2,1)}, u32[]{:S(2)}, u32[]{:S(2)}) %collective-permute-start.1) | collective-permute-done | bytes 276512 | tf_op jit(solution)/shard_map/ppermute | solution.py:327
  43.6 6.7 %collective-permute-done.2.refs_3_ = bf16[3,80,576]{2,1,0:T(8,128)(2,1)} collective-permute-done((bf16[3,80,576]{2,1,0:T(8,128)(2,1)}, bf16[3,80,576]{2,1,0:T(8,128)(2,1)}, u32[]{:S(2)}, u32[]{:S(2)}) %collective-permute-start.2) | collective-permute-done | bytes 276512 | tf_op jit(solution)/shard_map/ppermute | solution.py:327
  50.3 2.3 %collective-permute-start.5 = (bf16[16,288,128]{2,1,0:T(8,128)(2,1)S(1)}, bf16[16,288,128]{2,1,0:T(8,128)(2,1)S(1)}, u32[]{:S(2)}, u32[]{:S(2)}) collective-permute-start(bf16[16,288,128]{2,1,0:T(8,128)(2,1)S(1)} %all-to-all-done.ka), channel_id=1, source_target_pairs={{0,1},{1,0},{2,3},{3,2},{4,5},{5,4},{6,7},{7,6},{8,9},{9,8},{10,11... | collective-permute-start | bytes 3538952 | tf_op jit(solution)/shard_map/ppermute | solution.py:351
  52.6 2.5 %collective-permute-done.5.kb = bf16[16,288,128]{2,1,0:T(8,128)(2,1)S(1)} collective-permute-done((bf16[16,288,128]{2,1,0:T(8,128)(2,1)S(1)}, bf16[16,288,128]{2,1,0:T(8,128)(2,1)S(1)}, u32[]{:S(2)}, u32[]{:S(2)}) %collective-permute-start.5) | collective-permute-done | bytes 1179680 | tf_op jit(solution)/shard_map/ppermute | solution.py:351
  55.1 2.5 %shard_map.128 = (f32[16,80,128]{2,1,0:T(8,128)S(1)}, bf16[16,80,128]{2,1,0:T(8,128)(2,1)S(1)}) custom-call(s32[3]{0:T(128)S(1)} %pad_add_fusion.place, s32[16,16]{1,0:T(8,128)S(1)} %copy-done.9, bf16[256,288]{1,0:T(8,128)(2,1)S(1)} %get-tuple-element.62.qa, bf16[256,288]{1,0:T(8,128)(2,1)S(1)} %get-tuple-element.63.qb, ...), custom_call_target="tpu_custom_call" | custom-call | tf_op jit(solution)/shard_map/pallas_call | solution.py:353
  57.6 2.4 %collective-permute-start.6 = (bf16[16,80,128]{2,1,0:T(8,128)(2,1)S(1)}, bf16[16,80,128]{2,1,0:T(8,128)(2,1)S(1)}, u32[]{:S(2)}, u32[]{:S(2)}) collective-permute-start(bf16[16,80,128]{2,1,0:T(8,128)(2,1)S(1)} %get-tuple-element.69), channel_id=1, source_target_pairs={{0,1},{1,0},{2,3},{3,2},{4,5},{5,4},{6,7},{7,6},{8,9},{9,8},{10,11... | collective-permute-start | bytes 983048 | tf_op jit(solution)/shard_map/ppermute | solution.py:364
  62.0 10.3 %all-to-all-start.1 = ((bf16[16,80,128]{2,1,0:T(8,128)(2,1)}), bf16[16,80,128]{2,1,0:T(8,128)(2,1)S(1)}, u32[]{:S(2)}, u32[]{:S(2)}) async-start(bf16[16,80,128]{2,1,0:T(8,128)(2,1)} %add_convert_fusion), calls=%async_computation.1 | async-start | bytes 655360 | tf_op jit(solution)/shard_map/all_to_all | solution.py:249
  72.3 4.2 %collective-permute-start.7 = (bf16[3,80,576]{2,1,0:T(8,128)(2,1)S(1)}, bf16[3,80,576]{2,1,0:T(8,128)(2,1)S(1)}, u32[]{:S(2)}, u32[]{:S(2)}) collective-permute-start(bf16[3,80,576]{2,1,0:T(8,128)(2,1)S(1)} %copy-done.13), channel_id=1, source_target_pairs={{0,6},{1,7},{2,4},{3,5},{4,2},{5,3},{6,0},{7,1},{8,14},{9,15},{10,... | collective-permute-start | bytes 829448 | tf_op jit(solution)/shard_map/ppermute | solution.py:327
  76.5 2.8 %collective-permute-start.8 = (bf16[3,80,576]{2,1,0:T(8,128)(2,1)S(1)}, bf16[3,80,576]{2,1,0:T(8,128)(2,1)S(1)}, u32[]{:S(2)}, u32[]{:S(2)}) collective-permute-start(bf16[3,80,576]{2,1,0:T(8,128)(2,1)S(1)} %copy-done.11), channel_id=1, source_target_pairs={{0,7},{1,6},{2,5},{3,4},{4,3},{5,2},{6,1},{7,0},{8,15},{9,14},{10,... | collective-permute-start | bytes 829448 | tf_op jit(solution)/shard_map/ppermute | solution.py:327
  79.4 5.7 %all-to-all-done.1.parts = bf16[16,80,128]{2,1,0:T(8,128)(2,1)S(1)} async-done(((bf16[16,80,128]{2,1,0:T(8,128)(2,1)}), bf16[16,80,128]{2,1,0:T(8,128)(2,1)S(1)}, u32[]{:S(2)}, u32[]{:S(2)}) %all-to-all-start.1) | async-done | bytes 327712 | tf_op jit(solution)/shard_map/all_to_all | solution.py:249
  85.4 20.3 %all_to_all.40 = bf16[16,32,128]{2,1,0:T(8,128)(2,1)S(1)} all-to-all(bf16[16,32,128]{2,1,0:T(8,128)(2,1)S(1)} %bitcast.67), channel_id=1, replica_groups=mesh['y'=8,'xh'=2,'za'=4,'zb'=2,'xl'=2,'core'=2] {'y','xh'}, dimensions={0} | all-to-all | bytes 262144 | tf_op jit(solution)/shard_map/all_to_all | solution.py:249
  107.6 7.4 %all-to-all-start.3 = ((bf16[8,96,512]{2,1,0:T(8,128)(2,1)}), bf16[8,96,512]{2,1,0:T(8,128)(2,1)S(1)}, u32[]{:S(2)}, u32[]{:S(2)}) async-start(bf16[8,96,512]{2,1,0:T(8,128)(2,1)} %get-tuple-element.87), calls=%async_computation.3 | async-start | bytes 1572864 | tf_op jit(solution)/shard_map/all_to_all | solution.py:249
  119.7 6.0 %all-to-all-done.3.inputs = bf16[8,96,512]{2,1,0:T(8,128)(2,1)S(1)} async-done(((bf16[8,96,512]{2,1,0:T(8,128)(2,1)}), bf16[8,96,512]{2,1,0:T(8,128)(2,1)S(1)}, u32[]{:S(2)}, u32[]{:S(2)}) %all-to-all-start.3) | async-done | bytes 786464 | tf_op jit(solution)/shard_map/all_to_all | solution.py:249
  127.5 16.0 %all_to_all.41.got = bf16[4,112,512]{2,1,0:T(8,128)(2,1)S(1)} all-to-all(bf16[4,112,512]{2,1,0:T(8,128)(2,1)S(1)} %shard_map.132), channel_id=1, replica_groups=mesh['y'=8,'xh'=2,'za'=4,'zb'=2,'xl'=2,'core'=2] {'za'}, dimensions={0} | all-to-all | bytes 917504 | tf_op jit(solution)/shard_map/all_to_all | solution.py:249
  143.6 11.9 %all_to_all.42.acts = bf16[4,48,512]{2,1,0:T(8,128)(2,1)S(1)} all-to-all(bf16[4,48,512]{2,1,0:T(8,128)(2,1)S(1)} %shard_map.133), channel_id=1, replica_groups=mesh['y'=8,'xh'=2,'za'=4,'zb'=2,'xl'=2,'core'=2] {'za'}, dimensions={0} | all-to-all | bytes 393216 | tf_op jit(solution)/shard_map/all_to_all | solution.py:249
  157.2 15.4 %all_to_all.43.got = bf16[8,80,512]{2,1,0:T(8,128)(2,1)S(1)} all-to-all(bf16[8,80,512]{2,1,0:T(8,128)(2,1)S(1)} %shard_map.134), channel_id=1, replica_groups=mesh['y'=8,'xh'=2,'za'=4,'zb'=2,'xl'=2,'core'=2] {'zb','xl','core'}, dimensions={0} | all-to-all | bytes 1310720 | tf_op jit(solution)/shard_map/all_to_all | solution.py:249
  172.8 12.6 %all_to_all.44 = bf16[16,32,128]{2,1,0:T(8,128)(2,1)S(1)} all-to-all(bf16[16,32,128]{2,1,0:T(8,128)(2,1)S(1)} %bitcast.66), channel_id=1, replica_groups=mesh['y'=8,'xh'=2,'za'=4,'zb'=2,'xl'=2,'core'=2] {'y','xh'}, dimensions={0} | all-to-all | bytes 262144 | tf_op jit(solution)/shard_map/all_to_all | solution.py:249
  (89 shorter events, 25.5 us)
Async XLA Ops:
  2.1 10.4 %copy-start.17 = (s32[120,3]{0,1:T(4,128)S(1)}, s32[120,3]{0,1:T(4,128)}, u32[]{:S(2)}) copy-start(s32[120,3]{0,1:T(4,128)} %param.20) | copy-start | bytes 4324
  2.1 11.2 %copy-start.15 = (bf16[120,3,2]{0,2,1:T(2,128)(2,1)S(1)}, bf16[120,3,2]{0,2,1:T(2,128)(2,1)}, u32[]{:S(2)}) copy-start(bf16[120,3,2]{0,2,1:T(2,128)(2,1)} %param.22) | copy-start | bytes 4324
  2.1 11.2 %copy-start.16 = (s32[120,3,2]{0,2,1:T(2,128)S(1)}, s32[120,3,2]{0,2,1:T(2,128)}, u32[]{:S(2)}) copy-start(s32[120,3,2]{0,2,1:T(2,128)} %param.21) | copy-start | bytes 8644
  2.1 48.2 %all-to-all-start = ((bf16[16,288,128]{2,1,0:T(8,128)(2,1)}), bf16[16,288,128]{2,1,0:T(8,128)(2,1)S(1)}, u32[]{:S(2)}, u32[]{:S(2)}) async-start(bf16[16,288,128]{2,1,0:T(8,128)(2,1)} %broadcast_in_dim.7), calls=%async_computation | async-start | bytes 2359296 | tf_op jit(solution)/shard_map/all_to_all | solution.py:249
  12.5 1.8 copy-start
  12.5 1.8 copy-start.1
  14.1 19.7 %slice-start = ((bf16[2,512,128]{2,1,0:T(8,128)(2,1)}), bf16[2,224,128]{2,1,0:T(8,128)(2,1)S(1)}, s32[]{:S(2)}) async-start(bf16[2,512,128]{2,1,0:T(8,128)(2,1)} %param.16), calls=%async_computation.8 | async-start | bytes 229376 | tf_op jit(solution)/shard_map/slice | solution.py:335
  15.4 19.4 %copy-start.18 = (bf16[80]{0:T(256)(128)(2,1)S(1)}, bf16[80]{0:T(256)(128)(2,1)}, u32[]{:S(2)}) copy-start(bf16[80]{0:T(256)(128)(2,1)} %param.19) | copy-start | bytes 484
  19.5 17.3 %copy-start.3 = (bf16[3,80,576]{2,1,0:T(8,128)(2,1)}, bf16[3,80,576]{2,1,0:T(8,128)(2,1)S(1)}, u32[]{:S(2)}) copy-start(bf16[3,80,576]{2,1,0:T(8,128)(2,1)S(1)} %get-tuple-element.88.refs_0_) | copy-start | bytes 829444
  19.5 20.1 %collective-permute-start = (bf16[3,80,576]{2,1,0:T(8,128)(2,1)}, bf16[3,80,576]{2,1,0:T(8,128)(2,1)}, u32[]{:S(2)}, u32[]{:S(2)}) collective-permute-start(bf16[3,80,576]{2,1,0:T(8,128)(2,1)} %get-tuple-element.55), channel_id=1, source_target_pairs={{0,1},{1,0},{2,3},{3,2},{4,5},{5,4},{6,7},{7,6},{8,9},{9,8},{10,11... | collective-permute-start | bytes 829448 | tf_op jit(solution)/shard_map/ppermute | solution.py:327
  22.3 21.3 %collective-permute-start.1 = (bf16[3,80,576]{2,1,0:T(8,128)(2,1)}, bf16[3,80,576]{2,1,0:T(8,128)(2,1)}, u32[]{:S(2)}, u32[]{:S(2)}) collective-permute-start(bf16[3,80,576]{2,1,0:T(8,128)(2,1)} %get-tuple-element.56), channel_id=1, source_target_pairs={{0,2},{1,3},{2,0},{3,1},{4,6},{5,7},{6,4},{7,5},{8,10},{9,11},{10,... | collective-permute-start | bytes 829448 | tf_op jit(solution)/shard_map/ppermute | solution.py:327
  24.6 25.7 %collective-permute-start.2 = (bf16[3,80,576]{2,1,0:T(8,128)(2,1)}, bf16[3,80,576]{2,1,0:T(8,128)(2,1)}, u32[]{:S(2)}, u32[]{:S(2)}) collective-permute-start(bf16[3,80,576]{2,1,0:T(8,128)(2,1)} %get-tuple-element.57), channel_id=1, source_target_pairs={{0,3},{1,2},{2,1},{3,0},{4,7},{5,6},{6,5},{7,4},{8,11},{9,10},{10,... | collective-permute-start | bytes 829448 | tf_op jit(solution)/shard_map/ppermute | solution.py:327
  27.8 22.5 %collective-permute-start.3 = (bf16[3,80,576]{2,1,0:T(8,128)(2,1)}, bf16[3,80,576]{2,1,0:T(8,128)(2,1)}, u32[]{:S(2)}, u32[]{:S(2)}) collective-permute-start(bf16[3,80,576]{2,1,0:T(8,128)(2,1)} %get-tuple-element.58), channel_id=1, source_target_pairs={{0,4},{1,5},{2,6},{3,7},{4,0},{5,1},{6,2},{7,3},{8,12},{9,13},{10,... | collective-permute-start | bytes 829448 | tf_op jit(solution)/shard_map/ppermute | solution.py:327
  31.8 18.5 %collective-permute-start.4 = (bf16[3,80,576]{2,1,0:T(8,128)(2,1)}, bf16[3,80,576]{2,1,0:T(8,128)(2,1)}, u32[]{:S(2)}, u32[]{:S(2)}) collective-permute-start(bf16[3,80,576]{2,1,0:T(8,128)(2,1)} %get-tuple-element.59), channel_id=1, source_target_pairs={{0,5},{1,4},{2,7},{3,6},{4,1},{5,0},{6,3},{7,2},{8,13},{9,12},{10,... | collective-permute-start | bytes 829448 | tf_op jit(solution)/shard_map/ppermute | solution.py:327
  36.8 1.6 copy-start.14
  36.8 18.3 %copy-start.9 = (s32[16,16]{1,0:T(8,128)S(1)}, s32[16,16]{1,0:T(8,128)}, u32[]{:S(2)}) copy-start(s32[16,16]{1,0:T(8,128)} %mask.1) | copy-start | bytes 3076
  50.3 4.7 %collective-permute-start.5 = (bf16[16,288,128]{2,1,0:T(8,128)(2,1)S(1)}, bf16[16,288,128]{2,1,0:T(8,128)(2,1)S(1)}, u32[]{:S(2)}, u32[]{:S(2)}) collective-permute-start(bf16[16,288,128]{2,1,0:T(8,128)(2,1)S(1)} %all-to-all-done.ka), channel_id=1, source_target_pairs={{0,1},{1,0},{2,3},{3,2},{4,5},{5,4},{6,7},{7,6},{8,9},{9,8},{10,11... | collective-permute-start | bytes 3538952 | tf_op jit(solution)/shard_map/ppermute | solution.py:351
  57.6 14.7 %copy-start.13 = (bf16[3,80,576]{2,1,0:T(8,128)(2,1)S(1)}, bf16[3,80,576]{2,1,0:T(8,128)(2,1)}, u32[]{:S(2)}) copy-start(bf16[3,80,576]{2,1,0:T(8,128)(2,1)} %copy-done.12) | copy-start | bytes 829444
  57.6 18.9 %copy-start.11 = (bf16[3,80,576]{2,1,0:T(8,128)(2,1)S(1)}, bf16[3,80,576]{2,1,0:T(8,128)(2,1)}, u32[]{:S(2)}) copy-start(bf16[3,80,576]{2,1,0:T(8,128)(2,1)} %copy-done.10) | copy-start | bytes 829444
  57.6 3.7 %collective-permute-start.6 = (bf16[16,80,128]{2,1,0:T(8,128)(2,1)S(1)}, bf16[16,80,128]{2,1,0:T(8,128)(2,1)S(1)}, u32[]{:S(2)}, u32[]{:S(2)}) collective-permute-start(bf16[16,80,128]{2,1,0:T(8,128)(2,1)S(1)} %get-tuple-element.69), channel_id=1, source_target_pairs={{0,1},{1,0},{2,3},{3,2},{4,5},{5,4},{6,7},{7,6},{8,9},{9,8},{10,11... | collective-permute-start | bytes 983048 | tf_op jit(solution)/shard_map/ppermute | solution.py:364
  62.0 23.1 %all-to-all-start.1 = ((bf16[16,80,128]{2,1,0:T(8,128)(2,1)}), bf16[16,80,128]{2,1,0:T(8,128)(2,1)S(1)}, u32[]{:S(2)}, u32[]{:S(2)}) async-start(bf16[16,80,128]{2,1,0:T(8,128)(2,1)} %add_convert_fusion), calls=%async_computation.1 | async-start | bytes 655360 | tf_op jit(solution)/shard_map/all_to_all | solution.py:249
  72.3 34.4 %collective-permute-start.7 = (bf16[3,80,576]{2,1,0:T(8,128)(2,1)S(1)}, bf16[3,80,576]{2,1,0:T(8,128)(2,1)S(1)}, u32[]{:S(2)}, u32[]{:S(2)}) collective-permute-start(bf16[3,80,576]{2,1,0:T(8,128)(2,1)S(1)} %copy-done.13), channel_id=1, source_target_pairs={{0,6},{1,7},{2,4},{3,5},{4,2},{5,3},{6,0},{7,1},{8,14},{9,15},{10,... | collective-permute-start | bytes 829448 | tf_op jit(solution)/shard_map/ppermute | solution.py:327
  76.5 30.3 %collective-permute-start.8 = (bf16[3,80,576]{2,1,0:T(8,128)(2,1)S(1)}, bf16[3,80,576]{2,1,0:T(8,128)(2,1)S(1)}, u32[]{:S(2)}, u32[]{:S(2)}) collective-permute-start(bf16[3,80,576]{2,1,0:T(8,128)(2,1)S(1)} %copy-done.11), channel_id=1, source_target_pairs={{0,7},{1,6},{2,5},{3,4},{4,3},{5,2},{6,1},{7,0},{8,15},{9,14},{10,... | collective-permute-start | bytes 829448 | tf_op jit(solution)/shard_map/ppermute | solution.py:327
  107.6 18.2 %all-to-all-start.3 = ((bf16[8,96,512]{2,1,0:T(8,128)(2,1)}), bf16[8,96,512]{2,1,0:T(8,128)(2,1)S(1)}, u32[]{:S(2)}, u32[]{:S(2)}) async-start(bf16[8,96,512]{2,1,0:T(8,128)(2,1)} %get-tuple-element.87), calls=%async_computation.3 | async-start | bytes 1572864 | tf_op jit(solution)/shard_map/all_to_all | solution.py:249
  (8 other events, 7.0 us)

commit v5 on v4

--- a/solution.py
+++ b/solution.py
@@ -48,10 +48,44 @@
     return lax.dot_general(a, b, (((1,), (1,)), ((), ())), preferred_element_type=F32)
 
 
-def attend(
-    rows, width, place, mask, qa, qb, ka, kb, va, vb, wo, mine, theirs, top, total, acc_a, acc_b
-):
-    block, core = place[0], place[1]
+def spread_keys(keys, out):
+    count, half, _ = out.shape
+    width, rows = keys.shape
+    own = keys[pl.ds(pl.multiple_of(lax.axis_index("core") * half, half), half), :]
+    own = jnp.concatenate([own, jnp.zeros((half, TOK - rows), BF16)], axis=1)
+    for i in range(count):
+        out[i] = own
+
+
+def route(first, groups, experts, weights, places, shares):
+    picks, rows = groups.shape
+    slots = places.shape[0]
+    count = slots // SLOT
+    group = lax.broadcasted_iota(jnp.int32, (count, rows), 0)
+    hits = [jnp.where(groups[k : k + 1, :] == group, 1.0, 0.0) for k in range(picks)]
+    upto = lax.broadcasted_iota(jnp.int32, (rows, rows), 0)
+    upto = jnp.where(upto <= lax.broadcasted_iota(jnp.int32, (rows, rows), 1), 1.0, 0.0)
+    rank = dot(sum(hits).astype(BF16), upto.astype(BF16)) - 1.0
+    spot = lax.broadcasted_iota(jnp.int32, (count, SLOT, rows), 1).astype(F32)
+    here = jnp.where(rank[:, None, :] == spot, 1.0, 0.0)
+    lane = lax.broadcasted_iota(jnp.int32, (TOK, rows), 0)
+    every = jnp.zeros((slots, rows), F32)
+    share = jnp.zeros((slots, TOK), F32)
+    for k in range(picks):
+        placed = (hits[k][:, None, :] * here).reshape(slots, rows)
+        every = every + placed
+        table = jnp.zeros((TOK, rows), F32)
+        for m in range(experts.shape[1]):
+            weight = weights[k, m : m + 1, :].astype(F32)
+            table = table + jnp.where(lane == first + experts[k, m : m + 1, :], weight, 0.0)
+        share = share + dot_nt(placed.astype(BF16), table.astype(BF16))
+    every = jnp.concatenate([every, jnp.zeros((slots, TOK - rows), F32)], axis=1)
+    places[...] = every.astype(BF16)
+    shares[...] = share.astype(BF16)
+
+
+def attend(rows, width, mask, qa, qb, ka, kb, va, vb, out, top, total, acc_a, acc_b):
+    block = lax.axis_index(CTX)
     inverse_root = width**-0.5
     q_a, q_b = qa[...], qb[...]
     query = lax.broadcasted_iota(jnp.int32, (2 * TOK, TOK), 0) % TOK
@@ -98,12 +132,14 @@
             low = (latent - high.astype(F32)).astype(BF16)
             value = value + dot(high, up[head]) + dot(low, up[head])
         values.append(value.T.astype(BF16))
-    stacked = jnp.concatenate(values, axis=0)
-    runs, _, run, depth = wo.shape
-    mine[...] = dot(wo[:, core].reshape(runs * run, depth), stacked).reshape(runs, run, TOK)
-    theirs[...] = (
-        dot(wo[:, 1 - core].reshape(runs * run, depth), stacked).reshape(runs, run, TOK).astype(BF16)
-    )
+    out[...] = jnp.concatenate(values, axis=0)
+
+
+def project_out(mine, theirs, weights_mine, weights_theirs, out):
+    runs, run, depth = weights_mine.shape
+    total = dot(weights_mine[...].reshape(runs * run, depth), mine[...])
+    total = total + dot(weights_theirs[...].reshape(runs * run, depth), theirs[...])
+    out[...] = total.reshape(runs, run, TOK).astype(BF16)
 
 
 def split_pair(value):
@@ -148,7 +184,7 @@
     weight[...] = jnp.concatenate(picked, axis=0)
 
 
-def pack(place, gate, up, down, *refs):
+def pack(gate, up, down, *refs):
     outs, held = refs[:-1], refs[-1]
     count = held.shape[0]
     part = gate.shape[2] // count
@@ -161,7 +197,7 @@
             pieces += [down[2 * pair, :, span], down[2 * pair + 1, :, span]]
             held[near, pair] = jnp.concatenate(pieces, axis=1)
     for flip in range(count):
-        outs[flip][...] = held[place[2] ^ flip]
+        outs[flip][...] = held[lax.axis_index(NEAR) ^ flip]
 
 
 def unpack(part, *refs):
@@ -174,10 +210,10 @@
         back[flip] = jnp.concatenate([g[pair, :, 4 * part :] for pair in range(pairs)], axis=1)
 
 
-def project_up(run, sub, place, inputs, weights, keep, out):
+def project_up(run, sub, inputs, weights, keep, out):
     count, _, slots = inputs.shape
     features = jnp.concatenate(
-        [inputs[place[2] ^ flip, :run, :] for flip in range(count)], axis=0
+        [inputs[lax.axis_index(NEAR) ^ flip, :run, :] for flip in range(count)], axis=0
     )
     ends = inputs[:, run : run + 16, :].astype(F32)
     ends = jnp.sum(ends, axis=0)
@@ -213,7 +249,7 @@
         out[i] = rounded
 
 
-def project_down(sub, place, acts, keep, weights, out):
+def project_down(sub, acts, keep, weights, out):
     count, _, slots = acts.shape
     wide = acts[...].astype(F32)
     first = wide[:, :sub].reshape(count * sub, slots)
@@ -228,7 +264,7 @@
         )
     stacked = jnp.concatenate(picked, axis=0)
     for flip in range(weights.shape[0]):
-        out[place[2] ^ flip] = dot(weights[flip], stacked).astype(BF16)
+        out[lax.axis_index(NEAR) ^ flip] = dot(weights[flip], stacked).astype(BF16)
 
 
 def finish_rows(got, out):
@@ -267,7 +303,6 @@
     ctx_count = lax.axis_size(CTX)
     near_count = lax.axis_size(NEAR)
     far_count = lax.axis_size(FAR)
-    my_block = lax.axis_index(CTX)
     core = lax.axis_index("core")
     block_rows, key_width = latents.shape
     heads = queries.shape[1]
@@ -280,53 +315,29 @@
     part = hidden_units // near_count
     sub = part // far_count
 
-    keys = jnp.pad(latents.T, ((0, 0), (0, pad_rows)))
-    own_half = lax.dynamic_slice_in_dim(keys, core * half, half, 0)
-    keys_a = exchange(jnp.broadcast_to(own_half[None], (ctx_count, half, TOK)), CTX)
-
-    group_range = jnp.arange(ctx_count)
-    expert_range = jnp.arange(local_experts)
-    member = jnp.zeros((block_rows, ctx_count), jnp.int32)
-    shares = jnp.zeros((block_rows, ctx_count, local_experts), F32)
-    for group_slot in range(group_ids.shape[1]):
-        group_hit = group_ids[:, group_slot, None] == group_range[None, :]
-        member = member + group_hit.astype(jnp.int32)
-        for expert_slot in range(expert_ids.shape[2]):
-            expert_hit = (
-                expert_ids[:, group_slot, expert_slot, None] == expert_range[None, :]
-            ).astype(F32)
-            shares = shares + group_hit.astype(F32)[:, :, None] * expert_hit[
-                :, None, :
-            ] * route_weights[:, group_slot, expert_slot, None, None].astype(F32)
-    ranking = jnp.cumsum(member, axis=0) - 1
-    placement = (
-        (member[:, :, None] == 1) & (ranking[:, :, None] == jnp.arange(SLOT)[None, None, :])
-    ).astype(BF16)
+    spread = call(spread_keys, shape((ctx_count, half, TOK)), [VMEM])(latents.T)
+    keys_a = exchange(spread, CTX)
+
     first_share = run + 16
-    slot_shares = jnp.einsum(
-        "tge,tgc->gce", shares.astype(BF16), placement, preferred_element_type=F32
-    ).astype(BF16)
-    slot_shares = jnp.pad(
-        slot_shares.reshape(slots, local_experts),
-        ((0, 0), (first_share, TOK - first_share - local_experts)),
-    )
-    places = jnp.pad(placement.reshape(block_rows, slots).T, ((0, 0), (0, pad_rows)))
-
-    place = jnp.stack([my_block, core, lax.axis_index(NEAR)]).astype(jnp.int32)
+    places, slot_shares = call(
+        functools.partial(route, first_share), [shape((slots, TOK))] * 2, [VMEM] * 3
+    )(group_ids.T, expert_ids.transpose(1, 2, 0), route_weights.transpose(1, 2, 0))
+
     pairs = local_experts // 2
     block = (pairs, run, 6 * part)
     w_gate, places, slot_shares = lax.optimization_barrier((w_gate, places, slot_shares))
     packed = call(
         pack,
         [shape(block)] * near_count,
-        [SMEM] + [VMEM] * 3,
+        [VMEM] * 3,
         [pltpu.VMEM((near_count,) + block, BF16)],
-    )(place, w_gate, w_up, w_down.transpose(0, 2, 1))
+    )(w_gate, w_up, w_down.transpose(0, 2, 1))
 
     def flipped(x, flip):
         return lax.ppermute(x, NEAR, [(a, a ^ flip) for a in range(near_count)])
 
-    moved = [packed[0]] + [flipped(packed[i], i) for i in range(1, 6)]
+    early = {i: flipped(packed[i], i) for i in (2, 3, 4, 5, 1)}
+    moved = [packed[0]] + [early[i] for i in range(1, 6)]
 
     wide_q = jnp.pad(queries.transpose(1, 0, 2), ((0, 0), (0, pad_rows), (0, 0)))
     wide_q = wide_q.reshape(heads * TOK, key_width)
@@ -336,12 +347,16 @@
     flip = core == 1
     runs = D // run
     out_weights = out_proj.T.reshape(runs // 2, 2, run, heads * value_width)
+    out_mine = jnp.where(flip, out_weights[:, 1], out_weights[:, 0])
+    out_theirs = jnp.where(flip, out_weights[:, 0], out_weights[:, 1])
+    out_theirs = lax.ppermute(out_theirs, "core", [(0, 1), (1, 0)])
     operands = (
         jnp.where(flip, q_high, q_low),
         jnp.where(flip, q_low, q_high),
         jnp.where(flip, v_high, v_low),
         jnp.where(flip, v_low, v_high),
-        out_weights,
+        out_mine,
+        out_theirs,
     )
     resid = jnp.pad(residual.T, ((0, 0), (0, pad_rows)))
     gain = norm_gain.astype(F32)[:, None]
@@ -349,19 +364,22 @@
         (keys_a, operands, moved, places, slot_shares, resid, gain)
     )
     keys_b = lax.ppermute(keys_a, "core", [(0, 1), (1, 0)])
-    q_a, q_b, v_a, v_b, out_weights = operands
-    mine, theirs = call(
+    q_a, q_b, v_a, v_b, out_mine, out_theirs = operands
+    values = call(
         functools.partial(attend, block_rows, key_width),
-        [shape((runs // 2, run, TOK), F32), shape((runs // 2, run, TOK))],
-        [SMEM, SMEM] + [VMEM] * 7,
+        shape((heads * value_width, TOK)),
+        [SMEM] + [VMEM] * 6,
         [
             pltpu.VMEM((2 * TOK, 1), F32),
             pltpu.VMEM((2 * TOK, 1), F32),
             pltpu.VMEM((2 * TOK, half), F32),
             pltpu.VMEM((2 * TOK, half), F32),
         ],
-    )(place, block_mask, q_a, q_b, keys_a, keys_b, v_a, v_b, out_weights)
-    summed = (mine + lax.ppermute(theirs, "core", [(0, 1), (1, 0)]).astype(F32)).astype(BF16)
+    )(block_mask, q_a, q_b, keys_a, keys_b, v_a, v_b)
+    other_values = lax.ppermute(values, "core", [(0, 1), (1, 0)])
+    summed = call(project_out, shape((runs // 2, run, TOK)), [VMEM] * 4)(
+        values, other_values, out_mine, out_theirs
+    )
     summed, late = lax.optimization_barrier((summed, packed[6:]))
     parts = exchange(summed, ZX)
     moved += [flipped(x, i + 6) for i, x in enumerate(late)]
@@ -396,16 +414,16 @@
     partial_sums = call(
         functools.partial(project_up, run, sub),
         shape((far_count, 4 * sub + 16, slots)),
-        [SMEM] + [VMEM] * 3,
-    )(place, inputs, weights_in, keep)
+        [VMEM] * 3,
+    )(inputs, weights_in, keep)
     acts = call(functools.partial(activate, sub), shape((far_count, 2 * sub, slots)), [VMEM] * 2)(
         exchange(partial_sums, FAR), pick_weight
     )
     outputs = call(
         functools.partial(project_down, sub),
         shape((near_count, run, slots)),
-        [SMEM] + [VMEM] * 3,
-    )(place, exchange(acts, FAR), keep, weights_back)
+        [VMEM] * 3,
+    )(exchange(acts, FAR), keep, weights_back)
     returned = call(finish_rows, shape((slots, TOK)), [VMEM])(exchange(outputs, NEAR))
     returned = exchange(returned.reshape(ctx_count, SLOT, TOK), CTX).reshape(slots, TOK)
     out = call(combine, shape((run, block_rows)), [VMEM] * 3)(returned, places, hidden)

time: 187 us -> 186 us (level)
  waiting for transfers between devices: 26.2 us -> 21.5 us
  starting transfers between devices: 53.9 us -> 56.6 us
    unnamed x39 -> x52, local copies, waits for them, and re-layouts: 7.46 us -> 12.3 us
    ppermute x7, waiting for transfers between devices: 10.7 us -> 6.33 us  [flipped(): return lax.ppermute(x, NEAR, [(a, a ^ flip) for a in range(near_count)])]
    ppermute x1 -> x2, starting transfers between devices: 2.39 us -> 4.94 us  [the longest x1 2.52 us: on_device(): out_theirs = lax.ppermute(out_theirs, 'core', [(0, 1), (1, 0)])]
    select_n x0 -> x1, other arithmetic: none -> 2.26 us  [on_device(): out_theirs = jnp.where(flip, out_weights[:, 0], out_weights[:, 1])]
    pallas_call x2 -> x5, Pallas kernels: 5.12 us -> 7.11 us  [the longest x1 2.27 us: on_device(): call(pack, [shape(block)] * near_count, [VMEM] * 3, [pltpu.VMEM((near_cou...]
  transfers between devices with their start and end apart: 12 -> 13, of which waited for: 6 -> 5; matrix products, arithmetic and copies ran while one was open for 4% -> 4% of each run, Pallas kernels for 3% -> 3%
where the time goes in v5:
time: 186 us; the launch traced here: 185 us
  blocking collectives  77.2 us (42%)
  starting transfers between devices  56.6 us (30%)
  waiting for transfers between devices  21.5 us (12%)
  Pallas kernels  13.5 us (7%)
  local copies, waits for them, and re-layouts  13.4 us (7%)
  other arithmetic  2.45 us (1%)
    all_to_all x5, blocking collectives, exchange(): return lax.all_to_all(x, axes, split_axis=0, concat_axis=0, tiled=True)  77.2 us
    all_to_all x3, starting transfers between devices, exchange(): return lax.all_to_all(x, axes, split_axis=0, concat_axis=0, tiled=True)  28.1 us
    ppermute x7, starting transfers between devices, flipped(): return lax.ppermute(x, NEAR, [(a, a ^ flip) for a in range(near_count)])  21.2 us
    unnamed x52, local copies, waits for them, and re-layouts  12.3 us
    all_to_all x3, waiting for transfers between devices, exchange(): return lax.all_to_all(x, axes, split_axis=0, concat_axis=0, tiled=True)  11.8 us
    ppermute x7, waiting for transfers between devices, flipped(): return lax.ppermute(x, NEAR, [(a, a ^ flip) for a in range(near_count)])  6.33 us
  transfers between devices with their start and end apart: 13, of which 5 were waited for; matrix products, arithmetic and copies ran while one was open for 4% of the time, Pallas kernels for 3%

profile of v5, /device:TPU:1, one launch (start us, length us, event | category | flops | bytes accessed | tf_op | source)
XLA Modules:
  0.0 185.0 jit_solution(6099286357174403116)
XLA Ops:
  2.1 10.4 %all-to-all-start = ((bf16[16,288,128]{2,1,0:T(8,128)(2,1)}), bf16[16,288,128]{2,1,0:T(8,128)(2,1)S(1)}, u32[]{:S(2)}, u32[]{:S(2)}) async-start(bf16[16,288,128]{2,1,0:T(8,128)(2,1)} %shard_map.127), calls=%async_computation | async-start | bytes 2359296 | tf_op jit(solution)/shard_map/all_to_all | solution.py:285
  13.6 2.3 %shard_map.129 = (bf16[3,80,576]{2,1,0:T(8,128)(2,1)S(1)}, bf16[3,80,576]{2,1,0:T(8,128)(2,1)}, bf16[3,80,576]{2,1,0:T(8,128)(2,1)}, bf16[3,80,576]{2,1,0:T(8,12...) custom-call(bf16[6,80,768]{2,1,0:T(8,128)(2,1)S(1)} %copy-done, ...), custom_call_target="tpu_custom_call" | custom-call | tf_op jit(solution)/shard_map/pallas_call | solution.py:329
  17.3 2.9 %collective-permute-start.1 = (bf16[3,80,576]{2,1,0:T(8,128)(2,1)}, bf16[3,80,576]{2,1,0:T(8,128)(2,1)S(1)}, u32[]{:S(2)}, u32[]{:S(2)}) collective-permute-start(bf16[3,80,576]{2,1,0:T(8,128)(2,1)} %get-tuple-element.58), channel_id=1, source_target_pairs={{0,1},{1,0},{2,3},{3,2},{4,5},{5,4},{6,7},{7,6},{8,9},{9,8},{10,11... | collective-permute-start | bytes 829448 | tf_op jit(solution)/shard_map/ppermute | solution.py:337
  20.2 2.2 %collective-permute-start.2 = (bf16[3,80,576]{2,1,0:T(8,128)(2,1)}, bf16[3,80,576]{2,1,0:T(8,128)(2,1)}, u32[]{:S(2)}, u32[]{:S(2)}) collective-permute-start(bf16[3,80,576]{2,1,0:T(8,128)(2,1)} %get-tuple-element.59), channel_id=1, source_target_pairs={{0,2},{1,3},{2,0},{3,1},{4,6},{5,7},{6,4},{7,5},{8,10},{9,11},{10,... | collective-permute-start | bytes 829448 | tf_op jit(solution)/shard_map/ppermute | solution.py:337
  22.4 3.2 %collective-permute-start.3 = (bf16[3,80,576]{2,1,0:T(8,128)(2,1)}, bf16[3,80,576]{2,1,0:T(8,128)(2,1)}, u32[]{:S(2)}, u32[]{:S(2)}) collective-permute-start(bf16[3,80,576]{2,1,0:T(8,128)(2,1)} %get-tuple-element.60), channel_id=1, source_target_pairs={{0,3},{1,2},{2,1},{3,0},{4,7},{5,6},{6,5},{7,4},{8,11},{9,10},{10,... | collective-permute-start | bytes 829448 | tf_op jit(solution)/shard_map/ppermute | solution.py:337
  25.7 4.0 %collective-permute-start.4 = (bf16[3,80,576]{2,1,0:T(8,128)(2,1)}, bf16[3,80,576]{2,1,0:T(8,128)(2,1)}, u32[]{:S(2)}, u32[]{:S(2)}) collective-permute-start(bf16[3,80,576]{2,1,0:T(8,128)(2,1)} %get-tuple-element.61), channel_id=1, source_target_pairs={{0,4},{1,5},{2,6},{3,7},{4,0},{5,1},{6,2},{7,3},{8,12},{9,13},{10,... | collective-permute-start | bytes 829448 | tf_op jit(solution)/shard_map/ppermute | solution.py:337
  29.7 2.4 %copy.17 = bf16[256,2560]{0,1:T(8,128)(2,1)} copy(bf16[256,2560]{1,0:T(8,128)(2,1)} %param.17) | data formatting | bytes 2621440 | tf_op args[4]
  32.1 2.3 %select_bitcast_fusion = (bf16[16,80,256]{2,1,0:T(8,128)(2,1)}, bf16[16,80,256]{2,1,0:T(8,128)(2,1)S(1)}) fusion(pred[]{:T(512)S(6)} %eq.3, bf16[16,2,80,256]{3,2,1,0:T(8,128)(2,1)} %bitcast.44), kind=kLoop, calls=%fused_computation.2 | loop fusion | flops 655360 | bytes 2621441 | tf_op jit(solution)/shard_map/jit(_where)/select_n | solution.py:351
  34.4 2.5 %collective-permute-start = (bf16[16,80,256]{2,1,0:T(8,128)(2,1)}, bf16[16,80,256]{2,1,0:T(8,128)(2,1)S(1)}, u32[]{:S(2)}, u32[]{:S(2)}) collective-permute-start(bf16[16,80,256]{2,1,0:T(8,128)(2,1)} %get-tuple-element.103), channel_id=1, source_target_pairs={{0,1},{1,0},{2,3},{3,2},{4,5},{5,4},{6,7},{7,6},{8,9},{9,8},{10,11... | collective-permute-start | bytes 1966088 | tf_op jit(solution)/shard_map/ppermute | solution.py:352
  42.0 6.3 %collective-permute-done.3.refs_3_ = bf16[3,80,576]{2,1,0:T(8,128)(2,1)} collective-permute-done((bf16[3,80,576]{2,1,0:T(8,128)(2,1)}, bf16[3,80,576]{2,1,0:T(8,128)(2,1)}, u32[]{:S(2)}, u32[]{:S(2)}) %collective-permute-start.3) | collective-permute-done | bytes 276512 | tf_op jit(solution)/shard_map/ppermute | solution.py:337
  48.4 2.3 %collective-permute-start.6 = (bf16[16,288,128]{2,1,0:T(8,128)(2,1)S(1)}, bf16[16,288,128]{2,1,0:T(8,128)(2,1)S(1)}, u32[]{:S(2)}, u32[]{:S(2)}) collective-permute-start(bf16[16,288,128]{2,1,0:T(8,128)(2,1)S(1)} %all-to-all-done.ka), channel_id=1, source_target_pairs={{0,1},{1,0},{2,3},{3,2},{4,5},{5,4},{6,7},{7,6},{8,9},{9,8},{10,11... | collective-permute-start | bytes 3538952 | tf_op jit(solution)/shard_map/ppermute | solution.py:366
  50.6 2.5 %collective-permute-done.6.kb = bf16[16,288,128]{2,1,0:T(8,128)(2,1)S(1)} collective-permute-done((bf16[16,288,128]{2,1,0:T(8,128)(2,1)S(1)}, bf16[16,288,128]{2,1,0:T(8,128)(2,1)S(1)}, u32[]{:S(2)}, u32[]{:S(2)}) %collective-permute-start.6) | collective-permute-done | bytes 1179680 | tf_op jit(solution)/shard_map/ppermute | solution.py:366
  55.1 2.4 %collective-permute-start.7 = (bf16[256,128]{1,0:T(8,128)(2,1)S(1)}, bf16[256,128]{1,0:T(8,128)(2,1)S(1)}, u32[]{:S(2)}, u32[]{:S(2)}) collective-permute-start(bf16[256,128]{1,0:T(8,128)(2,1)S(1)} %shard_map.130.mine), channel_id=1, source_target_pairs={{0,1},{1,0},{2,3},{3,2},{4,5},{5,4},{6,7},{7,6},{8,9},{9,8},{10,11... | collective-permute-start | bytes 196616 | tf_op jit(solution)/shard_map/ppermute | solution.py:379
  59.7 10.4 %all-to-all-start.1 = ((bf16[16,80,128]{2,1,0:T(8,128)(2,1)}), bf16[16,80,128]{2,1,0:T(8,128)(2,1)S(1)}, u32[]{:S(2)}, u32[]{:S(2)}) async-start(bf16[16,80,128]{2,1,0:T(8,128)(2,1)} %shard_map.131), calls=%async_computation.1 | async-start | bytes 655360 | tf_op jit(solution)/shard_map/all_to_all | solution.py:285
  70.1 4.2 %collective-permute-start.8 = (bf16[3,80,576]{2,1,0:T(8,128)(2,1)}, bf16[3,80,576]{2,1,0:T(8,128)(2,1)S(1)}, u32[]{:S(2)}, u32[]{:S(2)}) collective-permute-start(bf16[3,80,576]{2,1,0:T(8,128)(2,1)} %get-tuple-element.87), channel_id=1, source_target_pairs={{0,6},{1,7},{2,4},{3,5},{4,2},{5,3},{6,0},{7,1},{8,14},{9,15},{10,... | collective-permute-start | bytes 829448 | tf_op jit(solution)/shard_map/ppermute | solution.py:337
  74.3 2.8 %collective-permute-start.9 = (bf16[3,80,576]{2,1,0:T(8,128)(2,1)S(1)}, bf16[3,80,576]{2,1,0:T(8,128)(2,1)S(1)}, u32[]{:S(2)}, u32[]{:S(2)}) collective-permute-start(bf16[3,80,576]{2,1,0:T(8,128)(2,1)S(1)} %copy-done.21), channel_id=1, source_target_pairs={{0,7},{1,6},{2,5},{3,4},{4,3},{5,2},{6,1},{7,0},{8,15},{9,14},{10,... | collective-permute-start | bytes 829448 | tf_op jit(solution)/shard_map/ppermute | solution.py:337
  77.2 5.7 %all-to-all-done.1.parts = bf16[16,80,128]{2,1,0:T(8,128)(2,1)S(1)} async-done(((bf16[16,80,128]{2,1,0:T(8,128)(2,1)}), bf16[16,80,128]{2,1,0:T(8,128)(2,1)S(1)}, u32[]{:S(2)}, u32[]{:S(2)}) %all-to-all-start.1) | async-done | bytes 327712 | tf_op jit(solution)/shard_map/all_to_all | solution.py:285
  83.8 21.1 %all_to_all.40 = bf16[16,32,128]{2,1,0:T(8,128)(2,1)S(1)} all-to-all(bf16[16,32,128]{2,1,0:T(8,128)(2,1)S(1)} %bitcast.40), channel_id=1, replica_groups=mesh['y'=8,'xh'=2,'za'=4,'zb'=2,'xl'=2,'core'=2] {'y','xh'}, dimensions={0} | all-to-all | bytes 262144 | tf_op jit(solution)/shard_map/all_to_all | solution.py:285
  107.4 7.3 %all-to-all-start.3 = ((bf16[8,96,512]{2,1,0:T(8,128)(2,1)}), bf16[8,96,512]{2,1,0:T(8,128)(2,1)S(1)}, u32[]{:S(2)}, u32[]{:S(2)}) async-start(bf16[8,96,512]{2,1,0:T(8,128)(2,1)} %get-tuple-element.89), calls=%async_computation.3 | async-start | bytes 1572864 | tf_op jit(solution)/shard_map/all_to_all | solution.py:285
  119.4 6.1 %all-to-all-done.3.inputs = bf16[8,96,512]{2,1,0:T(8,128)(2,1)S(1)} async-done(((bf16[8,96,512]{2,1,0:T(8,128)(2,1)}), bf16[8,96,512]{2,1,0:T(8,128)(2,1)S(1)}, u32[]{:S(2)}, u32[]{:S(2)}) %all-to-all-start.3) | async-done | bytes 786464 | tf_op jit(solution)/shard_map/all_to_all | solution.py:285
  126.7 16.0 %all_to_all.41.got = bf16[4,112,512]{2,1,0:T(8,128)(2,1)S(1)} all-to-all(bf16[4,112,512]{2,1,0:T(8,128)(2,1)S(1)} %shard_map.135), channel_id=1, replica_groups=mesh['y'=8,'xh'=2,'za'=4,'zb'=2,'xl'=2,'core'=2] {'za'}, dimensions={0} | all-to-all | bytes 917504 | tf_op jit(solution)/shard_map/all_to_all | solution.py:285
  142.9 11.9 %all_to_all.42.acts = bf16[4,48,512]{2,1,0:T(8,128)(2,1)S(1)} all-to-all(bf16[4,48,512]{2,1,0:T(8,128)(2,1)S(1)} %shard_map.136), channel_id=1, replica_groups=mesh['y'=8,'xh'=2,'za'=4,'zb'=2,'xl'=2,'core'=2] {'za'}, dimensions={0} | all-to-all | bytes 393216 | tf_op jit(solution)/shard_map/all_to_all | solution.py:285
  156.0 15.4 %all_to_all.43.got = bf16[8,80,512]{2,1,0:T(8,128)(2,1)S(1)} all-to-all(bf16[8,80,512]{2,1,0:T(8,128)(2,1)S(1)} %shard_map.137), channel_id=1, replica_groups=mesh['y'=8,'xh'=2,'za'=4,'zb'=2,'xl'=2,'core'=2] {'zb','xl','core'}, dimensions={0} | all-to-all | bytes 1310720 | tf_op jit(solution)/shard_map/all_to_all | solution.py:285
  171.6 12.6 %all_to_all.44 = bf16[16,32,128]{2,1,0:T(8,128)(2,1)S(1)} all-to-all(bf16[16,32,128]{2,1,0:T(8,128)(2,1)S(1)} %bitcast.38), channel_id=1, replica_groups=mesh['y'=8,'xh'=2,'za'=4,'zb'=2,'xl'=2,'core'=2] {'y','xh'}, dimensions={0} | all-to-all | bytes 262144 | tf_op jit(solution)/shard_map/all_to_all | solution.py:285
  (81 shorter events, 25.3 us)
Async XLA Ops:
  2.1 10.4 %copy-start.17 = (s32[120,3,2]{0,2,1:T(2,128)S(1)}, s32[120,3,2]{0,2,1:T(2,128)}, u32[]{:S(2)}) copy-start(s32[120,3,2]{0,2,1:T(2,128)} %param.21) | copy-start | bytes 8644
  2.1 10.4 %copy-start.18 = (s32[120,3]{0,1:T(4,128)S(1)}, s32[120,3]{0,1:T(4,128)}, u32[]{:S(2)}) copy-start(s32[120,3]{0,1:T(4,128)} %param.20) | copy-start | bytes 4324
  2.1 10.4 %copy-start.19 = (bf16[120,3,2]{0,2,1:T(2,128)(2,1)S(1)}, bf16[120,3,2]{0,2,1:T(2,128)(2,1)}, u32[]{:S(2)}) copy-start(bf16[120,3,2]{0,2,1:T(2,128)(2,1)} %param.22) | copy-start | bytes 4324
  2.1 11.5 %copy-start = (bf16[6,80,768]{2,1,0:T(8,128)(2,1)S(1)}, bf16[6,80,768]{2,1,0:T(8,128)(2,1)}, u32[]{:S(2)}) copy-start(bf16[6,80,768]{2,1,0:T(8,128)(2,1)} %gate) | copy-start | bytes 2211844
  2.1 11.5 %copy-start.1 = (bf16[6,80,768]{2,1,0:T(8,128)(2,1)S(1)}, bf16[6,80,768]{2,1,0:T(8,128)(2,1)}, u32[]{:S(2)}) copy-start(bf16[6,80,768]{2,1,0:T(8,128)(2,1)} %up.1) | copy-start | bytes 2211844
  2.1 11.5 %copy-start.2 = (bf16[6,768,80]{1,2,0:T(8,128)(2,1)S(1)}, bf16[6,768,80]{1,2,0:T(8,128)(2,1)}, u32[]{:S(2)}) copy-start(bf16[6,768,80]{1,2,0:T(8,128)(2,1)} %param.25) | copy-start | bytes 2211844
  2.1 46.2 %all-to-all-start = ((bf16[16,288,128]{2,1,0:T(8,128)(2,1)}), bf16[16,288,128]{2,1,0:T(8,128)(2,1)S(1)}, u32[]{:S(2)}, u32[]{:S(2)}) async-start(bf16[16,288,128]{2,1,0:T(8,128)(2,1)} %shard_map.127), calls=%async_computation | async-start | bytes 2359296 | tf_op jit(solution)/shard_map/all_to_all | solution.py:285
  17.3 19.7 %collective-permute-start.1 = (bf16[3,80,576]{2,1,0:T(8,128)(2,1)}, bf16[3,80,576]{2,1,0:T(8,128)(2,1)S(1)}, u32[]{:S(2)}, u32[]{:S(2)}) collective-permute-start(bf16[3,80,576]{2,1,0:T(8,128)(2,1)} %get-tuple-element.58), channel_id=1, source_target_pairs={{0,1},{1,0},{2,3},{3,2},{4,5},{5,4},{6,7},{7,6},{8,9},{9,8},{10,11... | collective-permute-start | bytes 829448 | tf_op jit(solution)/shard_map/ppermute | solution.py:337
  20.2 21.8 %collective-permute-start.2 = (bf16[3,80,576]{2,1,0:T(8,128)(2,1)}, bf16[3,80,576]{2,1,0:T(8,128)(2,1)}, u32[]{:S(2)}, u32[]{:S(2)}) collective-permute-start(bf16[3,80,576]{2,1,0:T(8,128)(2,1)} %get-tuple-element.59), channel_id=1, source_target_pairs={{0,2},{1,3},{2,0},{3,1},{4,6},{5,7},{6,4},{7,5},{8,10},{9,11},{10,... | collective-permute-start | bytes 829448 | tf_op jit(solution)/shard_map/ppermute | solution.py:337
  22.4 25.9 %collective-permute-start.3 = (bf16[3,80,576]{2,1,0:T(8,128)(2,1)}, bf16[3,80,576]{2,1,0:T(8,128)(2,1)}, u32[]{:S(2)}, u32[]{:S(2)}) collective-permute-start(bf16[3,80,576]{2,1,0:T(8,128)(2,1)} %get-tuple-element.60), channel_id=1, source_target_pairs={{0,3},{1,2},{2,1},{3,0},{4,7},{5,6},{6,5},{7,4},{8,11},{9,10},{10,... | collective-permute-start | bytes 829448 | tf_op jit(solution)/shard_map/ppermute | solution.py:337
  25.7 22.7 %collective-permute-start.4 = (bf16[3,80,576]{2,1,0:T(8,128)(2,1)}, bf16[3,80,576]{2,1,0:T(8,128)(2,1)}, u32[]{:S(2)}, u32[]{:S(2)}) collective-permute-start(bf16[3,80,576]{2,1,0:T(8,128)(2,1)} %get-tuple-element.61), channel_id=1, source_target_pairs={{0,4},{1,5},{2,6},{3,7},{4,0},{5,1},{6,2},{7,3},{8,12},{9,13},{10,... | collective-permute-start | bytes 829448 | tf_op jit(solution)/shard_map/ppermute | solution.py:337
  34.4 14.0 %collective-permute-start = (bf16[16,80,256]{2,1,0:T(8,128)(2,1)}, bf16[16,80,256]{2,1,0:T(8,128)(2,1)S(1)}, u32[]{:S(2)}, u32[]{:S(2)}) collective-permute-start(bf16[16,80,256]{2,1,0:T(8,128)(2,1)} %get-tuple-element.103), channel_id=1, source_target_pairs={{0,1},{1,0},{2,3},{3,2},{4,5},{5,4},{6,7},{7,6},{8,9},{9,8},{10,11... | collective-permute-start | bytes 1966088 | tf_op jit(solution)/shard_map/ppermute | solution.py:352
  36.9 16.2 %copy-start.16 = (s32[16,16]{1,0:T(8,128)S(1)}, s32[16,16]{1,0:T(8,128)}, u32[]{:S(2)}) copy-start(s32[16,16]{1,0:T(8,128)} %mask.1) | copy-start | bytes 3076
  37.0 11.3 %collective-permute-start.5 = (bf16[3,80,576]{2,1,0:T(8,128)(2,1)}, bf16[3,80,576]{2,1,0:T(8,128)(2,1)}, u32[]{:S(2)}, u32[]{:S(2)}) collective-permute-start(bf16[3,80,576]{2,1,0:T(8,128)(2,1)} %get-tuple-element.62), channel_id=1, source_target_pairs={{0,5},{1,4},{2,7},{3,6},{4,1},{5,0},{6,3},{7,2},{8,13},{9,12},{10,... | collective-permute-start | bytes 829448 | tf_op jit(solution)/shard_map/ppermute | solution.py:337
  48.4 4.7 %collective-permute-start.6 = (bf16[16,288,128]{2,1,0:T(8,128)(2,1)S(1)}, bf16[16,288,128]{2,1,0:T(8,128)(2,1)S(1)}, u32[]{:S(2)}, u32[]{:S(2)}) collective-permute-start(bf16[16,288,128]{2,1,0:T(8,128)(2,1)S(1)} %all-to-all-done.ka), channel_id=1, source_target_pairs={{0,1},{1,0},{2,3},{3,2},{4,5},{5,4},{6,7},{7,6},{8,9},{9,8},{10,11... | collective-permute-start | bytes 3538952 | tf_op jit(solution)/shard_map/ppermute | solution.py:366
  55.1 19.2 %copy-start.21 = (bf16[3,80,576]{2,1,0:T(8,128)(2,1)S(1)}, bf16[3,80,576]{2,1,0:T(8,128)(2,1)}, u32[]{:S(2)}) copy-start(bf16[3,80,576]{2,1,0:T(8,128)(2,1)} %copy-done.20) | copy-start | bytes 829444
  55.1 27.8 %copy-start.13 = (bf16[512,128]{1,0:T(8,128)(2,1)S(1)}, bf16[512,128]{1,0:T(8,128)(2,1)}, u32[]{:S(2)}) copy-start(bf16[512,128]{1,0:T(8,128)(2,1)} %copy-done.12) | copy-start | bytes 393220
  55.1 3.3 %collective-permute-start.7 = (bf16[256,128]{1,0:T(8,128)(2,1)S(1)}, bf16[256,128]{1,0:T(8,128)(2,1)S(1)}, u32[]{:S(2)}, u32[]{:S(2)}) collective-permute-start(bf16[256,128]{1,0:T(8,128)(2,1)S(1)} %shard_map.130.mine), channel_id=1, source_target_pairs={{0,1},{1,0},{2,3},{3,2},{4,5},{5,4},{6,7},{7,6},{8,9},{9,8},{10,11... | collective-permute-start | bytes 196616 | tf_op jit(solution)/shard_map/ppermute | solution.py:379
  59.7 23.3 %all-to-all-start.1 = ((bf16[16,80,128]{2,1,0:T(8,128)(2,1)}), bf16[16,80,128]{2,1,0:T(8,128)(2,1)S(1)}, u32[]{:S(2)}, u32[]{:S(2)}) async-start(bf16[16,80,128]{2,1,0:T(8,128)(2,1)} %shard_map.131), calls=%async_computation.1 | async-start | bytes 655360 | tf_op jit(solution)/shard_map/all_to_all | solution.py:285
  70.1 35.8 %collective-permute-start.8 = (bf16[3,80,576]{2,1,0:T(8,128)(2,1)}, bf16[3,80,576]{2,1,0:T(8,128)(2,1)S(1)}, u32[]{:S(2)}, u32[]{:S(2)}) collective-permute-start(bf16[3,80,576]{2,1,0:T(8,128)(2,1)} %get-tuple-element.87), channel_id=1, source_target_pairs={{0,6},{1,7},{2,4},{3,5},{4,2},{5,3},{6,0},{7,1},{8,14},{9,15},{10,... | collective-permute-start | bytes 829448 | tf_op jit(solution)/shard_map/ppermute | solution.py:337
  74.3 32.4 %collective-permute-start.9 = (bf16[3,80,576]{2,1,0:T(8,128)(2,1)S(1)}, bf16[3,80,576]{2,1,0:T(8,128)(2,1)S(1)}, u32[]{:S(2)}, u32[]{:S(2)}) collective-permute-start(bf16[3,80,576]{2,1,0:T(8,128)(2,1)S(1)} %copy-done.21), channel_id=1, source_target_pairs={{0,7},{1,6},{2,5},{3,4},{4,3},{5,2},{6,1},{7,0},{8,15},{9,14},{10,... | collective-permute-start | bytes 829448 | tf_op jit(solution)/shard_map/ppermute | solution.py:337
  77.2 37.5 %copy-start.4 = (bf16[3,80,576]{2,1,0:T(8,128)(2,1)S(1)}, bf16[3,80,576]{2,1,0:T(8,128)(2,1)}, u32[]{:S(2)}) copy-start(bf16[3,80,576]{2,1,0:T(8,128)(2,1)} %copy-done.3) | copy-start | bytes 829444
  107.4 18.1 %all-to-all-start.3 = ((bf16[8,96,512]{2,1,0:T(8,128)(2,1)}), bf16[8,96,512]{2,1,0:T(8,128)(2,1)S(1)}, u32[]{:S(2)}, u32[]{:S(2)}) async-start(bf16[8,96,512]{2,1,0:T(8,128)(2,1)} %get-tuple-element.89), calls=%async_computation.3 | async-start | bytes 1572864 | tf_op jit(solution)/shard_map/all_to_all | solution.py:285
  156.0 28.2 %copy-start.15 = (bf16[80,128]{1,0:T(8,128)(2,1)S(1)}, bf16[80,128]{1,0:T(8,128)(2,1)}, u32[]{:S(2)}) copy-start(bf16[80,128]{1,0:T(8,128)(2,1)} %copy-done.14) | copy-start | bytes 61444
  (15 other events, 36.7 us)

commit v6 on v5

--- a/solution.py
+++ b/solution.py
@@ -215,8 +215,7 @@
     features = jnp.concatenate(
         [inputs[lax.axis_index(NEAR) ^ flip, :run, :] for flip in range(count)], axis=0
     )
-    ends = inputs[:, run : run + 16, :].astype(F32)
-    ends = jnp.sum(ends, axis=0)
+    ends = jnp.sum(inputs[...].astype(F32)[:, run:], axis=0)
     square = ends[0:1] + ends[1:2]
     unit = 2 * sub * out.shape[0]
     sums = [jnp.zeros((unit, slots), F32) for _ in range(2)]
@@ -224,7 +223,7 @@
         part = dot(weights[expert * unit : (expert + 1) * unit, :], features)
         for pick in range(2):
             sums[pick] = sums[pick] + keep[2 * expert + pick : 2 * expert + pick + 1, :] * part
-    tail = tail_rows(square, 16)
+    tail = tail_rows(square, 8)
     for dest in range(out.shape[0]):
         pieces = []
         for pick in range(2):
@@ -336,8 +335,7 @@
     def flipped(x, flip):
         return lax.ppermute(x, NEAR, [(a, a ^ flip) for a in range(near_count)])
 
-    early = {i: flipped(packed[i], i) for i in (2, 3, 4, 5, 1)}
-    moved = [packed[0]] + [early[i] for i in range(1, 6)]
+    moved = {i: flipped(packed[i], i) for i in (1, 2, 4, 5)}
 
     wide_q = jnp.pad(queries.transpose(1, 0, 2), ((0, 0), (0, pad_rows), (0, 0)))
     wide_q = wide_q.reshape(heads * TOK, key_width)
@@ -380,9 +378,11 @@
     summed = call(project_out, shape((runs // 2, run, TOK)), [VMEM] * 4)(
         values, other_values, out_mine, out_theirs
     )
-    summed, late = lax.optimization_barrier((summed, packed[6:]))
+    summed, *late = lax.optimization_barrier((summed, packed[3], packed[6], packed[7]))
     parts = exchange(summed, ZX)
-    moved += [flipped(x, i + 6) for i, x in enumerate(late)]
+    for flip, x in zip((3, 6, 7), late):
+        moved[flip] = flipped(x, flip)
+    moved = [packed[0]] + [moved[flip] for flip in range(1, near_count)]
 
     hidden, sent = call(make_rows, [shape((run, TOK)), shape((slots, TOK))], [VMEM] * 5)(
         parts,
@@ -393,9 +393,9 @@
     )
     got = exchange(sent.reshape(ctx_count, SLOT, TOK), CTX).reshape(slots, TOK)
     spread, keep, pick_weight = call(
-        functools.partial(spread_rows, run + 16, first_share),
+        functools.partial(spread_rows, run + 8, first_share),
         [
-            shape((near_count, run + 16, slots)),
+            shape((near_count, run + 8, slots)),
             shape((2 * local_experts, slots), F32),
             shape((2, slots), F32),
         ],
@@ -413,7 +413,7 @@
     )(*moved)
     partial_sums = call(
         functools.partial(project_up, run, sub),
-        shape((far_count, 4 * sub + 16, slots)),
+        shape((far_count, 4 * sub + 8, slots)),
         [VMEM] * 3,
     )(inputs, weights_in, keep)
     acts = call(functools.partial(activate, sub), shape((far_count, 2 * sub, slots)), [VMEM] * 2)(

time: 186 us -> 184 us (0.989)
  waiting for transfers between devices: 21.5 us -> 17.4 us
  starting transfers between devices: 56.6 us -> 59.8 us
    ppermute x1, starting transfers between devices: 2.29 us -> 6.49 us  [on_device(): keys_b = lax.ppermute(keys_a, 'core', [(0, 1), (1, 0)])]
    all_to_all x3, waiting for transfers between devices: 11.8 us -> 7.91 us  [exchange(): return lax.all_to_all(x, axes, split_axis=0, concat_axis=0, tiled=True)]
    unnamed x52 -> x50, local copies, waits for them, and re-layouts: 12.3 us -> 11.6 us
  transfers between devices with their start and end apart: 13 -> 13, of which waited for: 5 -> 6; matrix products, arithmetic and copies ran while one was open for 4% -> 2% of each run, Pallas kernels for 3% -> 3%
where the time goes in v6:
time: 184 us; the launch traced here: 182 us
  blocking collectives  78.5 us (43%)
  starting transfers between devices  59.8 us (32%)
  waiting for transfers between devices  17.4 us (9%)
  Pallas kernels  13.4 us (7%)
  local copies, waits for them, and re-layouts  11.8 us (6%)
    all_to_all x5, blocking collectives, exchange(): return lax.all_to_all(x, axes, split_axis=0, concat_axis=0, tiled=True)  78.5 us
    all_to_all x3, starting transfers between devices, exchange(): return lax.all_to_all(x, axes, split_axis=0, concat_axis=0, tiled=True)  27.2 us
    ppermute x7, starting transfers between devices, flipped(): return lax.ppermute(x, NEAR, [(a, a ^ flip) for a in range(near_count)])  21.3 us
    unnamed x50, local copies, waits for them, and re-layouts  11.6 us
    all_to_all x3, waiting for transfers between devices, exchange(): return lax.all_to_all(x, axes, split_axis=0, concat_axis=0, tiled=True)  7.91 us
    ppermute x1, starting transfers between devices, on_device(): keys_b = lax.ppermute(keys_a, 'core', [(0, 1), (1, 0)])  6.49 us
    ppermute x7, waiting for transfers between devices, flipped(): return lax.ppermute(x, NEAR, [(a, a ^ flip) for a in range(near_count)])  6.13 us
  transfers between devices with their start and end apart: 13, of which 6 were waited for; matrix products, arithmetic and copies ran while one was open for 2% of the time, Pallas kernels for 3%

profile of v6, /device:TPU:1, one launch (start us, length us, event | category | flops | bytes accessed | tf_op | source)
XLA Modules:
  0.0 182.4 jit_solution(14315931773173795511)
XLA Ops:
  2.2 10.4 %all-to-all-start = ((bf16[16,288,128]{2,1,0:T(8,128)(2,1)}), bf16[16,288,128]{2,1,0:T(8,128)(2,1)S(1)}, u32[]{:S(2)}, u32[]{:S(2)}) async-start(bf16[16,288,128]{2,1,0:T(8,128)(2,1)} %shard_map.127), calls=%async_computation | async-start | bytes 2359296 | tf_op jit(solution)/shard_map/all_to_all | solution.py:284
  13.6 2.2 %shard_map.129 = (bf16[3,80,576]{2,1,0:T(8,128)(2,1)S(1)}, bf16[3,80,576]{2,1,0:T(8,128)(2,1)}, bf16[3,80,576]{2,1,0:T(8,128)(2,1)}, bf16[3,80,576]{2,1,0:T(8,12...) custom-call(bf16[6,80,768]{2,1,0:T(8,128)(2,1)S(1)} %copy-done, ...), custom_call_target="tpu_custom_call" | custom-call | tf_op jit(solution)/shard_map/pallas_call | solution.py:328
  18.0 2.9 %collective-permute-start.1 = (bf16[3,80,576]{2,1,0:T(8,128)(2,1)}, bf16[3,80,576]{2,1,0:T(8,128)(2,1)}, u32[]{:S(2)}, u32[]{:S(2)}) collective-permute-start(bf16[3,80,576]{2,1,0:T(8,128)(2,1)} %get-tuple-element.56), channel_id=1, source_target_pairs={{0,1},{1,0},{2,3},{3,2},{4,5},{5,4},{6,7},{7,6},{8,9},{9,8},{10,11... | collective-permute-start | bytes 829448 | tf_op jit(solution)/shard_map/ppermute | solution.py:336
  20.8 2.2 %collective-permute-start.2 = (bf16[3,80,576]{2,1,0:T(8,128)(2,1)}, bf16[3,80,576]{2,1,0:T(8,128)(2,1)}, u32[]{:S(2)}, u32[]{:S(2)}) collective-permute-start(bf16[3,80,576]{2,1,0:T(8,128)(2,1)} %get-tuple-element.57), channel_id=1, source_target_pairs={{0,2},{1,3},{2,0},{3,1},{4,6},{5,7},{6,4},{7,5},{8,10},{9,11},{10,... | collective-permute-start | bytes 829448 | tf_op jit(solution)/shard_map/ppermute | solution.py:336
  23.0 4.0 %collective-permute-start.3 = (bf16[3,80,576]{2,1,0:T(8,128)(2,1)}, bf16[3,80,576]{2,1,0:T(8,128)(2,1)}, u32[]{:S(2)}, u32[]{:S(2)}) collective-permute-start(bf16[3,80,576]{2,1,0:T(8,128)(2,1)} %get-tuple-element.58), channel_id=1, source_target_pairs={{0,4},{1,5},{2,6},{3,7},{4,0},{5,1},{6,2},{7,3},{8,12},{9,13},{10,... | collective-permute-start | bytes 829448 | tf_op jit(solution)/shard_map/ppermute | solution.py:336
  27.1 2.1 %collective-permute-start.4 = (bf16[3,80,576]{2,1,0:T(8,128)(2,1)}, bf16[3,80,576]{2,1,0:T(8,128)(2,1)}, u32[]{:S(2)}, u32[]{:S(2)}) collective-permute-start(bf16[3,80,576]{2,1,0:T(8,128)(2,1)} %get-tuple-element.59), channel_id=1, source_target_pairs={{0,5},{1,4},{2,7},{3,6},{4,1},{5,0},{6,3},{7,2},{8,13},{9,12},{10,... | collective-permute-start | bytes 829448 | tf_op jit(solution)/shard_map/ppermute | solution.py:336
  31.7 2.4 %collective-permute-start = (bf16[16,80,256]{2,1,0:T(8,128)(2,1)}, bf16[16,80,256]{2,1,0:T(8,128)(2,1)S(1)}, u32[]{:S(2)}, u32[]{:S(2)}) collective-permute-start(bf16[16,80,256]{2,1,0:T(8,128)(2,1)} %get-tuple-element.101), channel_id=1, source_target_pairs={{0,1},{1,0},{2,3},{3,2},{4,5},{5,4},{6,7},{7,6},{8,9},{9,8},{10,11... | collective-permute-start | bytes 1966088 | tf_op jit(solution)/shard_map/ppermute | solution.py:350
  35.7 3.5 %collective-permute-done.2.refs_2_ = bf16[3,80,576]{2,1,0:T(8,128)(2,1)} collective-permute-done((bf16[3,80,576]{2,1,0:T(8,128)(2,1)}, bf16[3,80,576]{2,1,0:T(8,128)(2,1)}, u32[]{:S(2)}, u32[]{:S(2)}) %collective-permute-start.2) | collective-permute-done | bytes 276512 | tf_op jit(solution)/shard_map/ppermute | solution.py:336
  39.1 2.6 %collective-permute-done.4.refs_5_ = bf16[3,80,576]{2,1,0:T(8,128)(2,1)} collective-permute-done((bf16[3,80,576]{2,1,0:T(8,128)(2,1)}, bf16[3,80,576]{2,1,0:T(8,128)(2,1)}, u32[]{:S(2)}, u32[]{:S(2)}) %collective-permute-start.4) | collective-permute-done | bytes 276512 | tf_op jit(solution)/shard_map/ppermute | solution.py:336
  41.8 6.5 %collective-permute-start.5 = (bf16[16,288,128]{2,1,0:T(8,128)(2,1)S(1)}, bf16[16,288,128]{2,1,0:T(8,128)(2,1)S(1)}, u32[]{:S(2)}, u32[]{:S(2)}) collective-permute-start(bf16[16,288,128]{2,1,0:T(8,128)(2,1)S(1)} %all-to-all-done.ka), channel_id=1, source_target_pairs={{0,1},{1,0},{2,3},{3,2},{4,5},{5,4},{6,7},{7,6},{8,9},{9,8},{10,11... | collective-permute-start | bytes 3538952 | tf_op jit(solution)/shard_map/ppermute | solution.py:364
  48.3 2.5 %collective-permute-done.5.kb = bf16[16,288,128]{2,1,0:T(8,128)(2,1)S(1)} collective-permute-done((bf16[16,288,128]{2,1,0:T(8,128)(2,1)S(1)}, bf16[16,288,128]{2,1,0:T(8,128)(2,1)S(1)}, u32[]{:S(2)}, u32[]{:S(2)}) %collective-permute-start.5) | collective-permute-done | bytes 1179680 | tf_op jit(solution)/shard_map/ppermute | solution.py:364
  52.8 2.4 %collective-permute-start.6 = (bf16[256,128]{1,0:T(8,128)(2,1)S(1)}, bf16[256,128]{1,0:T(8,128)(2,1)S(1)}, u32[]{:S(2)}, u32[]{:S(2)}) collective-permute-start(bf16[256,128]{1,0:T(8,128)(2,1)S(1)} %shard_map.130.mine), channel_id=1, source_target_pairs={{0,1},{1,0},{2,3},{3,2},{4,5},{5,4},{6,7},{7,6},{8,9},{9,8},{10,11... | collective-permute-start | bytes 196616 | tf_op jit(solution)/shard_map/ppermute | solution.py:377
  57.3 10.2 %all-to-all-start.1 = ((bf16[16,80,128]{2,1,0:T(8,128)(2,1)}), bf16[16,80,128]{2,1,0:T(8,128)(2,1)S(1)}, u32[]{:S(2)}, u32[]{:S(2)}) async-start(bf16[16,80,128]{2,1,0:T(8,128)(2,1)} %shard_map.131), calls=%async_computation.1 | async-start | bytes 655360 | tf_op jit(solution)/shard_map/all_to_all | solution.py:284
  67.5 4.2 %collective-permute-start.7 = (bf16[3,80,576]{2,1,0:T(8,128)(2,1)}, bf16[3,80,576]{2,1,0:T(8,128)(2,1)S(1)}, u32[]{:S(2)}, u32[]{:S(2)}) collective-permute-start(bf16[3,80,576]{2,1,0:T(8,128)(2,1)} %get-tuple-element.82), channel_id=1, source_target_pairs={{0,3},{1,2},{2,1},{3,0},{4,7},{5,6},{6,5},{7,4},{8,11},{9,10},{10,... | collective-permute-start | bytes 829448 | tf_op jit(solution)/shard_map/ppermute | solution.py:336
  71.7 3.1 %collective-permute-start.8 = (bf16[3,80,576]{2,1,0:T(8,128)(2,1)}, bf16[3,80,576]{2,1,0:T(8,128)(2,1)S(1)}, u32[]{:S(2)}, u32[]{:S(2)}) collective-permute-start(bf16[3,80,576]{2,1,0:T(8,128)(2,1)} %copy-done.20), channel_id=1, source_target_pairs={{0,6},{1,7},{2,4},{3,5},{4,2},{5,3},{6,0},{7,1},{8,14},{9,15},{10,... | collective-permute-start | bytes 829448 | tf_op jit(solution)/shard_map/ppermute | solution.py:336
  74.8 2.9 %collective-permute-start.9 = (bf16[3,80,576]{2,1,0:T(8,128)(2,1)S(1)}, bf16[3,80,576]{2,1,0:T(8,128)(2,1)S(1)}, u32[]{:S(2)}, u32[]{:S(2)}) collective-permute-start(bf16[3,80,576]{2,1,0:T(8,128)(2,1)S(1)} %copy-done.19), channel_id=1, source_target_pairs={{0,7},{1,6},{2,5},{3,4},{4,3},{5,2},{6,1},{7,0},{8,15},{9,14},{10,... | collective-permute-start | bytes 829448 | tf_op jit(solution)/shard_map/ppermute | solution.py:336
  77.8 2.5 %all-to-all-done.1.parts = bf16[16,80,128]{2,1,0:T(8,128)(2,1)S(1)} async-done(((bf16[16,80,128]{2,1,0:T(8,128)(2,1)}), bf16[16,80,128]{2,1,0:T(8,128)(2,1)S(1)}, u32[]{:S(2)}, u32[]{:S(2)}) %all-to-all-start.1) | async-done | bytes 327712 | tf_op jit(solution)/shard_map/all_to_all | solution.py:284
  80.5 18.6 %all_to_all.40 = bf16[16,32,128]{2,1,0:T(8,128)(2,1)S(1)} all-to-all(bf16[16,32,128]{2,1,0:T(8,128)(2,1)S(1)} %bitcast.40), channel_id=1, replica_groups=mesh['y'=8,'xh'=2,'za'=4,'zb'=2,'xl'=2,'core'=2] {'y','xh'}, dimensions={0} | all-to-all | bytes 262144 | tf_op jit(solution)/shard_map/all_to_all | solution.py:284
  102.2 6.7 %all-to-all-start.3 = ((bf16[8,88,512]{2,1,0:T(8,128)(2,1)}), bf16[8,88,512]{2,1,0:T(8,128)(2,1)S(1)}, u32[]{:S(2)}, u32[]{:S(2)}) async-start(bf16[8,88,512]{2,1,0:T(8,128)(2,1)} %get-tuple-element.87), calls=%async_computation.3 | async-start | bytes 1441792 | tf_op jit(solution)/shard_map/all_to_all | solution.py:284
  113.6 5.4 %all-to-all-done.3.inputs = bf16[8,88,512]{2,1,0:T(8,128)(2,1)S(1)} async-done(((bf16[8,88,512]{2,1,0:T(8,128)(2,1)}), bf16[8,88,512]{2,1,0:T(8,128)(2,1)S(1)}, u32[]{:S(2)}, u32[]{:S(2)}) %all-to-all-start.3) | async-done | bytes 720928 | tf_op jit(solution)/shard_map/all_to_all | solution.py:284
  120.2 14.8 %all_to_all.41.got = bf16[4,104,512]{2,1,0:T(8,128)(2,1)S(1)} all-to-all(bf16[4,104,512]{2,1,0:T(8,128)(2,1)S(1)} %shard_map.135), channel_id=1, replica_groups=mesh['y'=8,'xh'=2,'za'=4,'zb'=2,'xl'=2,'core'=2] {'za'}, dimensions={0} | all-to-all | bytes 851968 | tf_op jit(solution)/shard_map/all_to_all | solution.py:284
  135.1 12.5 %all_to_all.42.acts = bf16[4,48,512]{2,1,0:T(8,128)(2,1)S(1)} all-to-all(bf16[4,48,512]{2,1,0:T(8,128)(2,1)S(1)} %shard_map.136), channel_id=1, replica_groups=mesh['y'=8,'xh'=2,'za'=4,'zb'=2,'xl'=2,'core'=2] {'za'}, dimensions={0} | all-to-all | bytes 393216 | tf_op jit(solution)/shard_map/all_to_all | solution.py:284
  148.8 15.6 %all_to_all.43.got = bf16[8,80,512]{2,1,0:T(8,128)(2,1)S(1)} all-to-all(bf16[8,80,512]{2,1,0:T(8,128)(2,1)S(1)} %shard_map.137), channel_id=1, replica_groups=mesh['y'=8,'xh'=2,'za'=4,'zb'=2,'xl'=2,'core'=2] {'zb','xl','core'}, dimensions={0} | all-to-all | bytes 1310720 | tf_op jit(solution)/shard_map/all_to_all | solution.py:284
  164.6 17.0 %all_to_all.44 = bf16[16,32,128]{2,1,0:T(8,128)(2,1)S(1)} all-to-all(bf16[16,32,128]{2,1,0:T(8,128)(2,1)S(1)} %bitcast.38), channel_id=1, replica_groups=mesh['y'=8,'xh'=2,'za'=4,'zb'=2,'xl'=2,'core'=2] {'y','xh'}, dimensions={0} | all-to-all | bytes 262144 | tf_op jit(solution)/shard_map/all_to_all | solution.py:284
  (79 shorter events, 25.0 us)
Async XLA Ops:
  2.1 10.4 %copy-start.15 = (s32[120,3,2]{0,2,1:T(2,128)S(1)}, s32[120,3,2]{0,2,1:T(2,128)}, u32[]{:S(2)}) copy-start(s32[120,3,2]{0,2,1:T(2,128)} %param.21) | copy-start | bytes 8644
  2.1 10.4 %copy-start.16 = (s32[120,3]{0,1:T(4,128)S(1)}, s32[120,3]{0,1:T(4,128)}, u32[]{:S(2)}) copy-start(s32[120,3]{0,1:T(4,128)} %param.20) | copy-start | bytes 4324
  2.1 10.4 %copy-start.17 = (bf16[120,3,2]{0,2,1:T(2,128)(2,1)S(1)}, bf16[120,3,2]{0,2,1:T(2,128)(2,1)}, u32[]{:S(2)}) copy-start(bf16[120,3,2]{0,2,1:T(2,128)(2,1)} %param.22) | copy-start | bytes 4324
  2.1 11.5 %copy-start = (bf16[6,80,768]{2,1,0:T(8,128)(2,1)S(1)}, bf16[6,80,768]{2,1,0:T(8,128)(2,1)}, u32[]{:S(2)}) copy-start(bf16[6,80,768]{2,1,0:T(8,128)(2,1)} %gate) | copy-start | bytes 2211844
  2.1 11.5 %copy-start.1 = (bf16[6,80,768]{2,1,0:T(8,128)(2,1)S(1)}, bf16[6,80,768]{2,1,0:T(8,128)(2,1)}, u32[]{:S(2)}) copy-start(bf16[6,80,768]{2,1,0:T(8,128)(2,1)} %up.1) | copy-start | bytes 2211844
  2.1 11.5 %copy-start.2 = (bf16[6,768,80]{1,2,0:T(8,128)(2,1)S(1)}, bf16[6,768,80]{1,2,0:T(8,128)(2,1)}, u32[]{:S(2)}) copy-start(bf16[6,768,80]{1,2,0:T(8,128)(2,1)} %param.25) | copy-start | bytes 2211844
  2.2 39.6 %all-to-all-start = ((bf16[16,288,128]{2,1,0:T(8,128)(2,1)}), bf16[16,288,128]{2,1,0:T(8,128)(2,1)S(1)}, u32[]{:S(2)}, u32[]{:S(2)}) async-start(bf16[16,288,128]{2,1,0:T(8,128)(2,1)} %shard_map.127), calls=%async_computation | async-start | bytes 2359296 | tf_op jit(solution)/shard_map/all_to_all | solution.py:284
  18.0 17.7 %collective-permute-start.1 = (bf16[3,80,576]{2,1,0:T(8,128)(2,1)}, bf16[3,80,576]{2,1,0:T(8,128)(2,1)}, u32[]{:S(2)}, u32[]{:S(2)}) collective-permute-start(bf16[3,80,576]{2,1,0:T(8,128)(2,1)} %get-tuple-element.56), channel_id=1, source_target_pairs={{0,1},{1,0},{2,3},{3,2},{4,5},{5,4},{6,7},{7,6},{8,9},{9,8},{10,11... | collective-permute-start | bytes 829448 | tf_op jit(solution)/shard_map/ppermute | solution.py:336
  20.8 18.3 %collective-permute-start.2 = (bf16[3,80,576]{2,1,0:T(8,128)(2,1)}, bf16[3,80,576]{2,1,0:T(8,128)(2,1)}, u32[]{:S(2)}, u32[]{:S(2)}) collective-permute-start(bf16[3,80,576]{2,1,0:T(8,128)(2,1)} %get-tuple-element.57), channel_id=1, source_target_pairs={{0,2},{1,3},{2,0},{3,1},{4,6},{5,7},{6,4},{7,5},{8,10},{9,11},{10,... | collective-permute-start | bytes 829448 | tf_op jit(solution)/shard_map/ppermute | solution.py:336
  23.0 16.1 %collective-permute-start.3 = (bf16[3,80,576]{2,1,0:T(8,128)(2,1)}, bf16[3,80,576]{2,1,0:T(8,128)(2,1)}, u32[]{:S(2)}, u32[]{:S(2)}) collective-permute-start(bf16[3,80,576]{2,1,0:T(8,128)(2,1)} %get-tuple-element.58), channel_id=1, source_target_pairs={{0,4},{1,5},{2,6},{3,7},{4,0},{5,1},{6,2},{7,3},{8,12},{9,13},{10,... | collective-permute-start | bytes 829448 | tf_op jit(solution)/shard_map/ppermute | solution.py:336
  27.1 14.7 %collective-permute-start.4 = (bf16[3,80,576]{2,1,0:T(8,128)(2,1)}, bf16[3,80,576]{2,1,0:T(8,128)(2,1)}, u32[]{:S(2)}, u32[]{:S(2)}) collective-permute-start(bf16[3,80,576]{2,1,0:T(8,128)(2,1)} %get-tuple-element.59), channel_id=1, source_target_pairs={{0,5},{1,4},{2,7},{3,6},{4,1},{5,0},{6,3},{7,2},{8,13},{9,12},{10,... | collective-permute-start | bytes 829448 | tf_op jit(solution)/shard_map/ppermute | solution.py:336
  31.7 3.8 %copy-start.22 = (bf16[120,80]{0,1:T(8,128)(2,1)S(1)}, bf16[120,80]{0,1:T(8,128)(2,1)}, u32[]{:S(2)}) copy-start(bf16[120,80]{0,1:T(8,128)(2,1)} %param.18) | copy-start | bytes 57604
  31.7 10.0 %collective-permute-start = (bf16[16,80,256]{2,1,0:T(8,128)(2,1)}, bf16[16,80,256]{2,1,0:T(8,128)(2,1)S(1)}, u32[]{:S(2)}, u32[]{:S(2)}) collective-permute-start(bf16[16,80,256]{2,1,0:T(8,128)(2,1)} %get-tuple-element.101), channel_id=1, source_target_pairs={{0,1},{1,0},{2,3},{3,2},{4,5},{5,4},{6,7},{7,6},{8,9},{9,8},{10,11... | collective-permute-start | bytes 1966088 | tf_op jit(solution)/shard_map/ppermute | solution.py:350
  34.2 16.6 %copy-start.14 = (s32[16,16]{1,0:T(8,128)S(1)}, s32[16,16]{1,0:T(8,128)}, u32[]{:S(2)}) copy-start(s32[16,16]{1,0:T(8,128)} %mask.1) | copy-start | bytes 3076
  41.8 9.0 %collective-permute-start.5 = (bf16[16,288,128]{2,1,0:T(8,128)(2,1)S(1)}, bf16[16,288,128]{2,1,0:T(8,128)(2,1)S(1)}, u32[]{:S(2)}, u32[]{:S(2)}) collective-permute-start(bf16[16,288,128]{2,1,0:T(8,128)(2,1)S(1)} %all-to-all-done.ka), channel_id=1, source_target_pairs={{0,1},{1,0},{2,3},{3,2},{4,5},{5,4},{6,7},{7,6},{8,9},{9,8},{10,11... | collective-permute-start | bytes 3538952 | tf_op jit(solution)/shard_map/ppermute | solution.py:364
  52.8 22.0 %copy-start.19 = (bf16[3,80,576]{2,1,0:T(8,128)(2,1)S(1)}, bf16[3,80,576]{2,1,0:T(8,128)(2,1)}, u32[]{:S(2)}) copy-start(bf16[3,80,576]{2,1,0:T(8,128)(2,1)} %copy-done.18) | copy-start | bytes 829444
  52.8 27.5 %copy-start.13 = (bf16[512,128]{1,0:T(8,128)(2,1)S(1)}, bf16[512,128]{1,0:T(8,128)(2,1)}, u32[]{:S(2)}) copy-start(bf16[512,128]{1,0:T(8,128)(2,1)} %copy-done.12) | copy-start | bytes 393220
  52.8 3.3 %collective-permute-start.6 = (bf16[256,128]{1,0:T(8,128)(2,1)S(1)}, bf16[256,128]{1,0:T(8,128)(2,1)S(1)}, u32[]{:S(2)}, u32[]{:S(2)}) collective-permute-start(bf16[256,128]{1,0:T(8,128)(2,1)S(1)} %shard_map.130.mine), channel_id=1, source_target_pairs={{0,1},{1,0},{2,3},{3,2},{4,5},{5,4},{6,7},{7,6},{8,9},{9,8},{10,11... | collective-permute-start | bytes 196616 | tf_op jit(solution)/shard_map/ppermute | solution.py:377
  57.3 23.0 %all-to-all-start.1 = ((bf16[16,80,128]{2,1,0:T(8,128)(2,1)}), bf16[16,80,128]{2,1,0:T(8,128)(2,1)S(1)}, u32[]{:S(2)}, u32[]{:S(2)}) async-start(bf16[16,80,128]{2,1,0:T(8,128)(2,1)} %shard_map.131), calls=%async_computation.1 | async-start | bytes 655360 | tf_op jit(solution)/shard_map/all_to_all | solution.py:284
  67.5 41.4 %copy-start.4 = (bf16[3,80,576]{2,1,0:T(8,128)(2,1)S(1)}, bf16[3,80,576]{2,1,0:T(8,128)(2,1)}, u32[]{:S(2)}) copy-start(bf16[3,80,576]{2,1,0:T(8,128)(2,1)} %copy-done.3) | copy-start | bytes 829444
  67.5 32.6 %collective-permute-start.7 = (bf16[3,80,576]{2,1,0:T(8,128)(2,1)}, bf16[3,80,576]{2,1,0:T(8,128)(2,1)S(1)}, u32[]{:S(2)}, u32[]{:S(2)}) collective-permute-start(bf16[3,80,576]{2,1,0:T(8,128)(2,1)} %get-tuple-element.82), channel_id=1, source_target_pairs={{0,3},{1,2},{2,1},{3,0},{4,7},{5,6},{6,5},{7,4},{8,11},{9,10},{10,... | collective-permute-start | bytes 829448 | tf_op jit(solution)/shard_map/ppermute | solution.py:336
  71.7 29.1 %collective-permute-start.8 = (bf16[3,80,576]{2,1,0:T(8,128)(2,1)}, bf16[3,80,576]{2,1,0:T(8,128)(2,1)S(1)}, u32[]{:S(2)}, u32[]{:S(2)}) collective-permute-start(bf16[3,80,576]{2,1,0:T(8,128)(2,1)} %copy-done.20), channel_id=1, source_target_pairs={{0,6},{1,7},{2,4},{3,5},{4,2},{5,3},{6,0},{7,1},{8,14},{9,15},{10,... | collective-permute-start | bytes 829448 | tf_op jit(solution)/shard_map/ppermute | solution.py:336
  74.8 26.7 %collective-permute-start.9 = (bf16[3,80,576]{2,1,0:T(8,128)(2,1)S(1)}, bf16[3,80,576]{2,1,0:T(8,128)(2,1)S(1)}, u32[]{:S(2)}, u32[]{:S(2)}) collective-permute-start(bf16[3,80,576]{2,1,0:T(8,128)(2,1)S(1)} %copy-done.19), channel_id=1, source_target_pairs={{0,7},{1,6},{2,5},{3,4},{4,3},{5,2},{6,1},{7,0},{8,15},{9,14},{10,... | collective-permute-start | bytes 829448 | tf_op jit(solution)/shard_map/ppermute | solution.py:336
  102.2 16.8 %all-to-all-start.3 = ((bf16[8,88,512]{2,1,0:T(8,128)(2,1)}), bf16[8,88,512]{2,1,0:T(8,128)(2,1)S(1)}, u32[]{:S(2)}, u32[]{:S(2)}) async-start(bf16[8,88,512]{2,1,0:T(8,128)(2,1)} %get-tuple-element.87), calls=%async_computation.3 | async-start | bytes 1441792 | tf_op jit(solution)/shard_map/all_to_all | solution.py:284
  (14 other events, 19.1 us)

commit v7 on v6

--- a/solution.py
+++ b/solution.py
@@ -14,10 +14,12 @@
 CTX = ("y", "xh")
 EXP = ("za", "zb", "xl", "core")
 ZX = ("za", "zb", "xl")
+XC = ("xl", "core")
 NEAR = ("zb", "xl", "core")
 FAR = "za"
 TOK = 128
 SLOT = 32
+FEW = 5
 F32 = jnp.float32
 BF16 = jnp.bfloat16
 VMEM = pl.BlockSpec(memory_space=pltpu.VMEM)
@@ -49,12 +51,42 @@
 
 
 def spread_keys(keys, out):
-    count, half, _ = out.shape
-    width, rows = keys.shape
-    own = keys[pl.ds(pl.multiple_of(lax.axis_index("core") * half, half), half), :]
-    own = jnp.concatenate([own, jnp.zeros((half, TOK - rows), BF16)], axis=1)
+    count, part, _ = out.shape
+    rows = keys.shape[1]
+    own = keys[pl.ds(pl.multiple_of(lax.axis_index(XC) * part, part), part), :]
+    own = jnp.concatenate([own, jnp.zeros((part, TOK - rows), BF16)], axis=1)
     for i in range(count):
         out[i] = own
+
+
+def pick_keys(mask, pieces, out):
+    block = lax.axis_index(CTX)
+    out[...] = jnp.zeros_like(out)
+
+    def step(b, filled):
+        wanted = (mask[block, b] == 1) & (b != block)
+
+        @pl.when(wanted)
+        def _():
+            out[filled] = pieces[b]
+
+        return filled + wanted.astype(jnp.int32)
+
+    lax.fori_loop(0, mask.shape[1], step, 0)
+
+
+def prepare(queries, weights, wide, mine, theirs, turned):
+    heads, width, rows = queries.shape
+    for head in range(heads):
+        lanes = jnp.concatenate([queries[head], jnp.zeros((width, TOK - rows), BF16)], axis=1)
+        wide[head * TOK : (head + 1) * TOK, :] = lanes.T
+    for i in range(weights.shape[1] // TOK):
+        turned[i * TOK : (i + 1) * TOK, :] = weights[:, i * TOK : (i + 1) * TOK].T
+    core = lax.axis_index("core")
+    runs, run, _ = mine.shape
+    for i in range(runs):
+        for out, at in ((mine, 2 * i + core), (theirs, 2 * i + 1 - core)):
+            out[i] = turned[pl.ds(pl.multiple_of(at * run, run), run), :]
 
 
 def route(first, groups, experts, weights, places, shares):
@@ -84,54 +116,52 @@
     shares[...] = share.astype(BF16)
 
 
-def attend(rows, width, mask, qa, qb, ka, kb, va, vb, out, top, total, acc_a, acc_b):
-    block = lax.axis_index(CTX)
+def attend(mask, queries, own, up, *refs):
+    pieces, (out, held, top, total, acc) = refs[:4], refs[4:]
+    block, column = lax.axis_index(CTX), lax.axis_index(XC)
+    width, rows = own.shape
+    part = pieces[0].shape[1]
     inverse_root = width**-0.5
-    q_a, q_b = qa[...], qb[...]
+    wide = queries[...]
     query = lax.broadcasted_iota(jnp.int32, (2 * TOK, TOK), 0) % TOK
     key = lax.broadcasted_iota(jnp.int32, (2 * TOK, TOK), 1)
 
-    def scores_of(b):
-        return (dot(q_a, ka[b]) + dot(q_b, kb[b])) * inverse_root
-
-    own = (key <= query) & (key < rows)
-    masked = jnp.where(own, scores_of(block), MASKED_SCORE)
+    keys = jnp.concatenate([own[...], jnp.zeros((width, TOK - rows), BF16)], axis=1)
+    inside = (key <= query) & (key < rows)
+    masked = jnp.where(inside, dot(wide, keys) * inverse_root, MASKED_SCORE)
     best = jnp.max(masked, axis=1, keepdims=True)
-    terms = jnp.where(own, jnp.exp(masked - best), 0.0)
+    terms = jnp.where(inside, jnp.exp(masked - best), 0.0)
     top[...] = best
     total[...] = jnp.sum(terms, axis=1, keepdims=True)
-    acc_a[...] = dot_nt(terms.astype(BF16), ka[block])
-    acc_b[...] = dot_nt(terms.astype(BF16), kb[block])
-
-    def step(b, carry):
-        @pl.when((mask[block, b] == 1) & (b != block))
-        def _():
-            inside = key < rows
-            masked = jnp.where(inside, scores_of(b), MASKED_SCORE)
-            old = top[...]
-            best = jnp.maximum(old, jnp.max(masked, axis=1, keepdims=True))
-            terms = jnp.where(inside, jnp.exp(masked - best), 0.0)
-            shrink = jnp.exp(old - best)
-            top[...] = best
-            total[...] = total[...] * shrink + jnp.sum(terms, axis=1, keepdims=True)
-            rounded = terms.astype(BF16)
-            acc_a[...] = acc_a[...] * shrink + dot_nt(rounded, ka[b])
-            acc_b[...] = acc_b[...] * shrink + dot_nt(rounded, kb[b])
-
+    acc[...] = dot_nt(terms.astype(BF16), keys)
+
+    def count(b, filled):
+        return filled + ((mask[block, b] == 1) & (b != block)).astype(jnp.int32)
+
+    def step(slot, carry):
+        for flip, piece in enumerate(pieces):
+            start = pl.multiple_of((column ^ flip) * part, part)
+            held[pl.ds(start, part), :] = piece[slot]
+        inside = key < rows
+        masked = jnp.where(inside, dot(wide, held[...]) * inverse_root, MASKED_SCORE)
+        old = top[...]
+        best = jnp.maximum(old, jnp.max(masked, axis=1, keepdims=True))
+        terms = jnp.where(inside, jnp.exp(masked - best), 0.0)
+        shrink = jnp.exp(old - best)
+        top[...] = best
+        total[...] = total[...] * shrink + jnp.sum(terms, axis=1, keepdims=True)
+        acc[...] = acc[...] * shrink + dot_nt(terms.astype(BF16), held[...])
         return carry
 
-    lax.fori_loop(0, mask.shape[1], step, 0)
+    lax.fori_loop(0, lax.fori_loop(0, mask.shape[1], count, 0), step, 0)
     inverse = 1.0 / total[...]
     values = []
-    for head in range(2):
+    for head in range(up.shape[0]):
         span = slice(head * TOK, (head + 1) * TOK)
-        value = jnp.zeros((TOK, TOK), F32)
-        for acc, up in ((acc_a, va), (acc_b, vb)):
-            latent = acc[span, :] * inverse[span, :]
-            high = latent.astype(BF16)
-            low = (latent - high.astype(F32)).astype(BF16)
-            value = value + dot(high, up[head]) + dot(low, up[head])
-        values.append(value.T.astype(BF16))
+        latent = acc[span, : up.shape[1]] * inverse[span, :]
+        high = latent.astype(BF16)
+        low = (latent - high.astype(F32)).astype(BF16)
+        values.append((dot(high, up[head]) + dot(low, up[head])).T.astype(BF16))
     out[...] = jnp.concatenate(values, axis=0)
 
 
@@ -302,20 +332,23 @@
     ctx_count = lax.axis_size(CTX)
     near_count = lax.axis_size(NEAR)
     far_count = lax.axis_size(FAR)
-    core = lax.axis_index("core")
     block_rows, key_width = latents.shape
     heads = queries.shape[1]
-    latent_width, value_width = value_up.shape[1:]
+    value_width = value_up.shape[2]
     run = residual.shape[1]
     local_experts, _, hidden_units = w_gate.shape
-    half = key_width // 2
     pad_rows = TOK - block_rows
     slots = ctx_count * SLOT
     part = hidden_units // near_count
     sub = part // far_count
 
-    spread = call(spread_keys, shape((ctx_count, half, TOK)), [VMEM])(latents.T)
-    keys_a = exchange(spread, CTX)
+    quarter = key_width // lax.axis_size(XC)
+    turned_keys = latents.T
+    spread = call(spread_keys, shape((ctx_count, quarter, TOK)), [VMEM])(turned_keys)
+    pieces = exchange(spread, CTX)
+    apart = jnp.arange(ctx_count)[:, None] != jnp.arange(ctx_count)[None, :]
+    named = jnp.sum(jnp.where((block_mask == 1) & apart, 1, 0), axis=1)
+    few = jnp.max(named) <= FEW
 
     first_share = run + 16
     places, slot_shares = call(
@@ -335,45 +368,54 @@
     def flipped(x, flip):
         return lax.ppermute(x, NEAR, [(a, a ^ flip) for a in range(near_count)])
 
+    out_proj, *packed = lax.optimization_barrier((out_proj, *packed))
     moved = {i: flipped(packed[i], i) for i in (1, 2, 4, 5)}
 
-    wide_q = jnp.pad(queries.transpose(1, 0, 2), ((0, 0), (0, pad_rows), (0, 0)))
-    wide_q = wide_q.reshape(heads * TOK, key_width)
-    q_low, q_high = wide_q[:, :half], wide_q[:, half:]
-    v_low = value_up[:, :half]
-    v_high = jnp.pad(value_up[:, half:], ((0, 0), (0, key_width - latent_width), (0, 0)))
-    flip = core == 1
     runs = D // run
-    out_weights = out_proj.T.reshape(runs // 2, 2, run, heads * value_width)
-    out_mine = jnp.where(flip, out_weights[:, 1], out_weights[:, 0])
-    out_theirs = jnp.where(flip, out_weights[:, 0], out_weights[:, 1])
+    depth = heads * value_width
+    wide_q, out_mine, out_theirs = call(
+        prepare,
+        [shape((heads * TOK, key_width))] + [shape((runs // 2, run, depth))] * 2,
+        [VMEM] * 2,
+        [pltpu.VMEM((D, depth), BF16)],
+    )(queries.transpose(1, 2, 0), out_proj)
     out_theirs = lax.ppermute(out_theirs, "core", [(0, 1), (1, 0)])
-    operands = (
-        jnp.where(flip, q_high, q_low),
-        jnp.where(flip, q_low, q_high),
-        jnp.where(flip, v_high, v_low),
-        jnp.where(flip, v_low, v_high),
-        out_mine,
-        out_theirs,
-    )
     resid = jnp.pad(residual.T, ((0, 0), (0, pad_rows)))
     gain = norm_gain.astype(F32)[:, None]
-    keys_a, operands, moved, places, slot_shares, resid, gain = lax.optimization_barrier(
-        (keys_a, operands, moved, places, slot_shares, resid, gain)
-    )
-    keys_b = lax.ppermute(keys_a, "core", [(0, 1), (1, 0)])
-    q_a, q_b, v_a, v_b, out_mine, out_theirs = operands
-    values = call(
-        functools.partial(attend, block_rows, key_width),
-        shape((heads * value_width, TOK)),
-        [SMEM] + [VMEM] * 6,
-        [
-            pltpu.VMEM((2 * TOK, 1), F32),
-            pltpu.VMEM((2 * TOK, 1), F32),
-            pltpu.VMEM((2 * TOK, half), F32),
-            pltpu.VMEM((2 * TOK, half), F32),
-        ],
-    )(block_mask, q_a, q_b, keys_a, keys_b, v_a, v_b)
+    pieces, few, wide_q, out_mine, out_theirs, moved[1], places, slot_shares, resid, gain = (
+        lax.optimization_barrier(
+            (pieces, few, wide_q, out_mine, out_theirs, moved[1], places, slot_shares, resid, gain)
+        )
+    )
+
+    def attention(held_slots, mask, pieces, wide_q, turned_keys, value_up):
+        picked = call(pick_keys, shape((held_slots, quarter, TOK)), [SMEM, VMEM])(mask, pieces)
+        across = lax.ppermute(picked, "xl", [(0, 1), (1, 0)])
+        beside = lax.ppermute(picked, "core", [(0, 1), (1, 0)])
+        corner = lax.ppermute(across, "core", [(0, 1), (1, 0)])
+        return call(
+            attend,
+            shape((depth, TOK)),
+            [SMEM] + [VMEM] * 7,
+            [
+                pltpu.VMEM((key_width, TOK), BF16),
+                pltpu.VMEM((heads * TOK, 1), F32),
+                pltpu.VMEM((heads * TOK, 1), F32),
+                pltpu.VMEM((heads * TOK, key_width), F32),
+            ],
+        )(mask, wide_q, turned_keys, value_up, picked, beside, across, corner)
+
+    values = lax.cond(
+        few,
+        functools.partial(attention, FEW),
+        functools.partial(attention, ctx_count - 1),
+        block_mask,
+        pieces,
+        wide_q,
+        turned_keys,
+        value_up,
+    )
+    values, moved = lax.optimization_barrier((values, moved))
     other_values = lax.ppermute(values, "core", [(0, 1), (1, 0)])
     summed = call(project_out, shape((runs // 2, run, TOK)), [VMEM] * 4)(
         values, other_values, out_mine, out_theirs

time: 184 us -> 184 us (level)
  waiting for transfers between devices: 17.4 us -> 9.42 us
  Pallas kernels: 13.4 us -> 15.9 us
  starting transfers between devices: 59.8 us -> 62.3 us
    ppermute x7, waiting for transfers between devices: 6.13 us -> 0.02 us  [flipped(): return lax.ppermute(x, NEAR, [(a, a ^ flip) for a in range(near_count)])]
    pallas_call x2 -> x4, Pallas kernels: 3.22 us -> 7.01 us  [the longest x1 2.17 us: attention(): call(attend, shape((depth, TOK)), [SMEM] + [VMEM] * 7, [pltpu.VMEM((key_w...]
    all_to_all x3, waiting for transfers between devices: 7.91 us -> 5.44 us  [exchange(): return lax.all_to_all(x, axes, split_axis=0, concat_axis=0, tiled=True)]
    ppermute x1 -> x3, starting transfers between devices: 6.49 us -> 8.77 us  [the longest x1 3.13 us: attention(): corner = lax.ppermute(across, 'core', [(0, 1), (1, 0)])]
    unnamed x50 -> x62, local copies, waits for them, and re-layouts: 11.6 us -> 13.1 us
  transfers between devices with their start and end apart: 13 -> 15, of which waited for: 6 -> 5; matrix products, arithmetic and copies ran while one was open for 2% -> 0% of each run, Pallas kernels for 3% -> 5%
where the time goes in v7:
time: 184 us; the launch traced here: 183 us
  blocking collectives  80.1 us (44%)
  starting transfers between devices  62.3 us (34%)
  Pallas kernels  15.9 us (9%)
  local copies, waits for them, and re-layouts  13.2 us (7%)
  waiting for transfers between devices  9.42 us (5%)
    all_to_all x5, blocking collectives, exchange(): return lax.all_to_all(x, axes, split_axis=0, concat_axis=0, tiled=True)  80.1 us
    all_to_all x3, starting transfers between devices, exchange(): return lax.all_to_all(x, axes, split_axis=0, concat_axis=0, tiled=True)  27.7 us
    ppermute x7, starting transfers between devices, flipped(): return lax.ppermute(x, NEAR, [(a, a ^ flip) for a in range(near_count)])  20.7 us
    unnamed x62, local copies, waits for them, and re-layouts  13.1 us
    all_to_all x3, waiting for transfers between devices, exchange(): return lax.all_to_all(x, axes, split_axis=0, concat_axis=0, tiled=True)  5.44 us
  transfers between devices with their start and end apart: 15, of which 5 were waited for; matrix products, arithmetic and copies ran while one was open for 0% of the time, Pallas kernels for 5%

profile of v7, /device:TPU:1, one launch (start us, length us, event | category | flops | bytes accessed | tf_op | source)
XLA Modules:
  0.0 182.7 jit_solution(16012309649676932653)
XLA Ops:
  1.9 10.4 %all-to-all-start = ((bf16[16,144,128]{2,1,0:T(8,128)(2,1)}), bf16[16,144,128]{2,1,0:T(8,128)(2,1)}, u32[]{:S(2)}, u32[]{:S(2)}) async-start(bf16[16,144,128]{2,1,0:T(8,128)(2,1)} %shard_map.127), calls=%async_computation | async-start | bytes 1179648 | tf_op jit(solution)/shard_map/all_to_all | solution.py:314
  16.0 2.1 %shard_map.129 = (bf16[3,80,576]{2,1,0:T(8,128)(2,1)S(1)}, bf16[3,80,576]{2,1,0:T(8,128)(2,1)}, bf16[3,80,576]{2,1,0:T(8,128)(2,1)}, bf16[3,80,576]{2,1,0:T(8,12...) custom-call(bf16[6,80,768]{2,1,0:T(8,128)(2,1)S(1)} %copy-done.1, ...), custom_call_target="tpu_custom_call" | custom-call | tf_op jit(solution)/shard_map/pallas_call | solution.py:361
  19.6 2.8 %collective-permute-start.6 = (bf16[16,80,256]{2,1,0:T(8,128)(2,1)}, bf16[16,80,256]{2,1,0:T(8,128)(2,1)S(1)}, u32[]{:S(2)}, u32[]{:S(2)}) collective-permute-start(bf16[16,80,256]{2,1,0:T(8,128)(2,1)} %get-tuple-element.112), channel_id=1, source_target_pairs={{0,1},{1,0},{2,3},{3,2},{4,5},{5,4},{6,7},{7,6},{8,9},{9,8},{10,11... | collective-permute-start | bytes 1966088 | tf_op jit(solution)/shard_map/ppermute | solution.py:382
  24.4 2.2 %collective-permute-start.8 = (bf16[3,80,576]{2,1,0:T(8,128)(2,1)}, bf16[3,80,576]{2,1,0:T(8,128)(2,1)S(1)}, u32[]{:S(2)}, u32[]{:S(2)}) collective-permute-start(bf16[3,80,576]{2,1,0:T(8,128)(2,1)} %get-tuple-element.120), channel_id=1, source_target_pairs={{0,2},{1,3},{2,0},{3,1},{4,6},{5,7},{6,4},{7,5},{8,10},{9,11},{10,... | collective-permute-start | bytes 829448 | tf_op jit(solution)/shard_map/ppermute | solution.py:369
  26.6 4.0 %collective-permute-start.9 = (bf16[3,80,576]{2,1,0:T(8,128)(2,1)}, bf16[3,80,576]{2,1,0:T(8,128)(2,1)S(1)}, u32[]{:S(2)}, u32[]{:S(2)}) collective-permute-start(bf16[3,80,576]{2,1,0:T(8,128)(2,1)} %get-tuple-element.121), channel_id=1, source_target_pairs={{0,4},{1,5},{2,6},{3,7},{4,0},{5,1},{6,2},{7,3},{8,12},{9,13},{10,... | collective-permute-start | bytes 829448 | tf_op jit(solution)/shard_map/ppermute | solution.py:369
  30.6 2.6 %collective-permute-start.10 = (bf16[3,80,576]{2,1,0:T(8,128)(2,1)}, bf16[3,80,576]{2,1,0:T(8,128)(2,1)S(1)}, u32[]{:S(2)}, u32[]{:S(2)}) collective-permute-start(bf16[3,80,576]{2,1,0:T(8,128)(2,1)} %get-tuple-element.122), channel_id=1, source_target_pairs={{0,5},{1,4},{2,7},{3,6},{4,1},{5,0},{6,3},{7,2},{8,13},{9,12},{10,... | collective-permute-start | bytes 829448 | tf_op jit(solution)/shard_map/ppermute | solution.py:369
  35.4 15.4 %conditional.1 = (bf16[256,128]{1,0:T(8,128)(2,1)S(1)}) conditional(s32[]{:T(128)} %convert_element_type.6, (s32[16,16]{1,0:T(8,128)S(1)}, bf16[16,144,128]{2,1,0:T(8,128)(2,1)}, bf16[256,576]{1,0:T(8,128)(2,1)}, bf16[576,120]{1,0:T(8,128)(2,1)S(1)}, bf16[2,512,128]{2,1,0:T(8,128)(2,1)}) %tuple.28, (s32[16,16]{1,0:T(8,128)S(1)}, ...), branch_computations={%region_2.3_spmd, %region_3.4_spmd} | conditional | bytes 6635648 | solution.py:408
  36.8 3.1 %collective-permute-start.4 = (bf16[5,144,128]{2,1,0:T(8,128)(2,1)S(1)}, bf16[5,144,128]{2,1,0:T(8,128)(2,1)S(1)}, u32[]{:S(2)}, u32[]{:S(2)}) collective-permute-start(bf16[5,144,128]{2,1,0:T(8,128)(2,1)S(1)} %branch_1_fun.2.refs_0_), channel_id=1, source_target_pairs={{0,2},{2,0},{1,3},{3,1},{4,6},{6,4},{5,7},{7,5},{8,10},{10,8},{9,1... | collective-permute-start | bytes 552968 | tf_op jit(solution)/shard_map/cond/branch_1_fun/ppermute | solution.py:393
  39.9 2.6 %collective-permute-start.3 = (bf16[5,144,128]{2,1,0:T(8,128)(2,1)S(1)}, bf16[5,144,128]{2,1,0:T(8,128)(2,1)S(1)}, u32[]{:S(2)}, u32[]{:S(2)}) collective-permute-start(bf16[5,144,128]{2,1,0:T(8,128)(2,1)S(1)} %branch_1_fun.2.refs_0_), channel_id=1, source_target_pairs={{0,1},{1,0},{2,3},{3,2},{4,5},{5,4},{6,7},{7,6},{8,9},{9,8},{10,11... | collective-permute-start | bytes 552968 | tf_op jit(solution)/shard_map/cond/branch_1_fun/ppermute | solution.py:394
  44.5 3.1 %collective-permute-start.5 = (bf16[5,144,128]{2,1,0:T(8,128)(2,1)S(1)}, bf16[5,144,128]{2,1,0:T(8,128)(2,1)S(1)}, u32[]{:S(2)}, u32[]{:S(2)}) collective-permute-start(bf16[5,144,128]{2,1,0:T(8,128)(2,1)S(1)} %collective-permute-done.4.refs_2_), channel_id=1, source_target_pairs={{0,1},{1,0},{2,3},{3,2},{4,5},{5,4},{6,7},{7,6},{8,9},{9,8},{10,11... | collective-permute-start | bytes 552968 | tf_op jit(solution)/shard_map/cond/branch_1_fun/ppermute | solution.py:395
  48.7 2.2 %branch_1_fun.3 = bf16[256,128]{1,0:T(8,128)(2,1)S(1)} custom-call(s32[16,16]{1,0:T(8,128)S(1)} %get-tuple-element.33.mask, bf16[256,576]{1,0:T(8,128)(2,1)} %get-tuple-element.34.queries, bf16[576,120]{1,0:T(8,128)(2,1)S(1)} %get-tuple-element.35.own, bf16[2,512,128]{2,1,0:T(8,128)(2,1)} %get-tuple-element.36.up, ...), custom_call_target="tpu_custom_call" | custom-call | tf_op jit(solution)/shard_map/cond/branch_1_fun/pallas_call | solution.py:396
  50.9 2.3 %collective-permute-start.11 = (bf16[256,128]{1,0:T(8,128)(2,1)S(1)}, bf16[256,128]{1,0:T(8,128)(2,1)S(1)}, u32[]{:S(2)}, u32[]{:S(2)}) collective-permute-start(bf16[256,128]{1,0:T(8,128)(2,1)S(1)} %get-tuple-element.158.mine), channel_id=1, source_target_pairs={{0,1},{1,0},{2,3},{3,2},{4,5},{5,4},{6,7},{7,6},{8,9},{9,8},{10,11... | collective-permute-start | bytes 196616 | tf_op jit(solution)/shard_map/ppermute | solution.py:419
  55.3 10.6 %all-to-all-start.1 = ((bf16[16,80,128]{2,1,0:T(8,128)(2,1)}), bf16[16,80,128]{2,1,0:T(8,128)(2,1)S(1)}, u32[]{:S(2)}, u32[]{:S(2)}) async-start(bf16[16,80,128]{2,1,0:T(8,128)(2,1)} %shard_map.131), calls=%async_computation.1 | async-start | bytes 655360 | tf_op jit(solution)/shard_map/all_to_all | solution.py:314
  66.0 4.1 %collective-permute-start.12 = (bf16[3,80,576]{2,1,0:T(8,128)(2,1)}, bf16[3,80,576]{2,1,0:T(8,128)(2,1)S(1)}, u32[]{:S(2)}, u32[]{:S(2)}) collective-permute-start(bf16[3,80,576]{2,1,0:T(8,128)(2,1)} %copy-done.26), channel_id=1, source_target_pairs={{0,3},{1,2},{2,1},{3,0},{4,7},{5,6},{6,5},{7,4},{8,11},{9,10},{10,... | collective-permute-start | bytes 829448 | tf_op jit(solution)/shard_map/ppermute | solution.py:369
  70.0 3.1 %collective-permute-start.13 = (bf16[3,80,576]{2,1,0:T(8,128)(2,1)}, bf16[3,80,576]{2,1,0:T(8,128)(2,1)S(1)}, u32[]{:S(2)}, u32[]{:S(2)}) collective-permute-start(bf16[3,80,576]{2,1,0:T(8,128)(2,1)} %copy-done.25), channel_id=1, source_target_pairs={{0,6},{1,7},{2,4},{3,5},{4,2},{5,3},{6,0},{7,1},{8,14},{9,15},{10,... | collective-permute-start | bytes 829448 | tf_op jit(solution)/shard_map/ppermute | solution.py:369
  73.1 2.9 %collective-permute-start.14 = (bf16[3,80,576]{2,1,0:T(8,128)(2,1)}, bf16[3,80,576]{2,1,0:T(8,128)(2,1)S(1)}, u32[]{:S(2)}, u32[]{:S(2)}) collective-permute-start(bf16[3,80,576]{2,1,0:T(8,128)(2,1)} %copy-done.24), channel_id=1, source_target_pairs={{0,7},{1,6},{2,5},{3,4},{4,3},{5,2},{6,1},{7,0},{8,15},{9,14},{10,... | collective-permute-start | bytes 829448 | tf_op jit(solution)/shard_map/ppermute | solution.py:369
  76.1 2.6 %all-to-all-done.1.parts = bf16[16,80,128]{2,1,0:T(8,128)(2,1)S(1)} async-done(((bf16[16,80,128]{2,1,0:T(8,128)(2,1)}), bf16[16,80,128]{2,1,0:T(8,128)(2,1)S(1)}, u32[]{:S(2)}, u32[]{:S(2)}) %all-to-all-start.1) | async-done | bytes 327712 | tf_op jit(solution)/shard_map/all_to_all | solution.py:314
  79.9 20.5 %all_to_all.40 = bf16[16,32,128]{2,1,0:T(8,128)(2,1)S(1)} all-to-all(bf16[16,32,128]{2,1,0:T(8,128)(2,1)S(1)} %bitcast.20), channel_id=1, replica_groups=mesh['y'=8,'xh'=2,'za'=4,'zb'=2,'xl'=2,'core'=2] {'y','xh'}, dimensions={0} | all-to-all | bytes 262144 | tf_op jit(solution)/shard_map/all_to_all | solution.py:314
  102.9 6.7 %all-to-all-start.3 = ((bf16[8,88,512]{2,1,0:T(8,128)(2,1)}), bf16[8,88,512]{2,1,0:T(8,128)(2,1)S(1)}, u32[]{:S(2)}, u32[]{:S(2)}) async-start(bf16[8,88,512]{2,1,0:T(8,128)(2,1)} %get-tuple-element.144), calls=%async_computation.3 | async-start | bytes 1441792 | tf_op jit(solution)/shard_map/all_to_all | solution.py:314
  116.9 2.8 %all-to-all-done.3.inputs = bf16[8,88,512]{2,1,0:T(8,128)(2,1)S(1)} async-done(((bf16[8,88,512]{2,1,0:T(8,128)(2,1)}), bf16[8,88,512]{2,1,0:T(8,128)(2,1)S(1)}, u32[]{:S(2)}, u32[]{:S(2)}) %all-to-all-start.3) | async-done | bytes 720928 | tf_op jit(solution)/shard_map/all_to_all | solution.py:314
  120.8 15.0 %all_to_all.41.got = bf16[4,104,512]{2,1,0:T(8,128)(2,1)S(1)} all-to-all(bf16[4,104,512]{2,1,0:T(8,128)(2,1)S(1)} %shard_map.135), channel_id=1, replica_groups=mesh['y'=8,'xh'=2,'za'=4,'zb'=2,'xl'=2,'core'=2] {'za'}, dimensions={0} | all-to-all | bytes 851968 | tf_op jit(solution)/shard_map/all_to_all | solution.py:314
  135.9 12.3 %all_to_all.42.acts = bf16[4,48,512]{2,1,0:T(8,128)(2,1)S(1)} all-to-all(bf16[4,48,512]{2,1,0:T(8,128)(2,1)S(1)} %shard_map.136), channel_id=1, replica_groups=mesh['y'=8,'xh'=2,'za'=4,'zb'=2,'xl'=2,'core'=2] {'za'}, dimensions={0} | all-to-all | bytes 393216 | tf_op jit(solution)/shard_map/all_to_all | solution.py:314
  149.3 15.5 %all_to_all.43.got = bf16[8,80,512]{2,1,0:T(8,128)(2,1)S(1)} all-to-all(bf16[8,80,512]{2,1,0:T(8,128)(2,1)S(1)} %shard_map.137), channel_id=1, replica_groups=mesh['y'=8,'xh'=2,'za'=4,'zb'=2,'xl'=2,'core'=2] {'zb','xl','core'}, dimensions={0} | all-to-all | bytes 1310720 | tf_op jit(solution)/shard_map/all_to_all | solution.py:314
  165.0 16.8 %all_to_all.44 = bf16[16,32,128]{2,1,0:T(8,128)(2,1)S(1)} all-to-all(bf16[16,32,128]{2,1,0:T(8,128)(2,1)S(1)} %bitcast.18), channel_id=1, replica_groups=mesh['y'=8,'xh'=2,'za'=4,'zb'=2,'xl'=2,'core'=2] {'y','xh'}, dimensions={0} | all-to-all | bytes 262144 | tf_op jit(solution)/shard_map/all_to_all | solution.py:314
  (94 shorter events, 31.4 us)
Async XLA Ops:
  1.9 16.1 %copy-start = (bf16[256,2560]{1,0:T(8,128)(2,1)S(1)}, bf16[256,2560]{1,0:T(8,128)(2,1)}, u32[]{:S(2)}) copy-start(bf16[256,2560]{1,0:T(8,128)(2,1)} %weights) | copy-start | bytes 3932164
  1.9 32.8 %all-to-all-start = ((bf16[16,144,128]{2,1,0:T(8,128)(2,1)}), bf16[16,144,128]{2,1,0:T(8,128)(2,1)}, u32[]{:S(2)}, u32[]{:S(2)}) async-start(bf16[16,144,128]{2,1,0:T(8,128)(2,1)} %shard_map.127), calls=%async_computation | async-start | bytes 1179648 | tf_op jit(solution)/shard_map/all_to_all | solution.py:314
  16.0 17.3 %copy-start.28 = (s32[16,16]{1,0:T(8,128)S(1)}, s32[16,16]{1,0:T(8,128)}, u32[]{:S(2)}) copy-start(s32[16,16]{1,0:T(8,128)} %param.17) | copy-start | bytes 3076
  16.0 18.7 %copy-start.29 = (bf16[120,80]{0,1:T(8,128)(2,1)S(1)}, bf16[120,80]{0,1:T(8,128)(2,1)}, u32[]{:S(2)}) copy-start(bf16[120,80]{0,1:T(8,128)(2,1)} %param.20) | copy-start | bytes 57604
  16.0 18.7 %copy-start.30 = (bf16[80]{0:T(256)(128)(2,1)S(1)}, bf16[80]{0:T(256)(128)(2,1)}, u32[]{:S(2)}) copy-start(bf16[80]{0:T(256)(128)(2,1)} %param.21) | copy-start | bytes 484
  18.1 15.2 %copy-start.26 = (bf16[3,80,576]{2,1,0:T(8,128)(2,1)}, bf16[3,80,576]{2,1,0:T(8,128)(2,1)S(1)}, u32[]{:S(2)}) copy-start(bf16[3,80,576]{2,1,0:T(8,128)(2,1)S(1)} %get-tuple-element.139) | copy-start | bytes 829444
  18.1 16.7 %copy-start.27 = (bf16[120,576]{0,1:T(8,128)(2,1)S(1)}, bf16[120,576]{0,1:T(8,128)(2,1)}, u32[]{:S(2)}) copy-start(bf16[120,576]{0,1:T(8,128)(2,1)} %param.16) | copy-start | bytes 414724
  19.6 15.1 %collective-permute-start.6 = (bf16[16,80,256]{2,1,0:T(8,128)(2,1)}, bf16[16,80,256]{2,1,0:T(8,128)(2,1)S(1)}, u32[]{:S(2)}, u32[]{:S(2)}) collective-permute-start(bf16[16,80,256]{2,1,0:T(8,128)(2,1)} %get-tuple-element.112), channel_id=1, source_target_pairs={{0,1},{1,0},{2,3},{3,2},{4,5},{5,4},{6,7},{7,6},{8,9},{9,8},{10,11... | collective-permute-start | bytes 1966088 | tf_op jit(solution)/shard_map/ppermute | solution.py:382
  22.5 12.3 %collective-permute-start.7 = (bf16[3,80,576]{2,1,0:T(8,128)(2,1)}, bf16[3,80,576]{2,1,0:T(8,128)(2,1)S(1)}, u32[]{:S(2)}, u32[]{:S(2)}) collective-permute-start(bf16[3,80,576]{2,1,0:T(8,128)(2,1)} %get-tuple-element.113), channel_id=1, source_target_pairs={{0,1},{1,0},{2,3},{3,2},{4,5},{5,4},{6,7},{7,6},{8,9},{9,8},{10,11... | collective-permute-start | bytes 829448 | tf_op jit(solution)/shard_map/ppermute | solution.py:369
  24.4 26.5 %collective-permute-start.8 = (bf16[3,80,576]{2,1,0:T(8,128)(2,1)}, bf16[3,80,576]{2,1,0:T(8,128)(2,1)S(1)}, u32[]{:S(2)}, u32[]{:S(2)}) collective-permute-start(bf16[3,80,576]{2,1,0:T(8,128)(2,1)} %get-tuple-element.120), channel_id=1, source_target_pairs={{0,2},{1,3},{2,0},{3,1},{4,6},{5,7},{6,4},{7,5},{8,10},{9,11},{10,... | collective-permute-start | bytes 829448 | tf_op jit(solution)/shard_map/ppermute | solution.py:369
  26.6 24.3 %collective-permute-start.9 = (bf16[3,80,576]{2,1,0:T(8,128)(2,1)}, bf16[3,80,576]{2,1,0:T(8,128)(2,1)S(1)}, u32[]{:S(2)}, u32[]{:S(2)}) collective-permute-start(bf16[3,80,576]{2,1,0:T(8,128)(2,1)} %get-tuple-element.121), channel_id=1, source_target_pairs={{0,4},{1,5},{2,6},{3,7},{4,0},{5,1},{6,2},{7,3},{8,12},{9,13},{10,... | collective-permute-start | bytes 829448 | tf_op jit(solution)/shard_map/ppermute | solution.py:369
  30.6 20.3 %collective-permute-start.10 = (bf16[3,80,576]{2,1,0:T(8,128)(2,1)}, bf16[3,80,576]{2,1,0:T(8,128)(2,1)S(1)}, u32[]{:S(2)}, u32[]{:S(2)}) collective-permute-start(bf16[3,80,576]{2,1,0:T(8,128)(2,1)} %get-tuple-element.122), channel_id=1, source_target_pairs={{0,5},{1,4},{2,7},{3,6},{4,1},{5,0},{6,3},{7,2},{8,13},{9,12},{10,... | collective-permute-start | bytes 829448 | tf_op jit(solution)/shard_map/ppermute | solution.py:369
  36.8 7.7 %collective-permute-start.4 = (bf16[5,144,128]{2,1,0:T(8,128)(2,1)S(1)}, bf16[5,144,128]{2,1,0:T(8,128)(2,1)S(1)}, u32[]{:S(2)}, u32[]{:S(2)}) collective-permute-start(bf16[5,144,128]{2,1,0:T(8,128)(2,1)S(1)} %branch_1_fun.2.refs_0_), channel_id=1, source_target_pairs={{0,2},{2,0},{1,3},{3,1},{4,6},{6,4},{5,7},{7,5},{8,10},{10,8},{9,1... | collective-permute-start | bytes 552968 | tf_op jit(solution)/shard_map/cond/branch_1_fun/ppermute | solution.py:393
  39.9 7.8 %collective-permute-start.3 = (bf16[5,144,128]{2,1,0:T(8,128)(2,1)S(1)}, bf16[5,144,128]{2,1,0:T(8,128)(2,1)S(1)}, u32[]{:S(2)}, u32[]{:S(2)}) collective-permute-start(bf16[5,144,128]{2,1,0:T(8,128)(2,1)S(1)} %branch_1_fun.2.refs_0_), channel_id=1, source_target_pairs={{0,1},{1,0},{2,3},{3,2},{4,5},{5,4},{6,7},{7,6},{8,9},{9,8},{10,11... | collective-permute-start | bytes 552968 | tf_op jit(solution)/shard_map/cond/branch_1_fun/ppermute | solution.py:394
  44.5 4.2 %collective-permute-start.5 = (bf16[5,144,128]{2,1,0:T(8,128)(2,1)S(1)}, bf16[5,144,128]{2,1,0:T(8,128)(2,1)S(1)}, u32[]{:S(2)}, u32[]{:S(2)}) collective-permute-start(bf16[5,144,128]{2,1,0:T(8,128)(2,1)S(1)} %collective-permute-done.4.refs_2_), channel_id=1, source_target_pairs={{0,1},{1,0},{2,3},{3,2},{4,5},{5,4},{6,7},{7,6},{8,9},{9,8},{10,11... | collective-permute-start | bytes 552968 | tf_op jit(solution)/shard_map/cond/branch_1_fun/ppermute | solution.py:395
  50.9 29.0 %copy-start.6 = (bf16[3,80,576]{2,1,0:T(8,128)(2,1)}, bf16[3,80,576]{2,1,0:T(8,128)(2,1)S(1)}, u32[]{:S(2)}) copy-start(bf16[3,80,576]{2,1,0:T(8,128)(2,1)S(1)} %collective-permute-done.8.refs_2_) | copy-start | bytes 829444
  50.9 29.0 %copy-start.8 = (bf16[3,80,576]{2,1,0:T(8,128)(2,1)}, bf16[3,80,576]{2,1,0:T(8,128)(2,1)S(1)}, u32[]{:S(2)}) copy-start(bf16[3,80,576]{2,1,0:T(8,128)(2,1)S(1)} %collective-permute-done.9.refs_4_) | copy-start | bytes 829444
  50.9 29.0 %copy-start.10 = (bf16[3,80,576]{2,1,0:T(8,128)(2,1)}, bf16[3,80,576]{2,1,0:T(8,128)(2,1)S(1)}, u32[]{:S(2)}) copy-start(bf16[3,80,576]{2,1,0:T(8,128)(2,1)S(1)} %collective-permute-done.10.refs_5_) | copy-start | bytes 829444
  50.9 3.2 %collective-permute-start.11 = (bf16[256,128]{1,0:T(8,128)(2,1)S(1)}, bf16[256,128]{1,0:T(8,128)(2,1)S(1)}, u32[]{:S(2)}, u32[]{:S(2)}) collective-permute-start(bf16[256,128]{1,0:T(8,128)(2,1)S(1)} %get-tuple-element.158.mine), channel_id=1, source_target_pairs={{0,1},{1,0},{2,3},{3,2},{4,5},{5,4},{6,7},{7,6},{8,9},{9,8},{10,11... | collective-permute-start | bytes 196616 | tf_op jit(solution)/shard_map/ppermute | solution.py:419
  55.3 23.4 %all-to-all-start.1 = ((bf16[16,80,128]{2,1,0:T(8,128)(2,1)}), bf16[16,80,128]{2,1,0:T(8,128)(2,1)S(1)}, u32[]{:S(2)}, u32[]{:S(2)}) async-start(bf16[16,80,128]{2,1,0:T(8,128)(2,1)} %shard_map.131), calls=%async_computation.1 | async-start | bytes 655360 | tf_op jit(solution)/shard_map/all_to_all | solution.py:314
  66.0 35.4 %collective-permute-start.12 = (bf16[3,80,576]{2,1,0:T(8,128)(2,1)}, bf16[3,80,576]{2,1,0:T(8,128)(2,1)S(1)}, u32[]{:S(2)}, u32[]{:S(2)}) collective-permute-start(bf16[3,80,576]{2,1,0:T(8,128)(2,1)} %copy-done.26), channel_id=1, source_target_pairs={{0,3},{1,2},{2,1},{3,0},{4,7},{5,6},{6,5},{7,4},{8,11},{9,10},{10,... | collective-permute-start | bytes 829448 | tf_op jit(solution)/shard_map/ppermute | solution.py:369
  70.0 31.3 %collective-permute-start.13 = (bf16[3,80,576]{2,1,0:T(8,128)(2,1)}, bf16[3,80,576]{2,1,0:T(8,128)(2,1)S(1)}, u32[]{:S(2)}, u32[]{:S(2)}) collective-permute-start(bf16[3,80,576]{2,1,0:T(8,128)(2,1)} %copy-done.25), channel_id=1, source_target_pairs={{0,6},{1,7},{2,4},{3,5},{4,2},{5,3},{6,0},{7,1},{8,14},{9,15},{10,... | collective-permute-start | bytes 829448 | tf_op jit(solution)/shard_map/ppermute | solution.py:369
  73.1 29.0 %collective-permute-start.14 = (bf16[3,80,576]{2,1,0:T(8,128)(2,1)}, bf16[3,80,576]{2,1,0:T(8,128)(2,1)S(1)}, u32[]{:S(2)}, u32[]{:S(2)}) collective-permute-start(bf16[3,80,576]{2,1,0:T(8,128)(2,1)} %copy-done.24), channel_id=1, source_target_pairs={{0,7},{1,6},{2,5},{3,4},{4,3},{5,2},{6,1},{7,0},{8,15},{9,14},{10,... | collective-permute-start | bytes 829448 | tf_op jit(solution)/shard_map/ppermute | solution.py:369
  102.9 16.8 %all-to-all-start.3 = ((bf16[8,88,512]{2,1,0:T(8,128)(2,1)}), bf16[8,88,512]{2,1,0:T(8,128)(2,1)S(1)}, u32[]{:S(2)}, u32[]{:S(2)}) async-start(bf16[8,88,512]{2,1,0:T(8,128)(2,1)} %get-tuple-element.144), calls=%async_computation.3 | async-start | bytes 1441792 | tf_op jit(solution)/shard_map/all_to_all | solution.py:314
  (22 other events, 72.3 us)

commit v8 on v7

--- a/solution.py
+++ b/solution.py
@@ -14,7 +14,7 @@
 CTX = ("y", "xh")
 EXP = ("za", "zb", "xl", "core")
 ZX = ("za", "zb", "xl")
-XC = ("xl", "core")
+PAIR = ("zb", "core")
 NEAR = ("zb", "xl", "core")
 FAR = "za"
 TOK = 128
@@ -53,7 +53,7 @@
 def spread_keys(keys, out):
     count, part, _ = out.shape
     rows = keys.shape[1]
-    own = keys[pl.ds(pl.multiple_of(lax.axis_index(XC) * part, part), part), :]
+    own = keys[pl.ds(pl.multiple_of(lax.axis_index(PAIR) * part, part), part), :]
     own = jnp.concatenate([own, jnp.zeros((part, TOK - rows), BF16)], axis=1)
     for i in range(count):
         out[i] = own
@@ -118,7 +118,7 @@
 
 def attend(mask, queries, own, up, *refs):
     pieces, (out, held, top, total, acc) = refs[:4], refs[4:]
-    block, column = lax.axis_index(CTX), lax.axis_index(XC)
+    block, column = lax.axis_index(CTX), lax.axis_index(PAIR)
     width, rows = own.shape
     part = pieces[0].shape[1]
     inverse_root = width**-0.5
@@ -342,7 +342,7 @@
     part = hidden_units // near_count
     sub = part // far_count
 
-    quarter = key_width // lax.axis_size(XC)
+    quarter = key_width // lax.axis_size(PAIR)
     turned_keys = latents.T
     spread = call(spread_keys, shape((ctx_count, quarter, TOK)), [VMEM])(turned_keys)
     pieces = exchange(spread, CTX)
@@ -369,7 +369,7 @@
         return lax.ppermute(x, NEAR, [(a, a ^ flip) for a in range(near_count)])
 
     out_proj, *packed = lax.optimization_barrier((out_proj, *packed))
-    moved = {i: flipped(packed[i], i) for i in (1, 2, 4, 5)}
+    moved = {i: flipped(packed[i], i) for i in (2, 3, 6)}
 
     runs = D // run
     depth = heads * value_width
@@ -382,15 +382,15 @@
     out_theirs = lax.ppermute(out_theirs, "core", [(0, 1), (1, 0)])
     resid = jnp.pad(residual.T, ((0, 0), (0, pad_rows)))
     gain = norm_gain.astype(F32)[:, None]
-    pieces, few, wide_q, out_mine, out_theirs, moved[1], places, slot_shares, resid, gain = (
+    pieces, few, wide_q, out_mine, out_theirs, places, slot_shares, resid, gain = (
         lax.optimization_barrier(
-            (pieces, few, wide_q, out_mine, out_theirs, moved[1], places, slot_shares, resid, gain)
+            (pieces, few, wide_q, out_mine, out_theirs, places, slot_shares, resid, gain)
         )
     )
 
     def attention(held_slots, mask, pieces, wide_q, turned_keys, value_up):
         picked = call(pick_keys, shape((held_slots, quarter, TOK)), [SMEM, VMEM])(mask, pieces)
-        across = lax.ppermute(picked, "xl", [(0, 1), (1, 0)])
+        across = lax.ppermute(picked, "zb", [(0, 1), (1, 0)])
         beside = lax.ppermute(picked, "core", [(0, 1), (1, 0)])
         corner = lax.ppermute(across, "core", [(0, 1), (1, 0)])
         return call(
@@ -420,11 +420,10 @@
     summed = call(project_out, shape((runs // 2, run, TOK)), [VMEM] * 4)(
         values, other_values, out_mine, out_theirs
     )
-    summed, *late = lax.optimization_barrier((summed, packed[3], packed[6], packed[7]))
+    summed, *late = lax.optimization_barrier((summed, packed[7], packed[4], packed[5], packed[1]))
     parts = exchange(summed, ZX)
-    for flip, x in zip((3, 6, 7), late):
+    for flip, x in zip((7, 4, 5, 1), late):
         moved[flip] = flipped(x, flip)
-    moved = [packed[0]] + [moved[flip] for flip in range(1, near_count)]
 
     hidden, sent = call(make_rows, [shape((run, TOK)), shape((slots, TOK))], [VMEM] * 5)(
         parts,
@@ -434,6 +433,7 @@
         slot_shares,
     )
     got = exchange(sent.reshape(ctx_count, SLOT, TOK), CTX).reshape(slots, TOK)
+    moved = [packed[0]] + [moved[flip] for flip in range(1, near_count)]
     spread, keep, pick_weight = call(
         functools.partial(spread_rows, run + 8, first_share),
         [

time: 184 us -> 182 us (0.989)
  waiting for transfers between devices: 9.42 us -> 7.17 us
    all_to_all x3, waiting for transfers between devices: 5.44 us -> 2.79 us  [exchange(): return lax.all_to_all(x, axes, split_axis=0, concat_axis=0, tiled=True)]
    unnamed x62 -> x56, local copies, waits for them, and re-layouts: 13.1 us -> 11.6 us
  transfers between devices with their start and end apart: 15 -> 15, of which waited for: 5 -> 4; matrix products, arithmetic and copies ran while one was open for 0% -> 0% of each run, Pallas kernels for 5% -> 5%
where the time goes in v8:
time: 182 us; the launch traced here: 181 us
  blocking collectives  80.4 us (44%)
  starting transfers between devices  63.7 us (35%)
  Pallas kernels  16 us (9%)
  local copies, waits for them, and re-layouts  11.7 us (6%)
  waiting for transfers between devices  7.17 us (4%)
    all_to_all x5, blocking collectives, exchange(): return lax.all_to_all(x, axes, split_axis=0, concat_axis=0, tiled=True)  80.4 us
    all_to_all x3, starting transfers between devices, exchange(): return lax.all_to_all(x, axes, split_axis=0, concat_axis=0, tiled=True)  27.7 us
    ppermute x7, starting transfers between devices, flipped(): return lax.ppermute(x, NEAR, [(a, a ^ flip) for a in range(near_count)])  22 us
    unnamed x56, local copies, waits for them, and re-layouts  11.6 us
    ppermute x1, starting transfers between devices, attention(): beside = lax.ppermute(picked, 'core', [(0, 1), (1, 0)])  4.21 us
  transfers between devices with their start and end apart: 15, of which 4 were waited for; matrix products, arithmetic and copies ran while one was open for 0% of the time, Pallas kernels for 5%

profile of v8, /device:TPU:1, one launch (start us, length us, event | category | flops | bytes accessed | tf_op | source)
XLA Modules:
  0.0 180.9 jit_solution(12175852695145166821)
XLA Ops:
  1.9 10.4 %all-to-all-start = ((bf16[16,144,128]{2,1,0:T(8,128)(2,1)}), bf16[16,144,128]{2,1,0:T(8,128)(2,1)}, u32[]{:S(2)}, u32[]{:S(2)}) async-start(bf16[16,144,128]{2,1,0:T(8,128)(2,1)} %shard_map.127), calls=%async_computation | async-start | bytes 1179648 | tf_op jit(solution)/shard_map/all_to_all | solution.py:314
  15.9 2.3 %shard_map.129 = (bf16[3,80,576]{2,1,0:T(8,128)(2,1)S(1)}, bf16[3,80,576]{2,1,0:T(8,128)(2,1)}, bf16[3,80,576]{2,1,0:T(8,128)(2,1)}, bf16[3,80,576]{2,1,0:T(8,12...) custom-call(bf16[6,80,768]{2,1,0:T(8,128)(2,1)S(1)} %copy-done.1, ...), custom_call_target="tpu_custom_call" | custom-call | tf_op jit(solution)/shard_map/pallas_call | solution.py:361
  19.8 2.8 %collective-permute-start.6 = (bf16[16,80,256]{2,1,0:T(8,128)(2,1)}, bf16[16,80,256]{2,1,0:T(8,128)(2,1)S(1)}, u32[]{:S(2)}, u32[]{:S(2)}) collective-permute-start(bf16[16,80,256]{2,1,0:T(8,128)(2,1)} %get-tuple-element.111), channel_id=1, source_target_pairs={{0,1},{1,0},{2,3},{3,2},{4,5},{5,4},{6,7},{7,6},{8,9},{9,8},{10,11... | collective-permute-start | bytes 1966088 | tf_op jit(solution)/shard_map/ppermute | solution.py:382
  22.6 2.2 %collective-permute-start.7 = (bf16[3,80,576]{2,1,0:T(8,128)(2,1)}, bf16[3,80,576]{2,1,0:T(8,128)(2,1)S(1)}, u32[]{:S(2)}, u32[]{:S(2)}) collective-permute-start(bf16[3,80,576]{2,1,0:T(8,128)(2,1)} %get-tuple-element.117), channel_id=1, source_target_pairs={{0,2},{1,3},{2,0},{3,1},{4,6},{5,7},{6,4},{7,5},{8,10},{9,11},{10,... | collective-permute-start | bytes 829448 | tf_op jit(solution)/shard_map/ppermute | solution.py:369
  24.9 3.2 %collective-permute-start.8 = (bf16[3,80,576]{2,1,0:T(8,128)(2,1)}, bf16[3,80,576]{2,1,0:T(8,128)(2,1)S(1)}, u32[]{:S(2)}, u32[]{:S(2)}) collective-permute-start(bf16[3,80,576]{2,1,0:T(8,128)(2,1)} %get-tuple-element.118), channel_id=1, source_target_pairs={{0,3},{1,2},{2,1},{3,0},{4,7},{5,6},{6,5},{7,4},{8,11},{9,10},{10,... | collective-permute-start | bytes 829448 | tf_op jit(solution)/shard_map/ppermute | solution.py:369
  28.1 4.0 %collective-permute-start.9 = (bf16[3,80,576]{2,1,0:T(8,128)(2,1)}, bf16[3,80,576]{2,1,0:T(8,128)(2,1)S(1)}, u32[]{:S(2)}, u32[]{:S(2)}) collective-permute-start(bf16[3,80,576]{2,1,0:T(8,128)(2,1)} %get-tuple-element.119), channel_id=1, source_target_pairs={{0,6},{1,7},{2,4},{3,5},{4,2},{5,3},{6,0},{7,1},{8,14},{9,15},{10,... | collective-permute-start | bytes 829448 | tf_op jit(solution)/shard_map/ppermute | solution.py:369
  33.7 15.9 %conditional.1 = (bf16[256,128]{1,0:T(8,128)(2,1)S(1)}) conditional(s32[]{:T(128)} %convert_element_type.6, (s32[16,16]{1,0:T(8,128)S(1)}, bf16[16,144,128]{2,1,0:T(8,128)(2,1)}, bf16[256,576]{1,0:T(8,128)(2,1)}, bf16[576,120]{1,0:T(8,128)(2,1)S(1)}, bf16[2,512,128]{2,1,0:T(8,128)(2,1)S(1)}) %tuple.30, (s32[16,16]{1,0:T(8,128)S(1)}, ...), branch_computations={%region_2.3_spmd, %region_3.4_spmd} | conditional | bytes 6635648 | solution.py:408
  35.0 1.9 %collective-permute-start.4 = (bf16[5,144,128]{2,1,0:T(8,128)(2,1)S(1)}, bf16[5,144,128]{2,1,0:T(8,128)(2,1)S(1)}, u32[]{:S(2)}, u32[]{:S(2)}) collective-permute-start(bf16[5,144,128]{2,1,0:T(8,128)(2,1)S(1)} %branch_1_fun.2.refs_0_), channel_id=1, source_target_pairs={{0,4},{4,0},{1,5},{5,1},{2,6},{6,2},{3,7},{7,3},{8,12},{12,8},{9,1... | collective-permute-start | bytes 552968 | tf_op jit(solution)/shard_map/cond/branch_1_fun/ppermute | solution.py:393
  37.0 4.2 %collective-permute-start.3 = (bf16[5,144,128]{2,1,0:T(8,128)(2,1)S(1)}, bf16[5,144,128]{2,1,0:T(8,128)(2,1)S(1)}, u32[]{:S(2)}, u32[]{:S(2)}) collective-permute-start(bf16[5,144,128]{2,1,0:T(8,128)(2,1)S(1)} %branch_1_fun.2.refs_0_), channel_id=1, source_target_pairs={{0,1},{1,0},{2,3},{3,2},{4,5},{5,4},{6,7},{7,6},{8,9},{9,8},{10,11... | collective-permute-start | bytes 552968 | tf_op jit(solution)/shard_map/cond/branch_1_fun/ppermute | solution.py:394
  41.2 2.5 %collective-permute-done.4.refs_2_ = bf16[5,144,128]{2,1,0:T(8,128)(2,1)S(1)} collective-permute-done((bf16[5,144,128]{2,1,0:T(8,128)(2,1)S(1)}, bf16[5,144,128]{2,1,0:T(8,128)(2,1)S(1)}, u32[]{:S(2)}, u32[]{:S(2)}) %collective-permute-start.4) | collective-permute-done | bytes 184352 | tf_op jit(solution)/shard_map/cond/branch_1_fun/ppermute | solution.py:393
  43.7 2.8 %collective-permute-start.5 = (bf16[5,144,128]{2,1,0:T(8,128)(2,1)S(1)}, bf16[5,144,128]{2,1,0:T(8,128)(2,1)S(1)}, u32[]{:S(2)}, u32[]{:S(2)}) collective-permute-start(bf16[5,144,128]{2,1,0:T(8,128)(2,1)S(1)} %collective-permute-done.4.refs_2_), channel_id=1, source_target_pairs={{0,1},{1,0},{2,3},{3,2},{4,5},{5,4},{6,7},{7,6},{8,9},{9,8},{10,11... | collective-permute-start | bytes 552968 | tf_op jit(solution)/shard_map/cond/branch_1_fun/ppermute | solution.py:395
  47.5 2.1 %branch_1_fun.3 = bf16[256,128]{1,0:T(8,128)(2,1)S(1)} custom-call(s32[16,16]{1,0:T(8,128)S(1)} %get-tuple-element.33.mask, bf16[256,576]{1,0:T(8,128)(2,1)} %get-tuple-element.34.queries, bf16[576,120]{1,0:T(8,128)(2,1)S(1)} %get-tuple-element.35.own, bf16[2,512,128]{2,1,0:T(8,128)(2,1)S(1)} %get-tuple-element.36.up, ...), custom_call_target="tpu_custom_call" | custom-call | tf_op jit(solution)/shard_map/cond/branch_1_fun/pallas_call | solution.py:396
  49.6 2.3 %collective-permute-start.10 = (bf16[256,128]{1,0:T(8,128)(2,1)S(1)}, bf16[256,128]{1,0:T(8,128)(2,1)S(1)}, u32[]{:S(2)}, u32[]{:S(2)}) collective-permute-start(bf16[256,128]{1,0:T(8,128)(2,1)S(1)} %get-tuple-element.156.mine), channel_id=1, source_target_pairs={{0,1},{1,0},{2,3},{3,2},{4,5},{5,4},{6,7},{7,6},{8,9},{9,8},{10,11... | collective-permute-start | bytes 196616 | tf_op jit(solution)/shard_map/ppermute | solution.py:419
  54.0 10.4 %all-to-all-start.1 = ((bf16[16,80,128]{2,1,0:T(8,128)(2,1)}), bf16[16,80,128]{2,1,0:T(8,128)(2,1)S(1)}, u32[]{:S(2)}, u32[]{:S(2)}) async-start(bf16[16,80,128]{2,1,0:T(8,128)(2,1)} %shard_map.131), calls=%async_computation.1 | async-start | bytes 655360 | tf_op jit(solution)/shard_map/all_to_all | solution.py:314
  64.4 2.5 %collective-permute-start.11 = (bf16[3,80,576]{2,1,0:T(8,128)(2,1)}, bf16[3,80,576]{2,1,0:T(8,128)(2,1)S(1)}, u32[]{:S(2)}, u32[]{:S(2)}) collective-permute-start(bf16[3,80,576]{2,1,0:T(8,128)(2,1)} %get-tuple-element.135), channel_id=1, source_target_pairs={{0,1},{1,0},{2,3},{3,2},{4,5},{5,4},{6,7},{7,6},{8,9},{9,8},{10,11... | collective-permute-start | bytes 829448 | tf_op jit(solution)/shard_map/ppermute | solution.py:369
  67.0 3.5 %collective-permute-start.12 = (bf16[3,80,576]{2,1,0:T(8,128)(2,1)}, bf16[3,80,576]{2,1,0:T(8,128)(2,1)S(1)}, u32[]{:S(2)}, u32[]{:S(2)}) collective-permute-start(bf16[3,80,576]{2,1,0:T(8,128)(2,1)} %get-tuple-element.138), channel_id=1, source_target_pairs={{0,4},{1,5},{2,6},{3,7},{4,0},{5,1},{6,2},{7,3},{8,12},{9,13},{10,... | collective-permute-start | bytes 829448 | tf_op jit(solution)/shard_map/ppermute | solution.py:369
  72.5 4.5 %collective-permute-start.14 = (bf16[3,80,576]{2,1,0:T(8,128)(2,1)}, bf16[3,80,576]{2,1,0:T(8,128)(2,1)S(1)}, u32[]{:S(2)}, u32[]{:S(2)}) collective-permute-start(bf16[3,80,576]{2,1,0:T(8,128)(2,1)} %copy-done.22), channel_id=1, source_target_pairs={{0,7},{1,6},{2,5},{3,4},{4,3},{5,2},{6,1},{7,0},{8,15},{9,14},{10,... | collective-permute-start | bytes 829448 | tf_op jit(solution)/shard_map/ppermute | solution.py:369
  77.4 20.1 %all_to_all.40 = bf16[16,32,128]{2,1,0:T(8,128)(2,1)S(1)} all-to-all(bf16[16,32,128]{2,1,0:T(8,128)(2,1)S(1)} %bitcast.20), channel_id=1, replica_groups=mesh['y'=8,'xh'=2,'za'=4,'zb'=2,'xl'=2,'core'=2] {'y','xh'}, dimensions={0} | all-to-all | bytes 262144 | tf_op jit(solution)/shard_map/all_to_all | solution.py:314
  100.1 6.9 %all-to-all-start.3 = ((bf16[8,88,512]{2,1,0:T(8,128)(2,1)}), bf16[8,88,512]{2,1,0:T(8,128)(2,1)S(1)}, u32[]{:S(2)}, u32[]{:S(2)}) async-start(bf16[8,88,512]{2,1,0:T(8,128)(2,1)} %get-tuple-element.142), calls=%async_computation.3 | async-start | bytes 1441792 | tf_op jit(solution)/shard_map/all_to_all | solution.py:314
  114.4 2.8 %all-to-all-done.3.inputs = bf16[8,88,512]{2,1,0:T(8,128)(2,1)S(1)} async-done(((bf16[8,88,512]{2,1,0:T(8,128)(2,1)}), bf16[8,88,512]{2,1,0:T(8,128)(2,1)S(1)}, u32[]{:S(2)}, u32[]{:S(2)}) %all-to-all-start.3) | async-done | bytes 720928 | tf_op jit(solution)/shard_map/all_to_all | solution.py:314
  118.3 16.0 %all_to_all.41.got = bf16[4,104,512]{2,1,0:T(8,128)(2,1)S(1)} all-to-all(bf16[4,104,512]{2,1,0:T(8,128)(2,1)S(1)} %shard_map.135), channel_id=1, replica_groups=mesh['y'=8,'xh'=2,'za'=4,'zb'=2,'xl'=2,'core'=2] {'za'}, dimensions={0} | all-to-all | bytes 851968 | tf_op jit(solution)/shard_map/all_to_all | solution.py:314
  134.4 12.5 %all_to_all.42.acts = bf16[4,48,512]{2,1,0:T(8,128)(2,1)S(1)} all-to-all(bf16[4,48,512]{2,1,0:T(8,128)(2,1)S(1)} %shard_map.136), channel_id=1, replica_groups=mesh['y'=8,'xh'=2,'za'=4,'zb'=2,'xl'=2,'core'=2] {'za'}, dimensions={0} | all-to-all | bytes 393216 | tf_op jit(solution)/shard_map/all_to_all | solution.py:314
  148.1 15.6 %all_to_all.43.got = bf16[8,80,512]{2,1,0:T(8,128)(2,1)S(1)} all-to-all(bf16[8,80,512]{2,1,0:T(8,128)(2,1)S(1)} %shard_map.137), channel_id=1, replica_groups=mesh['y'=8,'xh'=2,'za'=4,'zb'=2,'xl'=2,'core'=2] {'zb','xl','core'}, dimensions={0} | all-to-all | bytes 1310720 | tf_op jit(solution)/shard_map/all_to_all | solution.py:314
  163.8 16.3 %all_to_all.44 = bf16[16,32,128]{2,1,0:T(8,128)(2,1)S(1)} all-to-all(bf16[16,32,128]{2,1,0:T(8,128)(2,1)S(1)} %bitcast.18), channel_id=1, replica_groups=mesh['y'=8,'xh'=2,'za'=4,'zb'=2,'xl'=2,'core'=2] {'y','xh'}, dimensions={0} | all-to-all | bytes 262144 | tf_op jit(solution)/shard_map/all_to_all | solution.py:314
  (88 shorter events, 27.9 us)
Async XLA Ops:
  1.9 16.3 %copy-start = (bf16[256,2560]{1,0:T(8,128)(2,1)S(1)}, bf16[256,2560]{1,0:T(8,128)(2,1)}, u32[]{:S(2)}) copy-start(bf16[256,2560]{1,0:T(8,128)(2,1)} %weights) | copy-start | bytes 3932164
  1.9 31.7 %all-to-all-start = ((bf16[16,144,128]{2,1,0:T(8,128)(2,1)}), bf16[16,144,128]{2,1,0:T(8,128)(2,1)}, u32[]{:S(2)}, u32[]{:S(2)}) async-start(bf16[16,144,128]{2,1,0:T(8,128)(2,1)} %shard_map.127), calls=%async_computation | async-start | bytes 1179648 | tf_op jit(solution)/shard_map/all_to_all | solution.py:314
  15.9 16.2 %copy-start.25 = (s32[16,16]{1,0:T(8,128)S(1)}, s32[16,16]{1,0:T(8,128)}, u32[]{:S(2)}) copy-start(s32[16,16]{1,0:T(8,128)} %param.17) | copy-start | bytes 3076
  15.9 17.6 %copy-start.26 = (bf16[120,80]{0,1:T(8,128)(2,1)S(1)}, bf16[120,80]{0,1:T(8,128)(2,1)}, u32[]{:S(2)}) copy-start(bf16[120,80]{0,1:T(8,128)(2,1)} %param.20) | copy-start | bytes 57604
  15.9 17.7 %copy-start.27 = (bf16[80]{0:T(256)(128)(2,1)S(1)}, bf16[80]{0:T(256)(128)(2,1)}, u32[]{:S(2)}) copy-start(bf16[80]{0:T(256)(128)(2,1)} %param.21) | copy-start | bytes 484
  18.2 15.4 %copy-start.23 = (bf16[120,576]{0,1:T(8,128)(2,1)S(1)}, bf16[120,576]{0,1:T(8,128)(2,1)}, u32[]{:S(2)}) copy-start(bf16[120,576]{0,1:T(8,128)(2,1)} %param.16) | copy-start | bytes 414724
  18.2 15.4 %copy-start.24 = (bf16[2,512,128]{2,1,0:T(8,128)(2,1)S(1)}, bf16[2,512,128]{2,1,0:T(8,128)(2,1)}, u32[]{:S(2)}) copy-start(bf16[2,512,128]{2,1,0:T(8,128)(2,1)} %param.18) | copy-start | bytes 786436
  19.8 13.8 %collective-permute-start.6 = (bf16[16,80,256]{2,1,0:T(8,128)(2,1)}, bf16[16,80,256]{2,1,0:T(8,128)(2,1)S(1)}, u32[]{:S(2)}, u32[]{:S(2)}) collective-permute-start(bf16[16,80,256]{2,1,0:T(8,128)(2,1)} %get-tuple-element.111), channel_id=1, source_target_pairs={{0,1},{1,0},{2,3},{3,2},{4,5},{5,4},{6,7},{7,6},{8,9},{9,8},{10,11... | collective-permute-start | bytes 1966088 | tf_op jit(solution)/shard_map/ppermute | solution.py:382
  22.6 27.0 %collective-permute-start.7 = (bf16[3,80,576]{2,1,0:T(8,128)(2,1)}, bf16[3,80,576]{2,1,0:T(8,128)(2,1)S(1)}, u32[]{:S(2)}, u32[]{:S(2)}) collective-permute-start(bf16[3,80,576]{2,1,0:T(8,128)(2,1)} %get-tuple-element.117), channel_id=1, source_target_pairs={{0,2},{1,3},{2,0},{3,1},{4,6},{5,7},{6,4},{7,5},{8,10},{9,11},{10,... | collective-permute-start | bytes 829448 | tf_op jit(solution)/shard_map/ppermute | solution.py:369
  24.9 24.7 %collective-permute-start.8 = (bf16[3,80,576]{2,1,0:T(8,128)(2,1)}, bf16[3,80,576]{2,1,0:T(8,128)(2,1)S(1)}, u32[]{:S(2)}, u32[]{:S(2)}) collective-permute-start(bf16[3,80,576]{2,1,0:T(8,128)(2,1)} %get-tuple-element.118), channel_id=1, source_target_pairs={{0,3},{1,2},{2,1},{3,0},{4,7},{5,6},{6,5},{7,4},{8,11},{9,10},{10,... | collective-permute-start | bytes 829448 | tf_op jit(solution)/shard_map/ppermute | solution.py:369
  28.1 21.5 %collective-permute-start.9 = (bf16[3,80,576]{2,1,0:T(8,128)(2,1)}, bf16[3,80,576]{2,1,0:T(8,128)(2,1)S(1)}, u32[]{:S(2)}, u32[]{:S(2)}) collective-permute-start(bf16[3,80,576]{2,1,0:T(8,128)(2,1)} %get-tuple-element.119), channel_id=1, source_target_pairs={{0,6},{1,7},{2,4},{3,5},{4,2},{5,3},{6,0},{7,1},{8,14},{9,15},{10,... | collective-permute-start | bytes 829448 | tf_op jit(solution)/shard_map/ppermute | solution.py:369
  35.0 8.6 %collective-permute-start.4 = (bf16[5,144,128]{2,1,0:T(8,128)(2,1)S(1)}, bf16[5,144,128]{2,1,0:T(8,128)(2,1)S(1)}, u32[]{:S(2)}, u32[]{:S(2)}) collective-permute-start(bf16[5,144,128]{2,1,0:T(8,128)(2,1)S(1)} %branch_1_fun.2.refs_0_), channel_id=1, source_target_pairs={{0,4},{4,0},{1,5},{5,1},{2,6},{6,2},{3,7},{7,3},{8,12},{12,8},{9,1... | collective-permute-start | bytes 552968 | tf_op jit(solution)/shard_map/cond/branch_1_fun/ppermute | solution.py:393
  37.0 9.5 %collective-permute-start.3 = (bf16[5,144,128]{2,1,0:T(8,128)(2,1)S(1)}, bf16[5,144,128]{2,1,0:T(8,128)(2,1)S(1)}, u32[]{:S(2)}, u32[]{:S(2)}) collective-permute-start(bf16[5,144,128]{2,1,0:T(8,128)(2,1)S(1)} %branch_1_fun.2.refs_0_), channel_id=1, source_target_pairs={{0,1},{1,0},{2,3},{3,2},{4,5},{5,4},{6,7},{7,6},{8,9},{9,8},{10,11... | collective-permute-start | bytes 552968 | tf_op jit(solution)/shard_map/cond/branch_1_fun/ppermute | solution.py:394
  43.7 3.8 %collective-permute-start.5 = (bf16[5,144,128]{2,1,0:T(8,128)(2,1)S(1)}, bf16[5,144,128]{2,1,0:T(8,128)(2,1)S(1)}, u32[]{:S(2)}, u32[]{:S(2)}) collective-permute-start(bf16[5,144,128]{2,1,0:T(8,128)(2,1)S(1)} %collective-permute-done.4.refs_2_), channel_id=1, source_target_pairs={{0,1},{1,0},{2,3},{3,2},{4,5},{5,4},{6,7},{7,6},{8,9},{9,8},{10,11... | collective-permute-start | bytes 552968 | tf_op jit(solution)/shard_map/cond/branch_1_fun/ppermute | solution.py:395
  49.6 27.8 %copy-start.4 = (bf16[3,80,576]{2,1,0:T(8,128)(2,1)}, bf16[3,80,576]{2,1,0:T(8,128)(2,1)S(1)}, u32[]{:S(2)}) copy-start(bf16[3,80,576]{2,1,0:T(8,128)(2,1)S(1)} %collective-permute-done.7.refs_2_) | copy-start | bytes 829444
  49.6 27.8 %copy-start.6 = (bf16[3,80,576]{2,1,0:T(8,128)(2,1)}, bf16[3,80,576]{2,1,0:T(8,128)(2,1)S(1)}, u32[]{:S(2)}) copy-start(bf16[3,80,576]{2,1,0:T(8,128)(2,1)S(1)} %collective-permute-done.8.refs_3_) | copy-start | bytes 829444
  49.6 27.8 %copy-start.8 = (bf16[3,80,576]{2,1,0:T(8,128)(2,1)}, bf16[3,80,576]{2,1,0:T(8,128)(2,1)S(1)}, u32[]{:S(2)}) copy-start(bf16[3,80,576]{2,1,0:T(8,128)(2,1)S(1)} %collective-permute-done.9.refs_6_) | copy-start | bytes 829444
  49.6 3.2 %collective-permute-start.10 = (bf16[256,128]{1,0:T(8,128)(2,1)S(1)}, bf16[256,128]{1,0:T(8,128)(2,1)S(1)}, u32[]{:S(2)}, u32[]{:S(2)}) collective-permute-start(bf16[256,128]{1,0:T(8,128)(2,1)S(1)} %get-tuple-element.156.mine), channel_id=1, source_target_pairs={{0,1},{1,0},{2,3},{3,2},{4,5},{5,4},{6,7},{7,6},{8,9},{9,8},{10,11... | collective-permute-start | bytes 196616 | tf_op jit(solution)/shard_map/ppermute | solution.py:419
  54.0 23.1 %all-to-all-start.1 = ((bf16[16,80,128]{2,1,0:T(8,128)(2,1)}), bf16[16,80,128]{2,1,0:T(8,128)(2,1)S(1)}, u32[]{:S(2)}, u32[]{:S(2)}) async-start(bf16[16,80,128]{2,1,0:T(8,128)(2,1)} %shard_map.131), calls=%async_computation.1 | async-start | bytes 655360 | tf_op jit(solution)/shard_map/all_to_all | solution.py:314
  64.4 34.0 %collective-permute-start.11 = (bf16[3,80,576]{2,1,0:T(8,128)(2,1)}, bf16[3,80,576]{2,1,0:T(8,128)(2,1)S(1)}, u32[]{:S(2)}, u32[]{:S(2)}) collective-permute-start(bf16[3,80,576]{2,1,0:T(8,128)(2,1)} %get-tuple-element.135), channel_id=1, source_target_pairs={{0,1},{1,0},{2,3},{3,2},{4,5},{5,4},{6,7},{7,6},{8,9},{9,8},{10,11... | collective-permute-start | bytes 829448 | tf_op jit(solution)/shard_map/ppermute | solution.py:369
  67.0 32.2 %collective-permute-start.12 = (bf16[3,80,576]{2,1,0:T(8,128)(2,1)}, bf16[3,80,576]{2,1,0:T(8,128)(2,1)S(1)}, u32[]{:S(2)}, u32[]{:S(2)}) collective-permute-start(bf16[3,80,576]{2,1,0:T(8,128)(2,1)} %get-tuple-element.138), channel_id=1, source_target_pairs={{0,4},{1,5},{2,6},{3,7},{4,0},{5,1},{6,2},{7,3},{8,12},{9,13},{10,... | collective-permute-start | bytes 829448 | tf_op jit(solution)/shard_map/ppermute | solution.py:369
  70.5 28.7 %collective-permute-start.13 = (bf16[3,80,576]{2,1,0:T(8,128)(2,1)}, bf16[3,80,576]{2,1,0:T(8,128)(2,1)S(1)}, u32[]{:S(2)}, u32[]{:S(2)}) collective-permute-start(bf16[3,80,576]{2,1,0:T(8,128)(2,1)} %get-tuple-element.139), channel_id=1, source_target_pairs={{0,5},{1,4},{2,7},{3,6},{4,1},{5,0},{6,3},{7,2},{8,13},{9,12},{10,... | collective-permute-start | bytes 829448 | tf_op jit(solution)/shard_map/ppermute | solution.py:369
  72.5 26.8 %collective-permute-start.14 = (bf16[3,80,576]{2,1,0:T(8,128)(2,1)}, bf16[3,80,576]{2,1,0:T(8,128)(2,1)S(1)}, u32[]{:S(2)}, u32[]{:S(2)}) collective-permute-start(bf16[3,80,576]{2,1,0:T(8,128)(2,1)} %copy-done.22), channel_id=1, source_target_pairs={{0,7},{1,6},{2,5},{3,4},{4,3},{5,2},{6,1},{7,0},{8,15},{9,14},{10,... | collective-permute-start | bytes 829448 | tf_op jit(solution)/shard_map/ppermute | solution.py:369
  100.1 17.0 %all-to-all-start.3 = ((bf16[8,88,512]{2,1,0:T(8,128)(2,1)}), bf16[8,88,512]{2,1,0:T(8,128)(2,1)S(1)}, u32[]{:S(2)}, u32[]{:S(2)}) async-start(bf16[8,88,512]{2,1,0:T(8,128)(2,1)} %get-tuple-element.142), calls=%async_computation.3 | async-start | bytes 1441792 | tf_op jit(solution)/shard_map/all_to_all | solution.py:314
  (19 other events, 51.6 us)

commit v9 on v8

--- a/solution.py
+++ b/solution.py
@@ -53,7 +53,10 @@
 def spread_keys(keys, out):
     count, part, _ = out.shape
     rows = keys.shape[1]
-    own = keys[pl.ds(pl.multiple_of(lax.axis_index(PAIR) * part, part), part), :]
+    column = lax.axis_index(PAIR)
+    own = keys[:part]
+    for i in range(1, keys.shape[0] // part):
+        own = jnp.where(column == i, keys[i * part : (i + 1) * part], own)
     own = jnp.concatenate([own, jnp.zeros((part, TOK - rows), BF16)], axis=1)
     for i in range(count):
         out[i] = own
@@ -214,8 +217,7 @@
     weight[...] = jnp.concatenate(picked, axis=0)
 
 
-def pack(gate, up, down, *refs):
-    outs, held = refs[:-1], refs[-1]
+def pack(gate, up, down, mine, swapped, far_x, far_z, far_xz, held):
     count = held.shape[0]
     part = gate.shape[2] // count
     for pair in range(held.shape[1]):
@@ -226,18 +228,32 @@
                 pieces += [gate[expert, :, span], up[expert, :, span]]
             pieces += [down[2 * pair, :, span], down[2 * pair + 1, :, span]]
             held[near, pair] = jnp.concatenate(pieces, axis=1)
-    for flip in range(count):
-        outs[flip][...] = held[lax.axis_index(NEAR) ^ flip]
-
-
-def unpack(part, *refs):
-    got, into, back = refs[:-2], refs[-2], refs[-1]
-    pairs = got[0].shape[0]
+    near = lax.axis_index(NEAR)
+    mine[...] = held[near]
+    swapped[...] = held[near ^ 1]
+    for out, flip in ((far_x, 2), (far_z, 4), (far_xz, 6)):
+        out[0] = held[near ^ flip]
+        out[1] = held[near ^ flip ^ 1]
+
+
+def gather_swap(swapped, far_x, far_z, far_xz, low, high):
+    low[0] = swapped[...]
+    low[1] = far_x[1]
+    high[0] = far_z[1]
+    high[1] = far_xz[1]
+
+
+def unpack(part, mine, far_x, far_z, far_xz, low, high, into, back):
+    pairs = mine.shape[0]
     for pair in range(pairs):
-        wide = jnp.concatenate([g[pair, :, : 4 * part] for g in got], axis=0)
+        rows = []
+        for i, own in enumerate((mine, far_x, far_z, far_xz)):
+            rows.append(own[pair] if i == 0 else own[0, pair])
+            rows.append((low, low, high, high)[i][i % 2, pair])
+        wide = jnp.concatenate([row[:, : 4 * part] for row in rows], axis=0)
         into[pair * 4 * part : (pair + 1) * 4 * part, :] = wide.T
-    for flip, g in enumerate(got):
-        back[flip] = jnp.concatenate([g[pair, :, 4 * part :] for pair in range(pairs)], axis=1)
+        for flip, row in enumerate(rows):
+            back[flip, :, pair * 2 * part : (pair + 1) * 2 * part] = row[:, 4 * part :]
 
 
 def project_up(run, sub, inputs, weights, keep, out):
@@ -357,19 +373,18 @@
 
     pairs = local_experts // 2
     block = (pairs, run, 6 * part)
-    w_gate, places, slot_shares = lax.optimization_barrier((w_gate, places, slot_shares))
-    packed = call(
+    mine, swapped, *far = call(
         pack,
-        [shape(block)] * near_count,
+        [shape(block)] * 2 + [shape((2,) + block)] * 3,
         [VMEM] * 3,
         [pltpu.VMEM((near_count,) + block, BF16)],
     )(w_gate, w_up, w_down.transpose(0, 2, 1))
+    out_proj, *far = lax.optimization_barrier((out_proj, *far))
 
     def flipped(x, flip):
         return lax.ppermute(x, NEAR, [(a, a ^ flip) for a in range(near_count)])
 
-    out_proj, *packed = lax.optimization_barrier((out_proj, *packed))
-    moved = {i: flipped(packed[i], i) for i in (2, 3, 6)}
+    far = [flipped(x, flip) for x, flip in zip(far, (2, 4, 6))]
 
     runs = D // run
     depth = heads * value_width
@@ -415,15 +430,16 @@
         turned_keys,
         value_up,
     )
-    values, moved = lax.optimization_barrier((values, moved))
     other_values = lax.ppermute(values, "core", [(0, 1), (1, 0)])
     summed = call(project_out, shape((runs // 2, run, TOK)), [VMEM] * 4)(
         values, other_values, out_mine, out_theirs
     )
-    summed, *late = lax.optimization_barrier((summed, packed[7], packed[4], packed[5], packed[1]))
+    summed, swapped = lax.optimization_barrier((summed, swapped))
     parts = exchange(summed, ZX)
-    for flip, x in zip((7, 4, 5, 1), late):
-        moved[flip] = flipped(x, flip)
+    swap = [
+        flipped(x, 1)
+        for x in call(gather_swap, [shape((2,) + block)] * 2, [VMEM] * 4)(swapped, *far)
+    ]
 
     hidden, sent = call(make_rows, [shape((run, TOK)), shape((slots, TOK))], [VMEM] * 5)(
         parts,
@@ -433,7 +449,6 @@
         slot_shares,
     )
     got = exchange(sent.reshape(ctx_count, SLOT, TOK), CTX).reshape(slots, TOK)
-    moved = [packed[0]] + [moved[flip] for flip in range(1, near_count)]
     spread, keep, pick_weight = call(
         functools.partial(spread_rows, run + 8, first_share),
         [
@@ -443,7 +458,7 @@
         ],
         [VMEM],
     )(got)
-    spread, moved = lax.optimization_barrier((spread, moved))
+    spread, swap = lax.optimization_barrier((spread, swap))
     inputs = exchange(spread, NEAR)
     weights_in, weights_back = call(
         functools.partial(unpack, part),
@@ -451,8 +466,8 @@
             shape((pairs * 4 * part, near_count * run)),
             shape((near_count, run, local_experts * part)),
         ],
-        [VMEM] * near_count,
-    )(*moved)
+        [VMEM] * 6,
+    )(mine, *far, *swap)
     partial_sums = call(
         functools.partial(project_up, run, sub),
         shape((far_count, 4 * sub + 8, slots)),

time: 182 us -> 192 us (1.055)
  waiting for transfers between devices: 7.17 us -> 29.6 us
  starting transfers between devices: 63.7 us -> 57.3 us
  blocking collectives: 80.4 us -> 75.2 us
  local copies, waits for them, and re-layouts: 11.7 us -> 6.82 us
  Pallas kernels: 16 us -> 19.9 us
    ppermute x1, waiting for transfers between devices: 2.45 us -> 16.6 us  [attention(): across = lax.ppermute(picked, 'zb', [(0, 1), (1, 0)])]
    ppermute x7 -> x5, starting transfers between devices: 22 us -> 13.5 us  [flipped(): return lax.ppermute(x, NEAR, [(a, a ^ flip) for a in range(near_count)])]
    all_to_all x3, waiting for transfers between devices: 2.79 us -> 10.9 us  [exchange(): return lax.all_to_all(x, axes, split_axis=0, concat_axis=0, tiled=True)]
    all_to_all x5, blocking collectives: 80.4 us -> 75.2 us  [exchange(): return lax.all_to_all(x, axes, split_axis=0, concat_axis=0, tiled=True)]
    unnamed x56 -> x42, local copies, waits for them, and re-layouts: 11.6 us -> 6.71 us
  transfers between devices with their start and end apart: 15 -> 13, of which waited for: 4 -> 5; matrix products, arithmetic and copies ran while one was open for 0% -> 0% of each run, Pallas kernels for 5% -> 8%
where the time goes in v9:
time: 192 us; the launch traced here: 191 us
  blocking collectives  75.2 us (39%)
  starting transfers between devices  57.3 us (30%)
  waiting for transfers between devices  29.6 us (15%)
  Pallas kernels  19.9 us (10%)
  local copies, waits for them, and re-layouts  6.82 us (4%)
    all_to_all x5, blocking collectives, exchange(): return lax.all_to_all(x, axes, split_axis=0, concat_axis=0, tiled=True)  75.2 us
    all_to_all x3, starting transfers between devices, exchange(): return lax.all_to_all(x, axes, split_axis=0, concat_axis=0, tiled=True)  27.5 us
    ppermute x1, waiting for transfers between devices, attention(): across = lax.ppermute(picked, 'zb', [(0, 1), (1, 0)])  16.6 us
    ppermute x5, starting transfers between devices, flipped(): return lax.ppermute(x, NEAR, [(a, a ^ flip) for a in range(near_count)])  13.5 us
    all_to_all x3, waiting for transfers between devices, exchange(): return lax.all_to_all(x, axes, split_axis=0, concat_axis=0, tiled=True)  10.9 us
    unnamed x42, local copies, waits for them, and re-layouts  6.71 us
    ppermute x1, starting transfers between devices, attention(): beside = lax.ppermute(picked, 'core', [(0, 1), (1, 0)])  5.01 us
  transfers between devices with their start and end apart: 13, of which 5 were waited for; matrix products, arithmetic and copies ran while one was open for 0% of the time, Pallas kernels for 8%

profile of v9, /device:TPU:1, one launch (start us, length us, event | category | flops | bytes accessed | tf_op | source)
XLA Modules:
  0.0 190.7 jit_solution(15798783719419421044)
XLA Ops:
  1.9 10.4 %all-to-all-start = ((bf16[16,144,128]{2,1,0:T(8,128)(2,1)}), bf16[16,144,128]{2,1,0:T(8,128)(2,1)}, u32[]{:S(2)}, u32[]{:S(2)}) async-start(bf16[16,144,128]{2,1,0:T(8,128)(2,1)} %shard_map.127), calls=%async_computation | async-start | bytes 1179648 | tf_op jit(solution)/shard_map/all_to_all | solution.py:330
  13.5 2.3 %shard_map.128 = (bf16[3,80,576]{2,1,0:T(8,128)(2,1)S(1)}, bf16[3,80,576]{2,1,0:T(8,128)(2,1)S(1)}, bf16[2,3,80,576]{3,2,1,0:T(8,128)(2,1)}, bf16[2,3,80,576]{3,2,1,0:T(8,128)(2,1)}, bf16[2,3,80,576]{3,2,1,0:T(8,128)(2,1)}) custom-call(bf16[6,80,768]{2,1,0:T(8,128)(2,1)S(1)} %copy-done.3, bf16[6,80,768]{2,1,0:T(8,128)(2,1)S(1)} %copy-done.4, ...), custom_call_target="tpu_custom_call" | custom-call | tf_op jit(solution)/shard_map/pallas_call | solution.py:376
  17.4 2.8 %collective-permute-start.6 = (bf16[16,80,256]{2,1,0:T(8,128)(2,1)}, bf16[16,80,256]{2,1,0:T(8,128)(2,1)S(1)}, u32[]{:S(2)}, u32[]{:S(2)}) collective-permute-start(bf16[16,80,256]{2,1,0:T(8,128)(2,1)} %get-tuple-element.81), channel_id=1, source_target_pairs={{0,1},{1,0},{2,3},{3,2},{4,5},{5,4},{6,7},{7,6},{8,9},{9,8},{10,11... | collective-permute-start | bytes 1966088 | tf_op jit(solution)/shard_map/ppermute | solution.py:397
  20.2 2.2 %collective-permute-start.8 = (bf16[2,3,80,576]{3,2,1,0:T(8,128)(2,1)}, bf16[2,3,80,576]{3,2,1,0:T(8,128)(2,1)S(1)}, u32[]{:S(2)}, u32[]{:S(2)}) collective-permute-start(bf16[2,3,80,576]{3,2,1,0:T(8,128)(2,1)} %get-tuple-element.98), channel_id=1, source_target_pairs={{0,2},{1,3},{2,0},{3,1},{4,6},{5,7},{6,4},{7,5},{8,10},{9,11},{10,... | collective-permute-start | bytes 1658888 | tf_op jit(solution)/shard_map/ppermute | solution.py:385
  22.4 4.0 %collective-permute-start.9 = (bf16[2,3,80,576]{3,2,1,0:T(8,128)(2,1)}, bf16[2,3,80,576]{3,2,1,0:T(8,128)(2,1)S(1)}, u32[]{:S(2)}, u32[]{:S(2)}) collective-permute-start(bf16[2,3,80,576]{3,2,1,0:T(8,128)(2,1)} %get-tuple-element.99), channel_id=1, source_target_pairs={{0,4},{1,5},{2,6},{3,7},{4,0},{5,1},{6,2},{7,3},{8,12},{9,13},{10,... | collective-permute-start | bytes 1658888 | tf_op jit(solution)/shard_map/ppermute | solution.py:385
  26.4 2.8 %collective-permute-start.10 = (bf16[2,3,80,576]{3,2,1,0:T(8,128)(2,1)}, bf16[2,3,80,576]{3,2,1,0:T(8,128)(2,1)S(1)}, u32[]{:S(2)}, u32[]{:S(2)}) collective-permute-start(bf16[2,3,80,576]{3,2,1,0:T(8,128)(2,1)} %get-tuple-element.100), channel_id=1, source_target_pairs={{0,6},{1,7},{2,4},{3,5},{4,2},{5,3},{6,0},{7,1},{8,14},{9,15},{10,... | collective-permute-start | bytes 1658888 | tf_op jit(solution)/shard_map/ppermute | solution.py:385
  31.2 33.2 %conditional.1 = (bf16[256,128]{1,0:T(8,128)(2,1)}) conditional(s32[]{:T(128)} %convert_element_type.6, (s32[16,16]{1,0:T(8,128)S(1)}, bf16[16,144,128]{2,1,0:T(8,128)(2,1)}, bf16[256,576]{1,0:T(8,128)(2,1)}, bf16[576,120]{1,0:T(8,128)(2,1)}, bf16[2,512,128]{2,1,0:T(8,128)(2,1)}) %tuple.24, (s32[16,16]{1,0:T(8,128)S(1)}, ...), branch_computations={%region_2.3_spmd, %region_3.4_spmd} | conditional | bytes 6635648 | solution.py:423
  32.6 3.6 %collective-permute-start.4 = (bf16[5,144,128]{2,1,0:T(8,128)(2,1)S(1)}, bf16[5,144,128]{2,1,0:T(8,128)(2,1)S(1)}, u32[]{:S(2)}, u32[]{:S(2)}) collective-permute-start(bf16[5,144,128]{2,1,0:T(8,128)(2,1)S(1)} %branch_1_fun.2.refs_0_), channel_id=1, source_target_pairs={{0,4},{4,0},{1,5},{5,1},{2,6},{6,2},{3,7},{7,3},{8,12},{12,8},{9,1... | collective-permute-start | bytes 552968 | tf_op jit(solution)/shard_map/cond/branch_1_fun/ppermute | solution.py:408
  36.2 5.0 %collective-permute-start.3 = (bf16[5,144,128]{2,1,0:T(8,128)(2,1)S(1)}, bf16[5,144,128]{2,1,0:T(8,128)(2,1)S(1)}, u32[]{:S(2)}, u32[]{:S(2)}) collective-permute-start(bf16[5,144,128]{2,1,0:T(8,128)(2,1)S(1)} %branch_1_fun.2.refs_0_), channel_id=1, source_target_pairs={{0,1},{1,0},{2,3},{3,2},{4,5},{5,4},{6,7},{7,6},{8,9},{9,8},{10,11... | collective-permute-start | bytes 552968 | tf_op jit(solution)/shard_map/cond/branch_1_fun/ppermute | solution.py:409
  41.2 16.6 %collective-permute-done.4.refs_2_ = bf16[5,144,128]{2,1,0:T(8,128)(2,1)S(1)} collective-permute-done((bf16[5,144,128]{2,1,0:T(8,128)(2,1)S(1)}, bf16[5,144,128]{2,1,0:T(8,128)(2,1)S(1)}, u32[]{:S(2)}, u32[]{:S(2)}) %collective-permute-start.4) | collective-permute-done | bytes 184352 | tf_op jit(solution)/shard_map/cond/branch_1_fun/ppermute | solution.py:408
  57.8 2.7 %collective-permute-start.5 = (bf16[5,144,128]{2,1,0:T(8,128)(2,1)S(1)}, bf16[5,144,128]{2,1,0:T(8,128)(2,1)S(1)}, u32[]{:S(2)}, u32[]{:S(2)}) collective-permute-start(bf16[5,144,128]{2,1,0:T(8,128)(2,1)S(1)} %collective-permute-done.4.refs_2_), channel_id=1, source_target_pairs={{0,1},{1,0},{2,3},{3,2},{4,5},{5,4},{6,7},{7,6},{8,9},{9,8},{10,11... | collective-permute-start | bytes 552968 | tf_op jit(solution)/shard_map/cond/branch_1_fun/ppermute | solution.py:410
  61.5 2.9 %branch_1_fun.3 = bf16[256,128]{1,0:T(8,128)(2,1)} custom-call(s32[16,16]{1,0:T(8,128)S(1)} %get-tuple-element.33.mask, bf16[256,576]{1,0:T(8,128)(2,1)} %get-tuple-element.34.queries, bf16[576,120]{1,0:T(8,128)(2,1)} %get-tuple-element.35.own, bf16[2,512,128]{2,1,0:T(8,128)(2,1)} %get-tuple-element.36.up, bf16[5,144,128]{2,1,0:T(8,128)(2,1)S(1)} %branch_1_fun.2.refs_0_, ...), custom_call_target="tpu_custom_call" | custom-call | tf_op jit(solution)/shard_map/cond/branch_1_fun/pallas_call | solution.py:411
  64.4 2.3 %collective-permute-start.7 = (bf16[256,128]{1,0:T(8,128)(2,1)}, bf16[256,128]{1,0:T(8,128)(2,1)S(1)}, u32[]{:S(2)}, u32[]{:S(2)}) collective-permute-start(bf16[256,128]{1,0:T(8,128)(2,1)} %get-tuple-element.112.mine), channel_id=1, source_target_pairs={{0,1},{1,0},{2,3},{3,2},{4,5},{5,4},{6,7},{7,6},{8,9},{9,8},{10,11... | collective-permute-start | bytes 196616 | tf_op jit(solution)/shard_map/ppermute | solution.py:433
  67.7 2.1 %shard_map.131 = bf16[16,80,128]{2,1,0:T(8,128)(2,1)} custom-call(bf16[256,128]{1,0:T(8,128)(2,1)} %get-tuple-element.112.mine, bf16[256,128]{1,0:T(8,128)(2,1)S(1)} %collective-permute-done.7.theirs, bf16[16,80,256]{2,1,0:T(8,128)(2,1)S(1)} %get-tuple-element.87.weights_mine, bf16[16,80,256]{2,1,0:T(8,128)(2,1)S(1)} %collective-permute-done.6.weights_theirs), custom_call_target="tpu_custom_call" | custom-call | tf_op jit(solution)/shard_map/pallas_call | solution.py:434
  69.8 10.4 %all-to-all-start.1 = ((bf16[16,80,128]{2,1,0:T(8,128)(2,1)}), bf16[16,80,128]{2,1,0:T(8,128)(2,1)S(1)}, u32[]{:S(2)}, u32[]{:S(2)}) async-start(bf16[16,80,128]{2,1,0:T(8,128)(2,1)} %shard_map.131), calls=%async_computation.1 | async-start | bytes 655360 | tf_op jit(solution)/shard_map/all_to_all | solution.py:330
  82.4 2.5 %collective-permute-start.11 = (bf16[2,3,80,576]{3,2,1,0:T(8,128)(2,1)}, bf16[2,3,80,576]{3,2,1,0:T(8,128)(2,1)S(1)}, u32[]{:S(2)}, u32[]{:S(2)}) collective-permute-start(bf16[2,3,80,576]{3,2,1,0:T(8,128)(2,1)} %get-tuple-element.101), channel_id=1, source_target_pairs={{0,1},{1,0},{2,3},{3,2},{4,5},{5,4},{6,7},{7,6},{8,9},{9,8},{10,11... | collective-permute-start | bytes 1658888 | tf_op jit(solution)/shard_map/ppermute | solution.py:385
  86.9 5.7 %all-to-all-done.1.parts = bf16[16,80,128]{2,1,0:T(8,128)(2,1)S(1)} async-done(((bf16[16,80,128]{2,1,0:T(8,128)(2,1)}), bf16[16,80,128]{2,1,0:T(8,128)(2,1)S(1)}, u32[]{:S(2)}, u32[]{:S(2)}) %all-to-all-start.1) | async-done | bytes 327712 | tf_op jit(solution)/shard_map/all_to_all | solution.py:330
  92.9 19.8 %all_to_all.40 = bf16[16,32,128]{2,1,0:T(8,128)(2,1)S(1)} all-to-all(bf16[16,32,128]{2,1,0:T(8,128)(2,1)S(1)} %bitcast.20), channel_id=1, replica_groups=mesh['y'=8,'xh'=2,'za'=4,'zb'=2,'xl'=2,'core'=2] {'y','xh'}, dimensions={0} | all-to-all | bytes 262144 | tf_op jit(solution)/shard_map/all_to_all | solution.py:330
  113.6 6.7 %all-to-all-start.3 = ((bf16[8,88,512]{2,1,0:T(8,128)(2,1)}), bf16[8,88,512]{2,1,0:T(8,128)(2,1)S(1)}, u32[]{:S(2)}, u32[]{:S(2)}) async-start(bf16[8,88,512]{2,1,0:T(8,128)(2,1)} %get-tuple-element.103), calls=%async_computation.3 | async-start | bytes 1441792 | tf_op jit(solution)/shard_map/all_to_all | solution.py:330
  125.2 5.3 %all-to-all-done.3.inputs = bf16[8,88,512]{2,1,0:T(8,128)(2,1)S(1)} async-done(((bf16[8,88,512]{2,1,0:T(8,128)(2,1)}), bf16[8,88,512]{2,1,0:T(8,128)(2,1)S(1)}, u32[]{:S(2)}, u32[]{:S(2)}) %all-to-all-start.3) | async-done | bytes 720928 | tf_op jit(solution)/shard_map/all_to_all | solution.py:330
  133.0 15.2 %all_to_all.41.got = bf16[4,104,512]{2,1,0:T(8,128)(2,1)S(1)} all-to-all(bf16[4,104,512]{2,1,0:T(8,128)(2,1)S(1)} %shard_map.136), channel_id=1, replica_groups=mesh['y'=8,'xh'=2,'za'=4,'zb'=2,'xl'=2,'core'=2] {'za'}, dimensions={0} | all-to-all | bytes 851968 | tf_op jit(solution)/shard_map/all_to_all | solution.py:330
  148.3 12.0 %all_to_all.42.acts = bf16[4,48,512]{2,1,0:T(8,128)(2,1)S(1)} all-to-all(bf16[4,48,512]{2,1,0:T(8,128)(2,1)S(1)} %shard_map.137), channel_id=1, replica_groups=mesh['y'=8,'xh'=2,'za'=4,'zb'=2,'xl'=2,'core'=2] {'za'}, dimensions={0} | all-to-all | bytes 393216 | tf_op jit(solution)/shard_map/all_to_all | solution.py:330
  161.4 15.6 %all_to_all.43.got = bf16[8,80,512]{2,1,0:T(8,128)(2,1)S(1)} all-to-all(bf16[8,80,512]{2,1,0:T(8,128)(2,1)S(1)} %shard_map.138), channel_id=1, replica_groups=mesh['y'=8,'xh'=2,'za'=4,'zb'=2,'xl'=2,'core'=2] {'zb','xl','core'}, dimensions={0} | all-to-all | bytes 1310720 | tf_op jit(solution)/shard_map/all_to_all | solution.py:330
  177.2 12.6 %all_to_all.44 = bf16[16,32,128]{2,1,0:T(8,128)(2,1)S(1)} all-to-all(bf16[16,32,128]{2,1,0:T(8,128)(2,1)S(1)} %bitcast.18), channel_id=1, replica_groups=mesh['y'=8,'xh'=2,'za'=4,'zb'=2,'xl'=2,'core'=2] {'y','xh'}, dimensions={0} | all-to-all | bytes 262144 | tf_op jit(solution)/shard_map/all_to_all | solution.py:330
  (71 shorter events, 24.3 us)
Async XLA Ops:
  0.0 12.3 %copy-start.4 = (bf16[6,80,768]{2,1,0:T(8,128)(2,1)S(1)}, bf16[6,80,768]{2,1,0:T(8,128)(2,1)}, u32[]{:S(2)}) copy-start(bf16[6,80,768]{2,1,0:T(8,128)(2,1)} %up.1) | copy-start | bytes 2211844
  0.0 12.3 %copy-start.3 = (bf16[6,80,768]{2,1,0:T(8,128)(2,1)S(1)}, bf16[6,80,768]{2,1,0:T(8,128)(2,1)}, u32[]{:S(2)}) copy-start(bf16[6,80,768]{2,1,0:T(8,128)(2,1)} %gate.1) | copy-start | bytes 2211844
  1.9 13.9 %copy-start.2 = (bf16[256,2560]{1,0:T(8,128)(2,1)S(1)}, bf16[256,2560]{1,0:T(8,128)(2,1)}, u32[]{:S(2)}) copy-start(bf16[256,2560]{1,0:T(8,128)(2,1)} %weights) | copy-start | bytes 3932164
  1.9 29.2 %all-to-all-start = ((bf16[16,144,128]{2,1,0:T(8,128)(2,1)}), bf16[16,144,128]{2,1,0:T(8,128)(2,1)}, u32[]{:S(2)}, u32[]{:S(2)}) async-start(bf16[16,144,128]{2,1,0:T(8,128)(2,1)} %shard_map.127), calls=%async_computation | async-start | bytes 1179648 | tf_op jit(solution)/shard_map/all_to_all | solution.py:330
  13.5 15.8 %copy-start.18 = (s32[16,16]{1,0:T(8,128)S(1)}, s32[16,16]{1,0:T(8,128)}, u32[]{:S(2)}) copy-start(s32[16,16]{1,0:T(8,128)} %param.17) | copy-start | bytes 3076
  13.5 17.2 %copy-start.19 = (bf16[120,80]{0,1:T(8,128)(2,1)S(1)}, bf16[120,80]{0,1:T(8,128)(2,1)}, u32[]{:S(2)}) copy-start(bf16[120,80]{0,1:T(8,128)(2,1)} %param.20) | copy-start | bytes 57604
  13.5 17.2 %copy-start.15 = (s32[120,3,2]{0,2,1:T(2,128)S(1)}, s32[120,3,2]{0,2,1:T(2,128)}, u32[]{:S(2)}) copy-start(s32[120,3,2]{0,2,1:T(2,128)} %param.23) | copy-start | bytes 8644
  13.5 17.2 %copy-start.16 = (s32[120,3]{0,1:T(4,128)S(1)}, s32[120,3]{0,1:T(4,128)}, u32[]{:S(2)}) copy-start(s32[120,3]{0,1:T(4,128)} %param.22) | copy-start | bytes 4324
  13.5 17.2 %copy-start.17 = (bf16[120,3,2]{0,2,1:T(2,128)(2,1)S(1)}, bf16[120,3,2]{0,2,1:T(2,128)(2,1)}, u32[]{:S(2)}) copy-start(bf16[120,3,2]{0,2,1:T(2,128)(2,1)} %param.24) | copy-start | bytes 4324
  13.5 17.6 %copy-start.20 = (bf16[80]{0:T(256)(128)(2,1)S(1)}, bf16[80]{0:T(256)(128)(2,1)}, u32[]{:S(2)}) copy-start(bf16[80]{0:T(256)(128)(2,1)} %param.21) | copy-start | bytes 484
  17.4 13.8 %collective-permute-start.6 = (bf16[16,80,256]{2,1,0:T(8,128)(2,1)}, bf16[16,80,256]{2,1,0:T(8,128)(2,1)S(1)}, u32[]{:S(2)}, u32[]{:S(2)}) collective-permute-start(bf16[16,80,256]{2,1,0:T(8,128)(2,1)} %get-tuple-element.81), channel_id=1, source_target_pairs={{0,1},{1,0},{2,3},{3,2},{4,5},{5,4},{6,7},{7,6},{8,9},{9,8},{10,11... | collective-permute-start | bytes 1966088 | tf_op jit(solution)/shard_map/ppermute | solution.py:397
  20.2 60.0 %collective-permute-start.8 = (bf16[2,3,80,576]{3,2,1,0:T(8,128)(2,1)}, bf16[2,3,80,576]{3,2,1,0:T(8,128)(2,1)S(1)}, u32[]{:S(2)}, u32[]{:S(2)}) collective-permute-start(bf16[2,3,80,576]{3,2,1,0:T(8,128)(2,1)} %get-tuple-element.98), channel_id=1, source_target_pairs={{0,2},{1,3},{2,0},{3,1},{4,6},{5,7},{6,4},{7,5},{8,10},{9,11},{10,... | collective-permute-start | bytes 1658888 | tf_op jit(solution)/shard_map/ppermute | solution.py:385
  22.4 57.8 %collective-permute-start.9 = (bf16[2,3,80,576]{3,2,1,0:T(8,128)(2,1)}, bf16[2,3,80,576]{3,2,1,0:T(8,128)(2,1)S(1)}, u32[]{:S(2)}, u32[]{:S(2)}) collective-permute-start(bf16[2,3,80,576]{3,2,1,0:T(8,128)(2,1)} %get-tuple-element.99), channel_id=1, source_target_pairs={{0,4},{1,5},{2,6},{3,7},{4,0},{5,1},{6,2},{7,3},{8,12},{9,13},{10,... | collective-permute-start | bytes 1658888 | tf_op jit(solution)/shard_map/ppermute | solution.py:385
  26.4 53.8 %collective-permute-start.10 = (bf16[2,3,80,576]{3,2,1,0:T(8,128)(2,1)}, bf16[2,3,80,576]{3,2,1,0:T(8,128)(2,1)S(1)}, u32[]{:S(2)}, u32[]{:S(2)}) collective-permute-start(bf16[2,3,80,576]{3,2,1,0:T(8,128)(2,1)} %get-tuple-element.100), channel_id=1, source_target_pairs={{0,6},{1,7},{2,4},{3,5},{4,2},{5,3},{6,0},{7,1},{8,14},{9,15},{10,... | collective-permute-start | bytes 1658888 | tf_op jit(solution)/shard_map/ppermute | solution.py:385
  32.6 25.2 %collective-permute-start.4 = (bf16[5,144,128]{2,1,0:T(8,128)(2,1)S(1)}, bf16[5,144,128]{2,1,0:T(8,128)(2,1)S(1)}, u32[]{:S(2)}, u32[]{:S(2)}) collective-permute-start(bf16[5,144,128]{2,1,0:T(8,128)(2,1)S(1)} %branch_1_fun.2.refs_0_), channel_id=1, source_target_pairs={{0,4},{4,0},{1,5},{5,1},{2,6},{6,2},{3,7},{7,3},{8,12},{12,8},{9,1... | collective-permute-start | bytes 552968 | tf_op jit(solution)/shard_map/cond/branch_1_fun/ppermute | solution.py:408
  36.2 24.3 %collective-permute-start.3 = (bf16[5,144,128]{2,1,0:T(8,128)(2,1)S(1)}, bf16[5,144,128]{2,1,0:T(8,128)(2,1)S(1)}, u32[]{:S(2)}, u32[]{:S(2)}) collective-permute-start(bf16[5,144,128]{2,1,0:T(8,128)(2,1)S(1)} %branch_1_fun.2.refs_0_), channel_id=1, source_target_pairs={{0,1},{1,0},{2,3},{3,2},{4,5},{5,4},{6,7},{7,6},{8,9},{9,8},{10,11... | collective-permute-start | bytes 552968 | tf_op jit(solution)/shard_map/cond/branch_1_fun/ppermute | solution.py:409
  57.8 3.7 %collective-permute-start.5 = (bf16[5,144,128]{2,1,0:T(8,128)(2,1)S(1)}, bf16[5,144,128]{2,1,0:T(8,128)(2,1)S(1)}, u32[]{:S(2)}, u32[]{:S(2)}) collective-permute-start(bf16[5,144,128]{2,1,0:T(8,128)(2,1)S(1)} %collective-permute-done.4.refs_2_), channel_id=1, source_target_pairs={{0,1},{1,0},{2,3},{3,2},{4,5},{5,4},{6,7},{7,6},{8,9},{9,8},{10,11... | collective-permute-start | bytes 552968 | tf_op jit(solution)/shard_map/cond/branch_1_fun/ppermute | solution.py:410
  64.4 3.4 %collective-permute-start.7 = (bf16[256,128]{1,0:T(8,128)(2,1)}, bf16[256,128]{1,0:T(8,128)(2,1)S(1)}, u32[]{:S(2)}, u32[]{:S(2)}) collective-permute-start(bf16[256,128]{1,0:T(8,128)(2,1)} %get-tuple-element.112.mine), channel_id=1, source_target_pairs={{0,1},{1,0},{2,3},{3,2},{4,5},{5,4},{6,7},{7,6},{8,9},{9,8},{10,11... | collective-permute-start | bytes 196616 | tf_op jit(solution)/shard_map/ppermute | solution.py:433
  69.8 22.8 %all-to-all-start.1 = ((bf16[16,80,128]{2,1,0:T(8,128)(2,1)}), bf16[16,80,128]{2,1,0:T(8,128)(2,1)S(1)}, u32[]{:S(2)}, u32[]{:S(2)}) async-start(bf16[16,80,128]{2,1,0:T(8,128)(2,1)} %shard_map.131), calls=%async_computation.1 | async-start | bytes 655360 | tf_op jit(solution)/shard_map/all_to_all | solution.py:330
  82.4 31.3 %collective-permute-start.11 = (bf16[2,3,80,576]{3,2,1,0:T(8,128)(2,1)}, bf16[2,3,80,576]{3,2,1,0:T(8,128)(2,1)S(1)}, u32[]{:S(2)}, u32[]{:S(2)}) collective-permute-start(bf16[2,3,80,576]{3,2,1,0:T(8,128)(2,1)} %get-tuple-element.101), channel_id=1, source_target_pairs={{0,1},{1,0},{2,3},{3,2},{4,5},{5,4},{6,7},{7,6},{8,9},{9,8},{10,11... | collective-permute-start | bytes 1658888 | tf_op jit(solution)/shard_map/ppermute | solution.py:385
  84.9 28.7 %collective-permute-start.12 = (bf16[2,3,80,576]{3,2,1,0:T(8,128)(2,1)}, bf16[2,3,80,576]{3,2,1,0:T(8,128)(2,1)}, u32[]{:S(2)}, u32[]{:S(2)}) collective-permute-start(bf16[2,3,80,576]{3,2,1,0:T(8,128)(2,1)} %get-tuple-element.102), channel_id=1, source_target_pairs={{0,1},{1,0},{2,3},{3,2},{4,5},{5,4},{6,7},{7,6},{8,9},{9,8},{10,11... | collective-permute-start | bytes 1658888 | tf_op jit(solution)/shard_map/ppermute | solution.py:385
  92.9 20.8 %copy-start.13 = (bf16[80,128]{1,0:T(8,128)(2,1)}, bf16[80,128]{1,0:T(8,128)(2,1)S(1)}, u32[]{:S(2)}) copy-start(bf16[80,128]{1,0:T(8,128)(2,1)S(1)} %get-tuple-element.111.hidden) | copy-start | bytes 61444
  113.6 16.8 %all-to-all-start.3 = ((bf16[8,88,512]{2,1,0:T(8,128)(2,1)}), bf16[8,88,512]{2,1,0:T(8,128)(2,1)S(1)}, u32[]{:S(2)}, u32[]{:S(2)}) async-start(bf16[8,88,512]{2,1,0:T(8,128)(2,1)} %get-tuple-element.103), calls=%async_computation.3 | async-start | bytes 1441792 | tf_op jit(solution)/shard_map/all_to_all | solution.py:330
  161.4 28.4 %copy-start.14 = (bf16[80,128]{1,0:T(8,128)(2,1)S(1)}, bf16[80,128]{1,0:T(8,128)(2,1)}, u32[]{:S(2)}) copy-start(bf16[80,128]{1,0:T(8,128)(2,1)} %copy-done.13) | copy-start | bytes 61444
  (10 other events, 33.0 us)

commit v10 on v9

--- a/solution.py
+++ b/solution.py
@@ -78,7 +78,7 @@
     lax.fori_loop(0, mask.shape[1], step, 0)
 
 
-def prepare(queries, weights, wide, mine, theirs, turned):
+def prepare(queries, weights, wide, mine, low, high, turned):
     heads, width, rows = queries.shape
     for head in range(heads):
         lanes = jnp.concatenate([queries[head], jnp.zeros((width, TOK - rows), BF16)], axis=1)
@@ -88,8 +88,12 @@
     core = lax.axis_index("core")
     runs, run, _ = mine.shape
     for i in range(runs):
-        for out, at in ((mine, 2 * i + core), (theirs, 2 * i + 1 - core)):
-            out[i] = turned[pl.ds(pl.multiple_of(at * run, run), run), :]
+        mine[i] = turned[pl.ds(pl.multiple_of((2 * i + core) * run, run), run), :]
+        theirs = turned[pl.ds(pl.multiple_of((2 * i + 1 - core) * run, run), run), :]
+        if i < runs // 2:
+            low[i] = theirs
+        else:
+            high[i - runs // 2] = theirs
 
 
 def route(first, groups, experts, weights, places, shares):
@@ -168,11 +172,13 @@
     out[...] = jnp.concatenate(values, axis=0)
 
 
-def project_out(mine, theirs, weights_mine, weights_theirs, out):
-    runs, run, depth = weights_mine.shape
-    total = dot(weights_mine[...].reshape(runs * run, depth), mine[...])
-    total = total + dot(weights_theirs[...].reshape(runs * run, depth), theirs[...])
-    out[...] = total.reshape(runs, run, TOK).astype(BF16)
+def project_out(mine, theirs, weights_mine, low, high, out):
+    half, run, depth = low.shape
+    for i, weights_theirs in enumerate((low, high)):
+        own = weights_mine[i * half : (i + 1) * half].reshape(half * run, depth)
+        total = dot(own, mine[...])
+        total = total + dot(weights_theirs[...].reshape(half * run, depth), theirs[...])
+        out[i * half : (i + 1) * half] = total.reshape(half, run, TOK).astype(BF16)
 
 
 def split_pair(value):
@@ -236,20 +242,23 @@
         out[1] = held[near ^ flip ^ 1]
 
 
-def gather_swap(swapped, far_x, far_z, far_xz, low, high):
+def gather_swap(swapped, far_x, far_z, low, high):
     low[0] = swapped[...]
     low[1] = far_x[1]
-    high[0] = far_z[1]
-    high[1] = far_xz[1]
-
-
-def unpack(part, mine, far_x, far_z, far_xz, low, high, into, back):
+    high[...] = far_z[1]
+
+
+def second_half(got, out):
+    out[...] = got[1]
+
+
+def unpack(part, mine, far_x, far_z, far_xz, low, high, last, into, back):
     pairs = mine.shape[0]
     for pair in range(pairs):
         rows = []
         for i, own in enumerate((mine, far_x, far_z, far_xz)):
             rows.append(own[pair] if i == 0 else own[0, pair])
-            rows.append((low, low, high, high)[i][i % 2, pair])
+            rows.append(low[i, pair] if i < 2 else (high, last)[i - 2][pair])
         wide = jnp.concatenate([row[:, : 4 * part] for row in rows], axis=0)
         into[pair * 4 * part : (pair + 1) * 4 * part, :] = wide.T
         for flip, row in enumerate(rows):
@@ -373,33 +382,35 @@
 
     pairs = local_experts // 2
     block = (pairs, run, 6 * part)
-    mine, swapped, *far = call(
+    mine, swapped, far_x, far_z, far_xz = call(
         pack,
         [shape(block)] * 2 + [shape((2,) + block)] * 3,
         [VMEM] * 3,
         [pltpu.VMEM((near_count,) + block, BF16)],
     )(w_gate, w_up, w_down.transpose(0, 2, 1))
-    out_proj, *far = lax.optimization_barrier((out_proj, *far))
+    out_proj, far_x, far_z, far_xz = lax.optimization_barrier((out_proj, far_x, far_z, far_xz))
 
     def flipped(x, flip):
         return lax.ppermute(x, NEAR, [(a, a ^ flip) for a in range(near_count)])
 
-    far = [flipped(x, flip) for x, flip in zip(far, (2, 4, 6))]
+    far_z = flipped(far_z, 4)
+    far_x = flipped(far_x, 2)
 
     runs = D // run
     depth = heads * value_width
-    wide_q, out_mine, out_theirs = call(
+    wide_q, out_mine, *out_theirs = call(
         prepare,
-        [shape((heads * TOK, key_width))] + [shape((runs // 2, run, depth))] * 2,
+        [shape((heads * TOK, key_width)), shape((runs // 2, run, depth))]
+        + [shape((runs // 4, run, depth))] * 2,
         [VMEM] * 2,
         [pltpu.VMEM((D, depth), BF16)],
     )(queries.transpose(1, 2, 0), out_proj)
-    out_theirs = lax.ppermute(out_theirs, "core", [(0, 1), (1, 0)])
+    out_theirs = [lax.ppermute(x, "core", [(0, 1), (1, 0)]) for x in out_theirs]
     resid = jnp.pad(residual.T, ((0, 0), (0, pad_rows)))
     gain = norm_gain.astype(F32)[:, None]
-    pieces, few, wide_q, out_mine, out_theirs, places, slot_shares, resid, gain = (
+    pieces, few, wide_q, out_mine, out_theirs, far_z, places, slot_shares, resid, gain = (
         lax.optimization_barrier(
-            (pieces, few, wide_q, out_mine, out_theirs, places, slot_shares, resid, gain)
+            (pieces, few, wide_q, out_mine, out_theirs, far_z, places, slot_shares, resid, gain)
         )
     )
 
@@ -431,15 +442,16 @@
         value_up,
     )
     other_values = lax.ppermute(values, "core", [(0, 1), (1, 0)])
-    summed = call(project_out, shape((runs // 2, run, TOK)), [VMEM] * 4)(
-        values, other_values, out_mine, out_theirs
-    )
-    summed, swapped = lax.optimization_barrier((summed, swapped))
+    summed = call(project_out, shape((runs // 2, run, TOK)), [VMEM] * 5)(
+        values, other_values, out_mine, *out_theirs
+    )
+    summed, swapped, far_xz = lax.optimization_barrier((summed, swapped, far_xz))
     parts = exchange(summed, ZX)
-    swap = [
-        flipped(x, 1)
-        for x in call(gather_swap, [shape((2,) + block)] * 2, [VMEM] * 4)(swapped, *far)
-    ]
+    far_xz = flipped(far_xz, 6)
+    low, high = call(gather_swap, [shape((2,) + block), shape(block)], [VMEM] * 3)(
+        swapped, far_x, far_z
+    )
+    low, high = flipped(low, 1), flipped(high, 1)
 
     hidden, sent = call(make_rows, [shape((run, TOK)), shape((slots, TOK))], [VMEM] * 5)(
         parts,
@@ -458,16 +470,17 @@
         ],
         [VMEM],
     )(got)
-    spread, swap = lax.optimization_barrier((spread, swap))
+    spread, low, high, far_xz = lax.optimization_barrier((spread, low, high, far_xz))
     inputs = exchange(spread, NEAR)
+    last = flipped(call(second_half, shape(block), [VMEM])(far_xz), 1)
     weights_in, weights_back = call(
         functools.partial(unpack, part),
         [
             shape((pairs * 4 * part, near_count * run)),
             shape((near_count, run, local_experts * part)),
         ],
-        [VMEM] * 6,
-    )(mine, *far, *swap)
+        [VMEM] * 7,
+    )(mine, far_x, far_z, far_xz, low, high, last)
     partial_sums = call(
         functools.partial(project_up, run, sub),
         shape((far_count, 4 * sub + 8, slots)),

time: 192 us -> 178 us (0.927)
  waiting for transfers between devices: 29.6 us -> 10.2 us
  starting transfers between devices: 57.3 us -> 63.2 us
  Pallas kernels: 19.9 us -> 17 us
    ppermute x1, waiting for transfers between devices: 16.6 us -> 0.01 us  [attention(): across = lax.ppermute(picked, 'zb', [(0, 1), (1, 0)])]
    all_to_all x3, waiting for transfers between devices: 10.9 us -> 4.35 us  [exchange(): return lax.all_to_all(x, axes, split_axis=0, concat_axis=0, tiled=True)]
    ppermute x5 -> x6, starting transfers between devices: 13.5 us -> 17.4 us  [flipped(): return lax.ppermute(x, NEAR, [(a, a ^ flip) for a in range(near_count)])]
    ppermute x5 -> x6, waiting for transfers between devices: 0.01 us -> 3.91 us  [flipped(): return lax.ppermute(x, NEAR, [(a, a ^ flip) for a in range(near_count)])]
    ppermute x1 -> x2, starting transfers between devices: 2.81 us -> 5.3 us  [on_device(): out_theirs = [lax.ppermute(x, 'core', [(0, 1), (1, 0)]) for x in out_theirs]]
    unnamed x42 -> x48, local copies, waits for them, and re-layouts: 6.71 us -> 8.16 us
    pallas_call x3 -> x4, Pallas kernels: 4.8 us -> 3.83 us  [the longest x1 1.52 us: on_device(): call(prepare, [shape((heads * TOK, key_width)), shape((runs // 2, run, de...]
  transfers between devices with their start and end apart: 13 -> 15, of which waited for: 5 -> 6; matrix products, arithmetic and copies ran while one was open for 0% -> 0% of each run, Pallas kernels for 8% -> 7%
where the time goes in v10:
time: 178 us; the launch traced here: 177 us
  blocking collectives  76.5 us (43%)
  starting transfers between devices  63.2 us (36%)
  Pallas kernels  17 us (10%)
  waiting for transfers between devices  10.2 us (6%)
  local copies, waits for them, and re-layouts  8.27 us (5%)
    all_to_all x5, blocking collectives, exchange(): return lax.all_to_all(x, axes, split_axis=0, concat_axis=0, tiled=True)  76.5 us
    all_to_all x3, starting transfers between devices, exchange(): return lax.all_to_all(x, axes, split_axis=0, concat_axis=0, tiled=True)  27.3 us
    ppermute x6, starting transfers between devices, flipped(): return lax.ppermute(x, NEAR, [(a, a ^ flip) for a in range(near_count)])  17.4 us
    unnamed x48, local copies, waits for them, and re-layouts  8.16 us
    ppermute x2, starting transfers between devices, on_device(): out_theirs = [lax.ppermute(x, 'core', [(0, 1), (1, 0)]) for x in out_theirs]  5.3 us
    all_to_all x3, waiting for transfers between devices, exchange(): return lax.all_to_all(x, axes, split_axis=0, concat_axis=0, tiled=True)  4.35 us
    ppermute x1, starting transfers between devices, attention(): beside = lax.ppermute(picked, 'core', [(0, 1), (1, 0)])  3.95 us
    ppermute x6, waiting for transfers between devices, flipped(): return lax.ppermute(x, NEAR, [(a, a ^ flip) for a in range(near_count)])  3.91 us
  transfers between devices with their start and end apart: 15, of which 6 were waited for; matrix products, arithmetic and copies ran while one was open for 0% of the time, Pallas kernels for 7%

profile of v10, /device:TPU:1, one launch (start us, length us, event | category | flops | bytes accessed | tf_op | source)
XLA Modules:
  0.0 177.1 jit_solution(786566328420646661)
XLA Ops:
  0.0 2.0 %shard_map.127 = bf16[16,144,128]{2,1,0:T(8,128)(2,1)} custom-call(bf16[576,120]{1,0:T(8,128)(2,1)} %bitcast.24), custom_call_target="tpu_custom_call" | custom-call | tf_op jit(solution)/shard_map/pallas_call | solution.py:372
  2.0 10.4 %all-to-all-start = ((bf16[16,144,128]{2,1,0:T(8,128)(2,1)}), bf16[16,144,128]{2,1,0:T(8,128)(2,1)}, u32[]{:S(2)}, u32[]{:S(2)}) async-start(bf16[16,144,128]{2,1,0:T(8,128)(2,1)} %shard_map.127), calls=%async_computation | async-start | bytes 1179648 | tf_op jit(solution)/shard_map/all_to_all | solution.py:339
  13.5 2.1 %shard_map.128 = (bf16[3,80,576]{2,1,0:T(8,128)(2,1)S(1)}, bf16[3,80,576]{2,1,0:T(8,128)(2,1)S(1)}, bf16[2,3,80,576]{3,2,1,0:T(8,128)(2,1)}, bf16[2,3,80,576]{3,2,1,0:T(8,128)(2,1)}, bf16[2,3,80,576]{3,2,1,0:T(8,128)(2,1)S(1)}) custom-call(bf16[6,80,768]{2,1,0:T(8,128)(2,1)S(1)} %copy-done.3, bf16[6,80,768]{2,1,0:T(8,128)(2,1)S(1)} %copy-done.4, ...), custom_call_target="tpu_custom_call" | custom-call | tf_op jit(solution)/shard_map/pallas_call | solution.py:385
  16.4 4.0 %collective-permute-start.8 = (bf16[2,3,80,576]{3,2,1,0:T(8,128)(2,1)}, bf16[2,3,80,576]{3,2,1,0:T(8,128)(2,1)S(1)}, u32[]{:S(2)}, u32[]{:S(2)}) collective-permute-start(bf16[2,3,80,576]{3,2,1,0:T(8,128)(2,1)} %get-tuple-element.88), channel_id=1, source_target_pairs={{0,4},{1,5},{2,6},{3,7},{4,0},{5,1},{6,2},{7,3},{8,12},{9,13},{10,... | collective-permute-start | bytes 1658888 | tf_op jit(solution)/shard_map/ppermute | solution.py:394
  20.4 2.2 %collective-permute-start.10 = (bf16[2,3,80,576]{3,2,1,0:T(8,128)(2,1)}, bf16[2,3,80,576]{3,2,1,0:T(8,128)(2,1)S(1)}, u32[]{:S(2)}, u32[]{:S(2)}) collective-permute-start(bf16[2,3,80,576]{3,2,1,0:T(8,128)(2,1)} %get-tuple-element.107), channel_id=1, source_target_pairs={{0,2},{1,3},{2,0},{3,1},{4,6},{5,7},{6,4},{7,5},{8,10},{9,11},{10,... | collective-permute-start | bytes 1658888 | tf_op jit(solution)/shard_map/ppermute | solution.py:394
  24.1 3.4 %collective-permute-start.6 = (bf16[8,80,256]{2,1,0:T(8,128)(2,1)}, bf16[8,80,256]{2,1,0:T(8,128)(2,1)S(1)}, u32[]{:S(2)}, u32[]{:S(2)}) collective-permute-start(bf16[8,80,256]{2,1,0:T(8,128)(2,1)} %get-tuple-element.86), channel_id=1, source_target_pairs={{0,1},{1,0},{2,3},{3,2},{4,5},{5,4},{6,7},{7,6},{8,9},{9,8},{10,11... | collective-permute-start | bytes 983048 | tf_op jit(solution)/shard_map/ppermute | solution.py:408
  31.4 2.4 %collective-permute-done.8.far_z = bf16[2,3,80,576]{3,2,1,0:T(8,128)(2,1)S(1)} collective-permute-done((bf16[2,3,80,576]{3,2,1,0:T(8,128)(2,1)}, bf16[2,3,80,576]{3,2,1,0:T(8,128)(2,1)S(1)}, u32[]{:S(2)}, u32[]{:S(2)}) %collective-permute-start.8) | collective-permute-done | bytes 552992 | tf_op jit(solution)/shard_map/ppermute | solution.py:394
  33.8 15.5 %conditional.1 = (bf16[256,128]{1,0:T(8,128)(2,1)S(1)}) conditional(s32[]{:T(128)} %convert_element_type.6, (s32[16,16]{1,0:T(8,128)S(1)}, bf16[16,144,128]{2,1,0:T(8,128)(2,1)}, bf16[256,576]{1,0:T(8,128)(2,1)}, bf16[576,120]{1,0:T(8,128)(2,1)}, bf16[2,512,128]{2,1,0:T(8,128)(2,1)}) %tuple.24, (s32[16,16]{1,0:T(8,128)S(1)}, ...), branch_computations={%region_2.3_spmd, %region_3.4_spmd} | conditional | bytes 6635648 | solution.py:434
  35.2 3.1 %collective-permute-start.4 = (bf16[5,144,128]{2,1,0:T(8,128)(2,1)S(1)}, bf16[5,144,128]{2,1,0:T(8,128)(2,1)S(1)}, u32[]{:S(2)}, u32[]{:S(2)}) collective-permute-start(bf16[5,144,128]{2,1,0:T(8,128)(2,1)S(1)} %branch_1_fun.2.refs_0_), channel_id=1, source_target_pairs={{0,4},{4,0},{1,5},{5,1},{2,6},{6,2},{3,7},{7,3},{8,12},{12,8},{9,1... | collective-permute-start | bytes 552968 | tf_op jit(solution)/shard_map/cond/branch_1_fun/ppermute | solution.py:419
  38.4 3.9 %collective-permute-start.3 = (bf16[5,144,128]{2,1,0:T(8,128)(2,1)S(1)}, bf16[5,144,128]{2,1,0:T(8,128)(2,1)S(1)}, u32[]{:S(2)}, u32[]{:S(2)}) collective-permute-start(bf16[5,144,128]{2,1,0:T(8,128)(2,1)S(1)} %branch_1_fun.2.refs_0_), channel_id=1, source_target_pairs={{0,1},{1,0},{2,3},{3,2},{4,5},{5,4},{6,7},{7,6},{8,9},{9,8},{10,11... | collective-permute-start | bytes 552968 | tf_op jit(solution)/shard_map/cond/branch_1_fun/ppermute | solution.py:420
  42.3 3.8 %collective-permute-start.5 = (bf16[5,144,128]{2,1,0:T(8,128)(2,1)S(1)}, bf16[5,144,128]{2,1,0:T(8,128)(2,1)S(1)}, u32[]{:S(2)}, u32[]{:S(2)}) collective-permute-start(bf16[5,144,128]{2,1,0:T(8,128)(2,1)S(1)} %collective-permute-done.4.refs_2_), channel_id=1, source_target_pairs={{0,1},{1,0},{2,3},{3,2},{4,5},{5,4},{6,7},{7,6},{8,9},{9,8},{10,11... | collective-permute-start | bytes 552968 | tf_op jit(solution)/shard_map/cond/branch_1_fun/ppermute | solution.py:421
  47.1 2.2 %branch_1_fun.3 = bf16[256,128]{1,0:T(8,128)(2,1)S(1)} custom-call(s32[16,16]{1,0:T(8,128)S(1)} %get-tuple-element.33.mask, bf16[256,576]{1,0:T(8,128)(2,1)} %get-tuple-element.34.queries, bf16[576,120]{1,0:T(8,128)(2,1)} %get-tuple-element.35.own, bf16[2,512,128]{2,1,0:T(8,128)(2,1)} %get-tuple-element.36.up, bf16[5,144,128]{2,1,0:T(8,128)(2,1)S(1)} %branch_1_fun.2.refs_0_, ...), custom_call_target="tpu_custom_call" | custom-call | tf_op jit(solution)/shard_map/cond/branch_1_fun/pallas_call | solution.py:422
  49.4 2.4 %collective-permute-start.9 = (bf16[256,128]{1,0:T(8,128)(2,1)S(1)}, bf16[256,128]{1,0:T(8,128)(2,1)S(1)}, u32[]{:S(2)}, u32[]{:S(2)}) collective-permute-start(bf16[256,128]{1,0:T(8,128)(2,1)S(1)} %get-tuple-element.122.mine), channel_id=1, source_target_pairs={{0,1},{1,0},{2,3},{3,2},{4,5},{5,4},{6,7},{7,6},{8,9},{9,8},{10,11... | collective-permute-start | bytes 196616 | tf_op jit(solution)/shard_map/ppermute | solution.py:444
  53.9 9.5 %all-to-all-start.1 = ((bf16[16,80,128]{2,1,0:T(8,128)(2,1)}), bf16[16,80,128]{2,1,0:T(8,128)(2,1)S(1)}, u32[]{:S(2)}, u32[]{:S(2)}) async-start(bf16[16,80,128]{2,1,0:T(8,128)(2,1)} %shard_map.131), calls=%async_computation.1 | async-start | bytes 655360 | tf_op jit(solution)/shard_map/all_to_all | solution.py:339
  63.5 4.2 %collective-permute-start.13 = (bf16[2,3,80,576]{3,2,1,0:T(8,128)(2,1)}, bf16[2,3,80,576]{3,2,1,0:T(8,128)(2,1)S(1)}, u32[]{:S(2)}, u32[]{:S(2)}) collective-permute-start(bf16[2,3,80,576]{3,2,1,0:T(8,128)(2,1)} %copy-done.20), channel_id=1, source_target_pairs={{0,6},{1,7},{2,4},{3,5},{4,2},{5,3},{6,0},{7,1},{8,14},{9,15},{10,... | collective-permute-start | bytes 1658888 | tf_op jit(solution)/shard_map/ppermute | solution.py:394
  68.7 3.1 %collective-permute-start.11 = (bf16[2,3,80,576]{3,2,1,0:T(8,128)(2,1)}, bf16[2,3,80,576]{3,2,1,0:T(8,128)(2,1)S(1)}, u32[]{:S(2)}, u32[]{:S(2)}) collective-permute-start(bf16[2,3,80,576]{3,2,1,0:T(8,128)(2,1)} %get-tuple-element.109), channel_id=1, source_target_pairs={{0,1},{1,0},{2,3},{3,2},{4,5},{5,4},{6,7},{7,6},{8,9},{9,8},{10,11... | collective-permute-start | bytes 1658888 | tf_op jit(solution)/shard_map/ppermute | solution.py:394
  73.8 2.5 %all-to-all-done.1.parts = bf16[16,80,128]{2,1,0:T(8,128)(2,1)S(1)} async-done(((bf16[16,80,128]{2,1,0:T(8,128)(2,1)}), bf16[16,80,128]{2,1,0:T(8,128)(2,1)S(1)}, u32[]{:S(2)}, u32[]{:S(2)}) %all-to-all-start.1) | async-done | bytes 327712 | tf_op jit(solution)/shard_map/all_to_all | solution.py:339
  76.6 21.3 %all_to_all.40 = bf16[16,32,128]{2,1,0:T(8,128)(2,1)S(1)} all-to-all(bf16[16,32,128]{2,1,0:T(8,128)(2,1)S(1)} %bitcast.20), channel_id=1, replica_groups=mesh['y'=8,'xh'=2,'za'=4,'zb'=2,'xl'=2,'core'=2] {'y','xh'}, dimensions={0} | all-to-all | bytes 262144 | tf_op jit(solution)/shard_map/all_to_all | solution.py:339
  99.6 7.3 %all-to-all-start.3 = ((bf16[8,88,512]{2,1,0:T(8,128)(2,1)}), bf16[8,88,512]{2,1,0:T(8,128)(2,1)S(1)}, u32[]{:S(2)}, u32[]{:S(2)}) async-start(bf16[8,88,512]{2,1,0:T(8,128)(2,1)} %get-tuple-element.112), calls=%async_computation.3 | async-start | bytes 1441792 | tf_op jit(solution)/shard_map/all_to_all | solution.py:339
  106.9 2.0 %collective-permute-start.14 = (bf16[3,80,576]{2,1,0:T(8,128)(2,1)S(1)}, bf16[3,80,576]{2,1,0:T(8,128)(2,1)S(1)}, u32[]{:S(2)}, u32[]{:S(2)}) collective-permute-start(bf16[3,80,576]{2,1,0:T(8,128)(2,1)S(1)} %shard_map.135), channel_id=1, source_target_pairs={{0,1},{1,0},{2,3},{3,2},{4,5},{5,4},{6,7},{7,6},{8,9},{9,8},{10,11... | collective-permute-start | bytes 829448 | tf_op jit(solution)/shard_map/ppermute | solution.py:394
  119.6 15.4 %all_to_all.41.got = bf16[4,104,512]{2,1,0:T(8,128)(2,1)S(1)} all-to-all(bf16[4,104,512]{2,1,0:T(8,128)(2,1)S(1)} %shard_map.137), channel_id=1, replica_groups=mesh['y'=8,'xh'=2,'za'=4,'zb'=2,'xl'=2,'core'=2] {'za'}, dimensions={0} | all-to-all | bytes 851968 | tf_op jit(solution)/shard_map/all_to_all | solution.py:339
  135.0 11.8 %all_to_all.42.acts = bf16[4,48,512]{2,1,0:T(8,128)(2,1)S(1)} all-to-all(bf16[4,48,512]{2,1,0:T(8,128)(2,1)S(1)} %shard_map.138), channel_id=1, replica_groups=mesh['y'=8,'xh'=2,'za'=4,'zb'=2,'xl'=2,'core'=2] {'za'}, dimensions={0} | all-to-all | bytes 393216 | tf_op jit(solution)/shard_map/all_to_all | solution.py:339
  148.0 15.4 %all_to_all.43.got = bf16[8,80,512]{2,1,0:T(8,128)(2,1)S(1)} all-to-all(bf16[8,80,512]{2,1,0:T(8,128)(2,1)S(1)} %shard_map.139), channel_id=1, replica_groups=mesh['y'=8,'xh'=2,'za'=4,'zb'=2,'xl'=2,'core'=2] {'zb','xl','core'}, dimensions={0} | all-to-all | bytes 1310720 | tf_op jit(solution)/shard_map/all_to_all | solution.py:339
  163.6 12.6 %all_to_all.44 = bf16[16,32,128]{2,1,0:T(8,128)(2,1)S(1)} all-to-all(bf16[16,32,128]{2,1,0:T(8,128)(2,1)S(1)} %bitcast.18), channel_id=1, replica_groups=mesh['y'=8,'xh'=2,'za'=4,'zb'=2,'xl'=2,'core'=2] {'y','xh'}, dimensions={0} | all-to-all | bytes 262144 | tf_op jit(solution)/shard_map/all_to_all | solution.py:339
  (82 shorter events, 28.9 us)
Async XLA Ops:
  2.0 20.6 %copy-start.2 = (bf16[256,2560]{1,0:T(8,128)(2,1)S(1)}, bf16[256,2560]{1,0:T(8,128)(2,1)}, u32[]{:S(2)}) copy-start(bf16[256,2560]{1,0:T(8,128)(2,1)} %weights) | copy-start | bytes 3932164
  2.0 31.9 %all-to-all-start = ((bf16[16,144,128]{2,1,0:T(8,128)(2,1)}), bf16[16,144,128]{2,1,0:T(8,128)(2,1)}, u32[]{:S(2)}, u32[]{:S(2)}) async-start(bf16[16,144,128]{2,1,0:T(8,128)(2,1)} %shard_map.127), calls=%async_computation | async-start | bytes 1179648 | tf_op jit(solution)/shard_map/all_to_all | solution.py:339
  13.5 17.4 %copy-start.22 = (bf16[120,80]{0,1:T(8,128)(2,1)S(1)}, bf16[120,80]{0,1:T(8,128)(2,1)}, u32[]{:S(2)}) copy-start(bf16[120,80]{0,1:T(8,128)(2,1)} %param.20) | copy-start | bytes 57604
  13.5 17.4 %copy-start.17 = (s32[120,3,2]{0,2,1:T(2,128)S(1)}, s32[120,3,2]{0,2,1:T(2,128)}, u32[]{:S(2)}) copy-start(s32[120,3,2]{0,2,1:T(2,128)} %param.23) | copy-start | bytes 8644
  13.5 17.4 %copy-start.18 = (s32[120,3]{0,1:T(4,128)S(1)}, s32[120,3]{0,1:T(4,128)}, u32[]{:S(2)}) copy-start(s32[120,3]{0,1:T(4,128)} %param.22) | copy-start | bytes 4324
  13.5 17.4 %copy-start.19 = (bf16[120,3,2]{0,2,1:T(2,128)(2,1)S(1)}, bf16[120,3,2]{0,2,1:T(2,128)(2,1)}, u32[]{:S(2)}) copy-start(bf16[120,3,2]{0,2,1:T(2,128)(2,1)} %param.24) | copy-start | bytes 4324
  13.5 17.8 %copy-start.23 = (bf16[80]{0:T(256)(128)(2,1)S(1)}, bf16[80]{0:T(256)(128)(2,1)}, u32[]{:S(2)}) copy-start(bf16[80]{0:T(256)(128)(2,1)} %param.21) | copy-start | bytes 484
  16.4 17.5 %collective-permute-start.8 = (bf16[2,3,80,576]{3,2,1,0:T(8,128)(2,1)}, bf16[2,3,80,576]{3,2,1,0:T(8,128)(2,1)S(1)}, u32[]{:S(2)}, u32[]{:S(2)}) collective-permute-start(bf16[2,3,80,576]{3,2,1,0:T(8,128)(2,1)} %get-tuple-element.88), channel_id=1, source_target_pairs={{0,4},{1,5},{2,6},{3,7},{4,0},{5,1},{6,2},{7,3},{8,12},{9,13},{10,... | collective-permute-start | bytes 1658888 | tf_op jit(solution)/shard_map/ppermute | solution.py:394
  20.4 47.3 %collective-permute-start.10 = (bf16[2,3,80,576]{3,2,1,0:T(8,128)(2,1)}, bf16[2,3,80,576]{3,2,1,0:T(8,128)(2,1)S(1)}, u32[]{:S(2)}, u32[]{:S(2)}) collective-permute-start(bf16[2,3,80,576]{3,2,1,0:T(8,128)(2,1)} %get-tuple-element.107), channel_id=1, source_target_pairs={{0,2},{1,3},{2,0},{3,1},{4,6},{5,7},{6,4},{7,5},{8,10},{9,11},{10,... | collective-permute-start | bytes 1658888 | tf_op jit(solution)/shard_map/ppermute | solution.py:394
  24.1 7.2 %collective-permute-start.6 = (bf16[8,80,256]{2,1,0:T(8,128)(2,1)}, bf16[8,80,256]{2,1,0:T(8,128)(2,1)S(1)}, u32[]{:S(2)}, u32[]{:S(2)}) collective-permute-start(bf16[8,80,256]{2,1,0:T(8,128)(2,1)} %get-tuple-element.86), channel_id=1, source_target_pairs={{0,1},{1,0},{2,3},{3,2},{4,5},{5,4},{6,7},{7,6},{8,9},{9,8},{10,11... | collective-permute-start | bytes 983048 | tf_op jit(solution)/shard_map/ppermute | solution.py:408
  27.5 3.8 %collective-permute-start.7 = (bf16[8,80,256]{2,1,0:T(8,128)(2,1)}, bf16[8,80,256]{2,1,0:T(8,128)(2,1)S(1)}, u32[]{:S(2)}, u32[]{:S(2)}) collective-permute-start(bf16[8,80,256]{2,1,0:T(8,128)(2,1)} %get-tuple-element.87), channel_id=1, source_target_pairs={{0,1},{1,0},{2,3},{3,2},{4,5},{5,4},{6,7},{7,6},{8,9},{9,8},{10,11... | collective-permute-start | bytes 983048 | tf_op jit(solution)/shard_map/ppermute | solution.py:408
  35.2 7.1 %collective-permute-start.4 = (bf16[5,144,128]{2,1,0:T(8,128)(2,1)S(1)}, bf16[5,144,128]{2,1,0:T(8,128)(2,1)S(1)}, u32[]{:S(2)}, u32[]{:S(2)}) collective-permute-start(bf16[5,144,128]{2,1,0:T(8,128)(2,1)S(1)} %branch_1_fun.2.refs_0_), channel_id=1, source_target_pairs={{0,4},{4,0},{1,5},{5,1},{2,6},{6,2},{3,7},{7,3},{8,12},{12,8},{9,1... | collective-permute-start | bytes 552968 | tf_op jit(solution)/shard_map/cond/branch_1_fun/ppermute | solution.py:419
  38.4 7.7 %collective-permute-start.3 = (bf16[5,144,128]{2,1,0:T(8,128)(2,1)S(1)}, bf16[5,144,128]{2,1,0:T(8,128)(2,1)S(1)}, u32[]{:S(2)}, u32[]{:S(2)}) collective-permute-start(bf16[5,144,128]{2,1,0:T(8,128)(2,1)S(1)} %branch_1_fun.2.refs_0_), channel_id=1, source_target_pairs={{0,1},{1,0},{2,3},{3,2},{4,5},{5,4},{6,7},{7,6},{8,9},{9,8},{10,11... | collective-permute-start | bytes 552968 | tf_op jit(solution)/shard_map/cond/branch_1_fun/ppermute | solution.py:420
  42.3 4.8 %collective-permute-start.5 = (bf16[5,144,128]{2,1,0:T(8,128)(2,1)S(1)}, bf16[5,144,128]{2,1,0:T(8,128)(2,1)S(1)}, u32[]{:S(2)}, u32[]{:S(2)}) collective-permute-start(bf16[5,144,128]{2,1,0:T(8,128)(2,1)S(1)} %collective-permute-done.4.refs_2_), channel_id=1, source_target_pairs={{0,1},{1,0},{2,3},{3,2},{4,5},{5,4},{6,7},{7,6},{8,9},{9,8},{10,11... | collective-permute-start | bytes 552968 | tf_op jit(solution)/shard_map/cond/branch_1_fun/ppermute | solution.py:421
  49.4 18.3 %copy-start.11 = (bf16[3,80,576]{2,1,0:T(8,128)(2,1)S(1)}, bf16[3,80,576]{2,1,0:T(8,128)(2,1)}, u32[]{:S(2)}) copy-start(bf16[3,80,576]{2,1,0:T(8,128)(2,1)} %copy-done.10) | copy-start | bytes 829444
  49.4 3.3 %collective-permute-start.9 = (bf16[256,128]{1,0:T(8,128)(2,1)S(1)}, bf16[256,128]{1,0:T(8,128)(2,1)S(1)}, u32[]{:S(2)}, u32[]{:S(2)}) collective-permute-start(bf16[256,128]{1,0:T(8,128)(2,1)S(1)} %get-tuple-element.122.mine), channel_id=1, source_target_pairs={{0,1},{1,0},{2,3},{3,2},{4,5},{5,4},{6,7},{7,6},{8,9},{9,8},{10,11... | collective-permute-start | bytes 196616 | tf_op jit(solution)/shard_map/ppermute | solution.py:444
  53.9 22.4 %all-to-all-start.1 = ((bf16[16,80,128]{2,1,0:T(8,128)(2,1)}), bf16[16,80,128]{2,1,0:T(8,128)(2,1)S(1)}, u32[]{:S(2)}, u32[]{:S(2)}) async-start(bf16[16,80,128]{2,1,0:T(8,128)(2,1)} %shard_map.131), calls=%async_computation.1 | async-start | bytes 655360 | tf_op jit(solution)/shard_map/all_to_all | solution.py:339
  63.5 36.1 %collective-permute-start.13 = (bf16[2,3,80,576]{3,2,1,0:T(8,128)(2,1)}, bf16[2,3,80,576]{3,2,1,0:T(8,128)(2,1)S(1)}, u32[]{:S(2)}, u32[]{:S(2)}) collective-permute-start(bf16[2,3,80,576]{3,2,1,0:T(8,128)(2,1)} %copy-done.20), channel_id=1, source_target_pairs={{0,6},{1,7},{2,4},{3,5},{4,2},{5,3},{6,0},{7,1},{8,14},{9,15},{10,... | collective-permute-start | bytes 1658888 | tf_op jit(solution)/shard_map/ppermute | solution.py:394
  68.7 30.9 %collective-permute-start.11 = (bf16[2,3,80,576]{3,2,1,0:T(8,128)(2,1)}, bf16[2,3,80,576]{3,2,1,0:T(8,128)(2,1)S(1)}, u32[]{:S(2)}, u32[]{:S(2)}) collective-permute-start(bf16[2,3,80,576]{3,2,1,0:T(8,128)(2,1)} %get-tuple-element.109), channel_id=1, source_target_pairs={{0,1},{1,0},{2,3},{3,2},{4,5},{5,4},{6,7},{7,6},{8,9},{9,8},{10,11... | collective-permute-start | bytes 1658888 | tf_op jit(solution)/shard_map/ppermute | solution.py:394
  71.8 27.0 %collective-permute-start.12 = (bf16[3,80,576]{2,1,0:T(8,128)(2,1)}, bf16[3,80,576]{2,1,0:T(8,128)(2,1)S(1)}, u32[]{:S(2)}, u32[]{:S(2)}) collective-permute-start(bf16[3,80,576]{2,1,0:T(8,128)(2,1)} %get-tuple-element.110), channel_id=1, source_target_pairs={{0,1},{1,0},{2,3},{3,2},{4,5},{5,4},{6,7},{7,6},{8,9},{9,8},{10,11... | collective-permute-start | bytes 829448 | tf_op jit(solution)/shard_map/ppermute | solution.py:394
  76.6 23.0 %copy-start.15 = (bf16[80,128]{1,0:T(8,128)(2,1)}, bf16[80,128]{1,0:T(8,128)(2,1)S(1)}, u32[]{:S(2)}) copy-start(bf16[80,128]{1,0:T(8,128)(2,1)S(1)} %get-tuple-element.121.hidden) | copy-start | bytes 61444
  99.6 17.5 %all-to-all-start.3 = ((bf16[8,88,512]{2,1,0:T(8,128)(2,1)}), bf16[8,88,512]{2,1,0:T(8,128)(2,1)S(1)}, u32[]{:S(2)}, u32[]{:S(2)}) async-start(bf16[8,88,512]{2,1,0:T(8,128)(2,1)} %get-tuple-element.112), calls=%async_computation.3 | async-start | bytes 1441792 | tf_op jit(solution)/shard_map/all_to_all | solution.py:339
  106.9 3.5 %collective-permute-start.14 = (bf16[3,80,576]{2,1,0:T(8,128)(2,1)S(1)}, bf16[3,80,576]{2,1,0:T(8,128)(2,1)S(1)}, u32[]{:S(2)}, u32[]{:S(2)}) collective-permute-start(bf16[3,80,576]{2,1,0:T(8,128)(2,1)S(1)} %shard_map.135), channel_id=1, source_target_pairs={{0,1},{1,0},{2,3},{3,2},{4,5},{5,4},{6,7},{7,6},{8,9},{9,8},{10,11... | collective-permute-start | bytes 829448 | tf_op jit(solution)/shard_map/ppermute | solution.py:394
  148.0 28.2 %copy-start.16 = (bf16[80,128]{1,0:T(8,128)(2,1)S(1)}, bf16[80,128]{1,0:T(8,128)(2,1)}, u32[]{:S(2)}) copy-start(bf16[80,128]{1,0:T(8,128)(2,1)} %copy-done.15) | copy-start | bytes 61444
  (15 other events, 91.1 us)
